TPU v7x, 32 devices: a whole 2x2x4 slice. The times are simulated.
32 devices in a mesh: node: 8 (over y, x, core), local: 4 (over z).
Axes of the slice: x: 2, y: 2, z: 4, core: 2. Of those that a mesh axis runs over, the one named last changes fastest.
Arguments:
- grad_out: bfloat16 [4096, 32, 384], P(('node', 'local')), may hold values from -6 to 6
- pooled: bfloat16 [4096, 32, 256], P(('node', 'local')), may hold values from -6 to 6
- proj: bfloat16 [32, 256, 128], P(('node', 'local')), may hold values from -0.5 to 0.5
- assign: int32 [32], replicated, may hold values from 0 to 31, each once
- indices: int32 [32, 4096, 3, 8], P(('node', 'local')), may hold values from 0 to 511
- lengths: int32 [32, 4096, 3], P(('node', 'local')), may hold values from 1 to 8
Outputs:
- table_grad: float32 [32, 512, 256], P(('node', 'local'))
- proj_grad: float32 [32, 256, 128], P(('node', 'local'))
Inputs may be any that keep to these rules, and one draw needn't show every extreme that they name: assign holds every group id once.
All inputs are finite; a program needn't handle non-finite values.
Results may differ from a plain program's by a relative error of at most 0.0029.
Values may be sent and summed in bfloat16 or wider, within the bound.
No kernel may reach another device: no remote copies, remote signals or barrier semaphores. Data moves between devices by JAX's collectives and lax.ppermute only.
A program may use at most 192 MiB of HBM per device.

v0:
```python
import functools
import math

import jax
import jax.numpy as jnp
from jax import lax
from jax.experimental import pallas as pl
from jax.experimental.pallas import tpu as pltpu
from jax.sharding import PartitionSpec as P

ROWS = 512
W1 = 16
W2 = 48
W3 = 192
PD = 128
W12 = W1 + W2
WSUM = W12 + W3
AXES = ("node", "local")
EB = 8
STEP = 32
MIB = 1024 * 1024


def params(grid):
    return pltpu.CompilerParams(dimension_semantics=("arbitrary",) * grid, vmem_limit_bytes=58 * MIB)


HBM = pl.BlockSpec(memory_space=pltpu.HBM)
ANY = pl.BlockSpec(memory_space=pl.ANY)


def cost(flops):
    return pl.CostEstimate(flops=int(flops), bytes_accessed=1024, transcendentals=0)


def permute_kernel(slots, pieces, assign_ref, grad_ref, pool_ref, *refs):
    outs, (perm_ref, grad_held, pool_held, sems) = refs[:3], refs[3:]
    step = pl.program_id(0)
    sources = ((grad_ref, grad_held), (pool_ref, pool_held))

    def copies(i):
        at = pl.ds(i * STEP, STEP)
        return [
            pltpu.make_async_copy(ref.at[at], held.at[at], sems.at[n, i]) for n, (ref, held) in enumerate(sources)
        ]

    @pl.when(step == 0)
    def _():
        for i in range(grad_ref.shape[0] // STEP):
            for copy in copies(i):
                copy.start()
        width = EB * slots
        lane = lax.broadcasted_iota(jnp.int32, (2 * EB, width), 1)
        row = lax.broadcasted_iota(jnp.int32, (2 * EB, width), 0)
        for s in range(0, slots, 2):
            group = jnp.where(row < EB, assign_ref[s], assign_ref[s + 1])
            hit = lane == (row % EB) * slots + group
            perm_ref[s * EB : (s + 2) * EB, :] = jnp.where(hit, 1.0, 0.0).astype(jnp.bfloat16)

    for copy, (_, held), cuts in zip(copies(step), sources, pieces):
        copy.wait()
        width = held.shape[2]
        for start in range(0, STEP, 2 * EB):
            pair = []
            for at in (start, start + EB):
                block = held[pl.ds(step * STEP + at, EB)].reshape(EB * slots, width)
                moved = jnp.dot(perm_ref[...], block, preferred_element_type=jnp.float32)
                pair.append(moved.reshape(slots, EB, width))
            both = jnp.concatenate(pair, axis=1).astype(jnp.bfloat16)
            for n, low, high in cuts:
                outs[n][:, start : start + 2 * EB, :] = both[:, :, low:high]


def permute(assign, grad_out, pooled):
    count, slots, _ = grad_out.shape
    widths = (2 * PD, PD, WSUM)
    pieces = (((0, 0, 2 * PD), (1, 2 * PD, 3 * PD)), ((2, 0, WSUM),))
    return pl.pallas_call(
        functools.partial(permute_kernel, slots, pieces),
        out_shape=[jax.ShapeDtypeStruct((slots, count, width), jnp.bfloat16) for width in widths],
        grid_spec=pltpu.PrefetchScalarGridSpec(
            num_scalar_prefetch=1,
            grid=(count // STEP,),
            in_specs=[HBM] * 2,
            out_specs=[pl.BlockSpec((slots, STEP, width), lambda i, a: (0, i, 0)) for width in widths],
            scratch_shapes=[
                pltpu.VMEM((EB * slots, EB * slots), jnp.bfloat16),
                pltpu.VMEM(grad_out.shape, jnp.bfloat16),
                pltpu.VMEM(pooled.shape, jnp.bfloat16),
                pltpu.SemaphoreType.DMA((2, count // STEP)),
            ],
        ),
        compiler_params=params(1),
        cost_estimate=cost(1e7),
        name="permute_groups",
    )(assign, grad_out, pooled)


def fetch(ref, held, sems, blocks, pick=lambda i: i):
    size = held.shape[0] // blocks
    copies = [
        pltpu.make_async_copy(ref.at[pl.ds(pick(i) * size, size)], held.at[pl.ds(i * size, size)], sems.at[i])
        for i in range(blocks)
    ]
    for copy in copies:
        copy.start()
    return copies


def narrow_kernel(blocks, place_ref, g_ref, w_ref, *refs):
    out_ref, g_held, w_held, out_held, g_sems, w_sems, out_sems = refs[-7:]
    weights = fetch(w_ref, w_held, w_sems, 1)
    loads = fetch(g_ref, g_held, g_sems, blocks)
    slots, count, _ = g_held.shape
    step, half = slots // blocks, count // 2
    column = lax.broadcasted_iota(jnp.int32, (count, W12), 1)
    dims = (((1,), (1,)), ((), ()))
    weights[0].wait()
    stores = []
    for i, load in enumerate(loads):
        load.wait()
        for s in range(i * step, (i + 1) * step):
            w = w_held[place_ref[s]]
            first = lax.dot_general(g_held[s, :, :PD], w, dims, preferred_element_type=jnp.float32)
            second = lax.dot_general(g_held[s, :, PD:], w, dims, preferred_element_type=jnp.float32)
            d = jnp.where(column < W1, first, second)
            out_held[s] = jnp.concatenate([d[:half], d[half:]], axis=1).astype(jnp.bfloat16)
        at = pl.ds(i * step, step)
        stores.append(pltpu.make_async_copy(out_held.at[at], out_ref.at[at], out_sems.at[i]))
        stores[-1].start()
    for store in stores:
        store.wait()


def narrow_dpool(place, g12, w12, after=()):
    slots, count, _ = g12.shape
    blocks = 4
    shape = (slots, count // 2, 2 * W12)
    return pl.pallas_call(
        functools.partial(narrow_kernel, blocks),
        out_shape=jax.ShapeDtypeStruct(shape, jnp.bfloat16),
        grid_spec=pltpu.PrefetchScalarGridSpec(
            num_scalar_prefetch=1,
            grid=(1,),
            in_specs=[HBM] * 2 + [ANY] * len(after),
            out_specs=HBM,
            scratch_shapes=[
                pltpu.VMEM(g12.shape, jnp.bfloat16),
                pltpu.VMEM(w12.shape, jnp.bfloat16),
                pltpu.VMEM(shape, jnp.bfloat16),
                pltpu.SemaphoreType.DMA((blocks,)),
                pltpu.SemaphoreType.DMA((1,)),
                pltpu.SemaphoreType.DMA((blocks,)),
            ],
        ),
        compiler_params=params(1),
        cost_estimate=cost(4e9),
        name="narrow_dpool",
    )(place, g12, w12, *after)


def partial_kernel(ins, added, results, node_ref, line_ref, *refs):
    blocks, size = node_ref.shape[0], line_ref.shape[0]
    operands, others = refs[:ins], refs[ins : ins + added]
    outs, scratch = refs[-3 - 2 * results - ins - added :][:results], refs[-3 - results - ins - added :]
    held, other_held, out_held = scratch[:ins], scratch[ins : ins + added], scratch[ins + added : -3]
    in_sems, other_sems, out_sems = scratch[-3:]

    def block(arrays, i):
        per = blocks // len(arrays)
        return arrays[i // per].at[pl.ds(i % per * size, size)]

    loads = [
        fetch(ref, at, in_sems.at[n], blocks, lambda i: node_ref[i])
        for n, (ref, at) in enumerate(zip(operands, held))
    ]
    if added:
        loads.append(
            [
                pltpu.make_async_copy(block(others, i), block(other_held, i), other_sems.at[i])
                for i in range(blocks)
            ]
        )
        for copy in loads[-1]:
            copy.start()
    stores = []
    for i in range(blocks):
        for copies in loads:
            copies[i].wait()
        out = block(out_held, i)
        for l in range(size):
            slot = i * size + line_ref[l]
            q = held[0][slot].T
            narrow = jnp.dot(q[:W12], held[1][slot], preferred_element_type=jnp.float32)
            wide = jnp.dot(q[W12:], held[2][slot], preferred_element_type=jnp.float32)
            pieces = ((0, W1, narrow[:W1, :PD]), (W1, W12, narrow[W1:, PD:]), (W12, WSUM, wide))
            for start, end, piece in pieces:
                if added:
                    piece = piece + block(other_held, i)[l, start:end]
                out[l, start:end] = piece.astype(out.dtype)
        stores.append(pltpu.make_async_copy(out, block(outs, i), out_sems.at[i]))
        stores[-1].start()
    for store in stores:
        store.wait()


def partial_proj(nodes, lines, q, g12, g3, results, others=()):
    _, count, _ = q.shape
    blocks, size = nodes.shape[0], lines.shape[0]
    kinds = [jnp.bfloat16 if others and i else jnp.float32 for i in range(results)]
    shapes = [jax.ShapeDtypeStruct((blocks // results * size, WSUM, PD), kind) for kind in kinds]
    operands = (q, g12, g3)
    return pl.pallas_call(
        functools.partial(partial_kernel, len(operands), len(others), results),
        out_shape=shapes,
        grid_spec=pltpu.PrefetchScalarGridSpec(
            num_scalar_prefetch=2,
            grid=(1,),
            in_specs=[HBM] * len(operands) + [ANY] * len(others),
            out_specs=[HBM] * results,
            scratch_shapes=[pltpu.VMEM((blocks * size, count, x.shape[2]), jnp.bfloat16) for x in operands]
            + [pltpu.VMEM(x.shape, x.dtype) for x in others]
            + [pltpu.VMEM(x.shape, x.dtype) for x in shapes]
            + [
                pltpu.SemaphoreType.DMA((len(operands), blocks)),
                pltpu.SemaphoreType.DMA((blocks,)),
                pltpu.SemaphoreType.DMA((blocks,)),
            ],
        ),
        compiler_params=params(1),
        cost_estimate=cost(4e9 if others else 1e7),
        name="partial_proj",
    )(nodes, lines, *operands, *others)


def count_kernel(index_ref, length_ref, *refs):
    out_ref = refs[-1]
    bag, block = index_ref.shape[1], index_ref.shape[2]
    lanes, chunk, low = 256, 16, ROWS // 8

    def one(i, carry):
        at = pl.ds(pl.multiple_of(i * lanes, lanes), lanes)
        index = index_ref[0, :, at]
        which = lax.broadcasted_iota(jnp.int32, (bag, lanes), 0)
        key = jnp.where(which < length_ref[0, :, at], index & (low - 1), -1)
        unit = jnp.left_shift(jnp.int32(1), jnp.right_shift(index, 6) * 4)
        ids = lax.broadcasted_iota(jnp.int32, (chunk, lanes), 0)
        for c in range(low // chunk):
            total = jnp.zeros((chunk, lanes), jnp.int32)
            for j in range(bag):
                total = total + jnp.where(key[j : j + 1] == ids + c * chunk, unit[j : j + 1], 0)
            out_ref[0, c * chunk : (c + 1) * chunk, at] = total
        return carry

    lax.fori_loop(0, block // lanes, one, 0)


def count_hits(lookups, counts, after=()):
    tables, bag, examples = lookups.shape
    block = 4096
    return pl.pallas_call(
        count_kernel,
        out_shape=jax.ShapeDtypeStruct((tables, ROWS // 8, examples), jnp.int32),
        grid=(tables, examples // block),
        in_specs=[
            pl.BlockSpec((1, bag, block), lambda k, i: (k, 0, i)),
            pl.BlockSpec((1, 1, block), lambda k, i: (k, 0, i)),
        ]
        + [ANY] * len(after),
        out_specs=pl.BlockSpec((1, ROWS // 8, block), lambda k, i: (k, 0, i)),
        compiler_params=params(2),
        cost_estimate=cost(5e9),
        name="count_hits",
    )(lookups, counts, *after)


def unpacked(words):
    rows = [lax.shift_right_logical(words, jnp.int32(4 * n)) & 15 for n in range(8)]
    return jnp.concatenate([r.astype(jnp.float32).astype(jnp.bfloat16) for r in rows], axis=0)


def wide_kernel(hits_ref, g_ref, w_ref, *refs):
    out_ref = refs[-1]

    @pl.when(pl.program_id(0) == 0)
    def _():
        out_ref[...] = jnp.zeros_like(out_ref)

    block = g_ref.shape[0]
    column = lax.broadcasted_iota(jnp.int32, (block, WSUM), 1)
    d = lax.dot_general(g_ref[...], w_ref[...], (((1,), (1,)), ((), ())), preferred_element_type=jnp.float32)
    d = jnp.where(column < W12, 0.0, d).astype(jnp.bfloat16)
    out_ref[...] += jnp.dot(unpacked(hits_ref[0]), d, preferred_element_type=jnp.float32)


def wide_sum(hits, g3, weights, after=()):
    _, words, examples = hits.shape
    block = 1024
    return pl.pallas_call(
        wide_kernel,
        out_shape=jax.ShapeDtypeStruct((ROWS, WSUM), jnp.float32),
        grid=(examples // block,),
        in_specs=[
            pl.BlockSpec((1, words, block), lambda i: (2, 0, i)),
            pl.BlockSpec((block, PD), lambda i: (i, 0)),
            pl.BlockSpec((WSUM, PD), lambda i: (0, 0)),
        ]
        + [ANY] * len(after),
        out_specs=pl.BlockSpec((ROWS, WSUM), lambda i: (0, 0)),
        compiler_params=params(1),
        cost_estimate=cost(1e7),
        name="wide_sum",
    )(hits, g3, weights, *after)


def narrow_sum_kernel(hits_ref, d_ref, wide_ref, *refs):
    out_ref = refs[-1]

    @pl.when(pl.program_id(0) == 0)
    def _():
        out_ref[...] = wide_ref[...]

    sources = d_ref.shape[0]
    block = hits_ref.shape[2]
    column = lax.broadcasted_iota(jnp.int32, (block, PD), 1)
    pieces = []
    for d in range(sources):
        packed = d_ref[d].astype(jnp.float32)
        pieces += [packed, pltpu.roll(packed, PD - W12, 1)]
    both = jnp.concatenate(pieces, axis=0)
    d1 = jnp.where(column < W1, both, 0.0).astype(jnp.bfloat16)
    d2 = jnp.where((column >= W1) & (column < W12), both, 0.0).astype(jnp.bfloat16)
    out_ref[...] += jnp.dot(unpacked(hits_ref[0]), d1, preferred_element_type=jnp.float32) + jnp.dot(
        unpacked(hits_ref[1]), d2, preferred_element_type=jnp.float32
    )


def narrow_sum(hits, narrow, wide, after=()):
    _, words, examples = hits.shape
    sources, half, _ = narrow.shape
    block = 1024
    per = block // (2 * half)
    return pl.pallas_call(
        narrow_sum_kernel,
        out_shape=jax.ShapeDtypeStruct((ROWS, WSUM), jnp.float32),
        grid=(examples // block,),
        in_specs=[
            pl.BlockSpec((2, words, block), lambda i: (0, 0, i)),
            pl.BlockSpec((per, half, 2 * W12), lambda i: (i, 0, 0)),
            pl.BlockSpec((ROWS, PD), lambda i: (0, 0)),
        ]
        + [ANY] * len(after),
        out_specs=pl.BlockSpec((ROWS, PD), lambda i: (0, 0)),
        input_output_aliases={2: 0},
        compiler_params=params(1),
        cost_estimate=cost(1e7),
        name="narrow_sum",
    )(hits, narrow, wide, *after)


def plane_kernel(terms, kept_ref, *refs):
    own_ref, outs = refs[terms + 1], refs[terms + 2 :]
    for i in range(kept_ref.shape[0]):
        total = kept_ref[i]
        for term in refs[:terms]:
            total = total + term[i].astype(jnp.float32)
        if i == 0:
            own_ref[0] = total
        else:
            outs[i - 1][0] = total.astype(jnp.bfloat16)


def plane_sum(kept, arrived, after):
    vmem = pl.BlockSpec(memory_space=pltpu.VMEM)
    others = kept.shape[0] - 1
    shape = (1,) + kept.shape[1:]
    return pl.pallas_call(
        functools.partial(plane_kernel, len(arrived)),
        out_shape=[jax.ShapeDtypeStruct(shape, jnp.float32)] + [jax.ShapeDtypeStruct(shape, jnp.bfloat16)] * others,
        in_specs=[vmem] * (1 + len(arrived)) + [ANY],
        out_specs=[vmem] * (1 + others),
        compiler_params=pltpu.CompilerParams(vmem_limit_bytes=16 * MIB),
        cost_estimate=cost(9e9),
        name="plane_sum",
    )(kept, *arrived, after)


def swap(x, axis, size, bits):
    return lax.ppermute(x, axis, [(d, d ^ bits) for d in range(size)])


def local(sizes, grad_out, pooled, proj, assign, indices, lengths):
    count, slots, _ = grad_out.shape
    scale = 1.0 / math.sqrt(count * slots)
    n_node, n_local = sizes["node"], sizes["local"]
    n_plane = n_node // 2
    node, loc = lax.axis_index("node"), lax.axis_index("local")

    rows = proj[:, :W12]
    rows = jnp.concatenate([rows] + [swap(rows, "local", n_local, d) for d in range(1, n_local)])
    g12, g3, q = permute(assign, grad_out, pooled)
    rows, g3 = lax.optimization_barrier((rows, g3))
    g3_got = lax.all_to_all(g3, AXES, split_axis=0, concat_axis=0, tiled=True)

    plane = jnp.arange(n_plane, dtype=jnp.int32) ^ (node // 2)
    lines = jnp.arange(n_local, dtype=jnp.int32) ^ loc
    sent = partial_proj(plane * 2 + 1 - node % 2, lines, q, g12, g3, 2)
    got = [swap(x, "node", n_node, 1) for x in sent]

    rows, sent = lax.optimization_barrier((rows, sent))
    rows = jnp.concatenate([rows] + [swap(rows, "node", n_node, 2 * d) for d in range(1, n_plane)])
    hits = count_hits(indices[0].transpose(1, 2, 0), lengths[0].T[:, None, :], after=sent[:1])
    kept = partial_proj(plane * 2 + node % 2, lines, q, g12, g3, n_plane, got)
    rows = jnp.concatenate([rows, swap(rows, "node", n_node, 1)])
    slot = jnp.arange(slots, dtype=jnp.int32)
    slot_node = slot // n_local ^ node
    slot_place = slot_node % 2 * (slots // 2) + slot_node // 2 * n_local + (slot % n_local ^ loc)
    narrow = narrow_dpool(slot_place, g12, rows, after=kept[:1])

    narrow, hits, g3_got, kept = lax.optimization_barrier((narrow, hits, g3_got, kept))
    narrow_got = lax.all_to_all(narrow, AXES, split_axis=0, concat_axis=0, tiled=True)
    wide = wide_sum(hits, g3_got.reshape(-1, PD), proj[0])
    arrived = [swap(kept[d], "node", n_node, 2 * d) for d in range(1, n_plane)]
    own, *sums = plane_sum(kept[0], arrived, wide)
    terms = [swap(x, "local", n_local, d) for d, x in enumerate(sums, 1)]

    table_grad = narrow_sum(hits, narrow_got, wide)[None]
    terms, table_grad = lax.optimization_barrier((terms, table_grad))
    proj_grad = sum((term.astype(jnp.float32) for term in terms), own) * scale
    return (table_grad, proj_grad)


def solution(mesh):
    placed = (
        P(AXES, None, None),
        P(AXES, None, None),
        P(AXES, None, None),
        P(),
        P(AXES, None, None, None),
        P(AXES, None, None),
    )
    return jax.shard_map(
        functools.partial(local, dict(mesh.shape)),
        mesh=mesh,
        in_specs=placed,
        out_specs=(P(AXES, None, None), P(AXES, None, None)),
        check_vma=False,
    )
```

profile of v0, /device:TPU:0, one launch (start us, length us, event | category | flops | bytes accessed | tf_op | source)
XLA Modules:
  0.0 81.0 jit_solution(17603357656369369194)
XLA Ops:
  0.6 0.7 slice.3
  1.4 5.0 %collective-permute-start.2 = (bf16[1,64,128]{2,1,0:T(8,128)(2,1)S(1)}, bf16[1,64,128]{2,1,0:T(8,128)(2,1)S(1)}, u32[]{:S(2)}, u32[]{:S(2)}) collective-permute-start(bf16[1,64,128]{2,1,0:T(8,128)(2,1)S(1)} %slice.3), channel_id=1, source_target_pairs={{0,3},{1,2},{2,1},{3,0},{4,7},{5,6},{6,5},{7,4},{8,11},{9,10},{10,... | collective-permute-start | bytes 49160 | tf_op jit(solution)/shard_map/ppermute | solution.py:389
  7.5 6.4 %permute_groups.1 = (bf16[32,128,256]{2,1,0:T(8,128)(2,1)}, bf16[32,128,128]{2,1,0:T(8,128)(2,1)}, bf16[32,128,256]{2,1,0:T(8,128)(2,1)}) custom-call(s32[32]{0:T(128)} %assign_ref.1, bf16[128,32,384]{2,1,0:T(8,128)(2,1)} %grad_ref.1, bf16[128,32,256]{2,1,0:T(8,128)(2,1)} %pool_ref.1), custom_call_target="tpu_custom_call" | custom-call | flops 10000000 | bytes 1024 | tf_op jit(solution)/shard_map/permute_groups/pallas_call | solution.py:78
  14.0 6.1 %all-to-all-start = ((bf16[32,128,128]{2,1,0:T(8,128)(2,1)}), bf16[32,128,128]{2,1,0:T(8,128)(2,1)S(1)}, u32[]{:S(2)}, u32[]{:S(2)}) async-start(bf16[32,128,128]{2,1,0:T(8,128)(2,1)} %get-tuple-element.34.refs_2_), calls=%async_computation | async-start | bytes 2097152 | tf_op jit(solution)/shard_map/all_to_all | solution.py:403
  21.8 4.3 %partial_proj.2 = (f32[8,256,128]{2,1,0:T(8,128)}, f32[8,256,128]{2,1,0:T(8,128)}) custom-call(s32[4]{0:T(128)} %get-tuple-element.59.node_ref, s32[4]{0:T(128)} %get-tuple-element.58.line_ref, bf16[32,128,256]{2,1,0:T(8,128)(2,1)} %get-tuple-element.33.refs_0_, bf16[32,128,256]{2,1,0:T(8,128)(2,1)} %get-tuple-element.30.refs_1_.g_ref, ...), custom_call_target="tpu_custom_call" | custom-call | flops 10000000 | bytes 1024 | tf_op jit(solution)/shard_map/partial_proj/pallas_call | solution.py:213
  26.2 1.8 %collective-permute-start.3 = (bf16[4,64,128]{2,1,0:T(8,128)(2,1)S(1)}, bf16[4,64,128]{2,1,0:T(8,128)(2,1)S(1)}, u32[]{:S(2)}, u32[]{:S(2)}) collective-permute-start(bf16[4,64,128]{2,1,0:T(8,128)(2,1)S(1)} %pad_maximum_fusion.1), channel_id=1, source_target_pairs={{0,8},{4,12},{8,0},{12,4},{16,24},{20,28},{24,16},{28,20},{1,9},{5... | collective-permute-start | bytes 196616 | tf_op jit(solution)/shard_map/ppermute | solution.py:389
  28.0 1.5 %collective-permute-start.4 = (bf16[4,64,128]{2,1,0:T(8,128)(2,1)S(1)}, bf16[4,64,128]{2,1,0:T(8,128)(2,1)S(1)}, u32[]{:S(2)}, u32[]{:S(2)}) collective-permute-start(bf16[4,64,128]{2,1,0:T(8,128)(2,1)S(1)} %pad_maximum_fusion.1), channel_id=1, source_target_pairs={{0,16},{4,20},{8,24},{12,28},{16,0},{20,4},{24,8},{28,12},{1,17},{... | collective-permute-start | bytes 196616 | tf_op jit(solution)/shard_map/ppermute | solution.py:389
  30.2 5.0 %count_hits.1.hits_ref = s32[3,64,4096]{2,1,0:T(8,128)} custom-call(s32[3,8,4096]{2,1,0:T(8,128)} %bitcast.15, s32[3,1,4096]{2,1,0:T(1,128)} %broadcast_in_dim.6.length_ref, f32[8,256,128]{2,1,0:T(8,128)} %get-tuple-element.39.refs_0_), custom_call_target="tpu_custom_call" | custom-call | flops 5000000000 | bytes 1024 | tf_op jit(solution)/shard_map/count_hits/pallas_call | solution.py:261
  35.4 1.5 %collective-permute-done.6 = bf16[16,64,128]{2,1,0:T(8,128)(2,1)S(1)} collective-permute-done((bf16[16,64,128]{2,1,0:T(8,128)(2,1)S(1)}, bf16[16,64,128]{2,1,0:T(8,128)(2,1)S(1)}, u32[]{:S(2)}, u32[]{:S(2)}) %collective-permute-start.6) | collective-permute-done | bytes 262176 | tf_op jit(solution)/shard_map/ppermute | solution.py:389
  37.0 1.0 %copy-done.6 = f32[8,256,128]{2,1,0:T(8,128)} copy-done((f32[8,256,128]{2,1,0:T(8,128)}, f32[8,256,128]{2,1,0:T(8,128)S(1)}, u32[]{:S(2)}) %copy-start.6) | copy-done | bytes 1048600
  38.0 1.0 %copy-done.7 = f32[8,256,128]{2,1,0:T(8,128)} copy-done((f32[8,256,128]{2,1,0:T(8,128)}, f32[8,256,128]{2,1,0:T(8,128)S(1)}, u32[]{:S(2)}) %copy-start.7) | copy-done | bytes 1048600
  39.0 4.4 %partial_proj.3 = (f32[4,256,128]{2,1,0:T(8,128)}, bf16[4,256,128]{2,1,0:T(8,128)(2,1)}, bf16[4,256,128]{2,1,0:T(8,128)(2,1)}, bf16[4,256,128]{2,1,0:T(8,128)(2,1)}) custom-call(s32[4]{0:T(128)} %fusion.5.node_ref, s32[4]{0:T(128)} %get-tuple-element.58.line_ref, bf16[32,128,256]{2,1,0:T(8,128)(2,1)} %get-tuple-element.33.refs_0_, ...), custom_call_target="tpu_custom_call" | custom-call | flops 4000000000 | bytes 1024 | tf_op jit(solution)/shard_map/partial_proj/pallas_call | solution.py:213
  43.5 4.5 %narrow_dpool.1 = bf16[32,64,128]{2,1,0:T(8,128)(2,1)} custom-call(s32[32]{0:T(128)} %fusion.1.place_ref, bf16[32,128,256]{2,1,0:T(8,128)(2,1)} %get-tuple-element.30.refs_1_.g_ref, bf16[32,64,128]{2,1,0:T(8,128)(2,1)} %copy-done.5, f32[4,256,128]{2,1,0:T(8,128)} %get-tuple-element.43.refs_0_.kept_ref), custom_call_target="tpu_custom_call" | custom-call | flops 4000000000 | bytes 1024 | tf_op jit(solution)/shard_map/narrow_dpool/pallas_call | solution.py:139
  48.0 1.8 %collective-permute-start.9 = (bf16[4,256,128]{2,1,0:T(8,128)(2,1)S(1)}, bf16[4,256,128]{2,1,0:T(8,128)(2,1)S(1)}, u32[]{:S(2)}, u32[]{:S(2)}) collective-permute-start(bf16[4,256,128]{2,1,0:T(8,128)(2,1)S(1)} %copy-done.10), channel_id=1, source_target_pairs={{0,8},{4,12},{8,0},{12,4},{16,24},{20,28},{24,16},{28,20},{1,9},{5... | collective-permute-start | bytes 786440 | tf_op jit(solution)/shard_map/ppermute | solution.py:389
  49.8 1.5 %collective-permute-start.10 = (bf16[4,256,128]{2,1,0:T(8,128)(2,1)S(1)}, bf16[4,256,128]{2,1,0:T(8,128)(2,1)S(1)}, u32[]{:S(2)}, u32[]{:S(2)}) collective-permute-start(bf16[4,256,128]{2,1,0:T(8,128)(2,1)S(1)} %copy-done.9), channel_id=1, source_target_pairs={{0,16},{4,20},{8,24},{12,28},{16,0},{20,4},{24,8},{28,12},{1,17},{... | collective-permute-start | bytes 786440 | tf_op jit(solution)/shard_map/ppermute | solution.py:389
  51.6 5.8 %all-to-all-start.1 = ((bf16[32,64,128]{2,1,0:T(8,128)(2,1)}), bf16[32,64,128]{2,1,0:T(8,128)(2,1)S(1)}, u32[]{:S(2)}, u32[]{:S(2)}) async-start(bf16[32,64,128]{2,1,0:T(8,128)(2,1)} %narrow_dpool.1), calls=%async_computation.1 | async-start | bytes 1048576 | tf_op jit(solution)/shard_map/all_to_all | solution.py:421
  57.4 5.5 %wide_sum.1.refs_3_.wide_ref = f32[512,256]{1,0:T(8,128)} custom-call(s32[3,64,4096]{2,1,0:T(8,128)} %count_hits.1.hits_ref, bf16[4096,128]{1,0:T(8,128)(2,1)} %bitcast.12, bf16[256,128]{1,0:T(8,128)(2,1)} %bitcast.14), custom_call_target="tpu_custom_call" | custom-call | flops 10000000 | bytes 1024 | tf_op jit(solution)/shard_map/wide_sum/pallas_call | solution.py:299
  62.9 3.7 %collective-permute-done.10.refs_1_ = bf16[4,256,128]{2,1,0:T(8,128)(2,1)S(1)} collective-permute-done((bf16[4,256,128]{2,1,0:T(8,128)(2,1)S(1)}, bf16[4,256,128]{2,1,0:T(8,128)(2,1)S(1)}, u32[]{:S(2)}, u32[]{:S(2)}) %collective-permute-start.10) | collective-permute-done | bytes 262176 | tf_op jit(solution)/shard_map/ppermute | solution.py:389
  66.6 1.0 %copy-done = f32[512,256]{1,0:T(8,128)S(1)} copy-done((f32[512,256]{1,0:T(8,128)S(1)}, f32[512,256]{1,0:T(8,128)}, u32[]{:S(2)}) %copy-start) | copy-done | bytes 524312
  67.8 1.7 %collective-permute-start.12 = (bf16[1,256,128]{2,1,0:T(8,128)(2,1)S(1)}, bf16[1,256,128]{2,1,0:T(8,128)(2,1)S(1)}, u32[]{:S(2)}, u32[]{:S(2)}) collective-permute-start(bf16[1,256,128]{2,1,0:T(8,128)(2,1)S(1)} %get-tuple-element.49), channel_id=1, source_target_pairs={{0,1},{1,0},{2,3},{3,2},{4,5},{5,4},{6,7},{7,6},{8,9},{9,8},{10,11... | collective-permute-start | bytes 196616 | tf_op jit(solution)/shard_map/ppermute | solution.py:389
  69.4 3.5 %collective-permute-start.13 = (bf16[1,256,128]{2,1,0:T(8,128)(2,1)S(1)}, bf16[1,256,128]{2,1,0:T(8,128)(2,1)S(1)}, u32[]{:S(2)}, u32[]{:S(2)}) collective-permute-start(bf16[1,256,128]{2,1,0:T(8,128)(2,1)S(1)} %get-tuple-element.50), channel_id=1, source_target_pairs={{0,2},{1,3},{2,0},{3,1},{4,6},{5,7},{6,4},{7,5},{8,10},{9,11},{10,... | collective-permute-start | bytes 196616 | tf_op jit(solution)/shard_map/ppermute | solution.py:389
  73.0 1.1 %collective-permute-start.14 = (bf16[1,256,128]{2,1,0:T(8,128)(2,1)S(1)}, bf16[1,256,128]{2,1,0:T(8,128)(2,1)S(1)}, u32[]{:S(2)}, u32[]{:S(2)}) collective-permute-start(bf16[1,256,128]{2,1,0:T(8,128)(2,1)S(1)} %get-tuple-element.51), channel_id=1, source_target_pairs={{0,3},{1,2},{2,1},{3,0},{4,7},{5,6},{6,5},{7,4},{8,11},{9,10},{10,... | collective-permute-start | bytes 196616 | tf_op jit(solution)/shard_map/ppermute | solution.py:389
  74.1 0.8 copy-done.3
  74.9 5.4 %narrow_sum.1 = f32[512,256]{1,0:T(8,128)} custom-call(s32[3,64,4096]{2,1,0:T(8,128)} %count_hits.1.hits_ref, bf16[32,64,128]{2,1,0:T(8,128)(2,1)} %copy-done.3, f32[512,256]{1,0:T(8,128)} %wide_sum.1.refs_3_.wide_ref), custom_call_target="tpu_custom_call", output_to_operand_aliasing={{}: (2, {})} | custom-call | flops 10000000 | bytes 1024 | tf_op jit(solution)/shard_map/narrow_sum/pallas_call | solution.py:343
  (54 shorter events, 5.0 us)
Async XLA Ops:
  1.4 12.6 %collective-permute-start.2 = (bf16[1,64,128]{2,1,0:T(8,128)(2,1)S(1)}, bf16[1,64,128]{2,1,0:T(8,128)(2,1)S(1)}, u32[]{:S(2)}, u32[]{:S(2)}) collective-permute-start(bf16[1,64,128]{2,1,0:T(8,128)(2,1)S(1)} %slice.3), channel_id=1, source_target_pairs={{0,3},{1,2},{2,1},{3,0},{4,7},{5,6},{6,5},{7,4},{8,11},{9,10},{10,... | collective-permute-start | bytes 49160 | tf_op jit(solution)/shard_map/ppermute | solution.py:389
  6.4 7.5 %collective-permute-start.1 = (bf16[1,64,128]{2,1,0:T(8,128)(2,1)S(1)}, bf16[1,64,128]{2,1,0:T(8,128)(2,1)S(1)}, u32[]{:S(2)}, u32[]{:S(2)}) collective-permute-start(bf16[1,64,128]{2,1,0:T(8,128)(2,1)S(1)} %slice.3), channel_id=1, source_target_pairs={{0,2},{1,3},{2,0},{3,1},{4,6},{5,7},{6,4},{7,5},{8,10},{9,11},{10,... | collective-permute-start | bytes 49160 | tf_op jit(solution)/shard_map/ppermute | solution.py:389
  6.4 7.5 %collective-permute-start = (bf16[1,64,128]{2,1,0:T(8,128)(2,1)S(1)}, bf16[1,64,128]{2,1,0:T(8,128)(2,1)S(1)}, u32[]{:S(2)}, u32[]{:S(2)}) collective-permute-start(bf16[1,64,128]{2,1,0:T(8,128)(2,1)S(1)} %slice.3), channel_id=1, source_target_pairs={{0,1},{1,0},{2,3},{3,2},{4,5},{5,4},{6,7},{7,6},{8,9},{9,8},{10,11... | collective-permute-start | bytes 49160 | tf_op jit(solution)/shard_map/ppermute | solution.py:389
  13.9 6.6 %copy-start.4 = (s32[1,4096,3]{1,0,2:T(1,128)S(1)}, s32[1,4096,3]{1,0,2:T(1,128)}, u32[]{:S(2)}) copy-start(s32[1,4096,3]{1,0,2:T(1,128)} %param.11) | copy-start | bytes 147460
  14.0 34.0 %all-to-all-start = ((bf16[32,128,128]{2,1,0:T(8,128)(2,1)}), bf16[32,128,128]{2,1,0:T(8,128)(2,1)S(1)}, u32[]{:S(2)}, u32[]{:S(2)}) async-start(bf16[32,128,128]{2,1,0:T(8,128)(2,1)} %get-tuple-element.34.refs_2_), calls=%async_computation | async-start | bytes 2097152 | tf_op jit(solution)/shard_map/all_to_all | solution.py:403
  26.2 9.0 %collective-permute-start.3 = (bf16[4,64,128]{2,1,0:T(8,128)(2,1)S(1)}, bf16[4,64,128]{2,1,0:T(8,128)(2,1)S(1)}, u32[]{:S(2)}, u32[]{:S(2)}) collective-permute-start(bf16[4,64,128]{2,1,0:T(8,128)(2,1)S(1)} %pad_maximum_fusion.1), channel_id=1, source_target_pairs={{0,8},{4,12},{8,0},{12,4},{16,24},{20,28},{24,16},{28,20},{1,9},{5... | collective-permute-start | bytes 196616 | tf_op jit(solution)/shard_map/ppermute | solution.py:389
  28.0 7.2 %collective-permute-start.4 = (bf16[4,64,128]{2,1,0:T(8,128)(2,1)S(1)}, bf16[4,64,128]{2,1,0:T(8,128)(2,1)S(1)}, u32[]{:S(2)}, u32[]{:S(2)}) collective-permute-start(bf16[4,64,128]{2,1,0:T(8,128)(2,1)S(1)} %pad_maximum_fusion.1), channel_id=1, source_target_pairs={{0,16},{4,20},{8,24},{12,28},{16,0},{20,4},{24,8},{28,12},{1,17},{... | collective-permute-start | bytes 196616 | tf_op jit(solution)/shard_map/ppermute | solution.py:389
  29.5 5.8 %collective-permute-start.5 = (bf16[4,64,128]{2,1,0:T(8,128)(2,1)S(1)}, bf16[4,64,128]{2,1,0:T(8,128)(2,1)S(1)}, u32[]{:S(2)}, u32[]{:S(2)}) collective-permute-start(bf16[4,64,128]{2,1,0:T(8,128)(2,1)S(1)} %pad_maximum_fusion.1), channel_id=1, source_target_pairs={{0,24},{4,28},{8,16},{12,20},{16,8},{20,12},{24,0},{28,4},{1,25},{... | collective-permute-start | bytes 196616 | tf_op jit(solution)/shard_map/ppermute | solution.py:389
  29.7 7.2 %collective-permute-start.7 = (f32[8,256,128]{2,1,0:T(8,128)}, f32[8,256,128]{2,1,0:T(8,128)S(1)}, u32[]{:S(2)}, u32[]{:S(2)}) collective-permute-start(f32[8,256,128]{2,1,0:T(8,128)} %get-tuple-element.39.refs_0_), channel_id=1, source_target_pairs={{0,4},{4,0},{8,12},{12,8},{16,20},{20,16},{24,28},{28,24},{1,5},{5... | collective-permute-start | bytes 3145736 | tf_op jit(solution)/shard_map/ppermute | solution.py:389
  29.7 7.2 %collective-permute-start.8 = (f32[8,256,128]{2,1,0:T(8,128)}, f32[8,256,128]{2,1,0:T(8,128)S(1)}, u32[]{:S(2)}, u32[]{:S(2)}) collective-permute-start(f32[8,256,128]{2,1,0:T(8,128)} %get-tuple-element.36), channel_id=1, source_target_pairs={{0,4},{4,0},{8,12},{12,8},{16,20},{20,16},{24,28},{28,24},{1,5},{5... | collective-permute-start | bytes 3145736 | tf_op jit(solution)/shard_map/ppermute | solution.py:389
  35.3 1.6 %collective-permute-start.6 = (bf16[16,64,128]{2,1,0:T(8,128)(2,1)S(1)}, bf16[16,64,128]{2,1,0:T(8,128)(2,1)S(1)}, u32[]{:S(2)}, u32[]{:S(2)}) collective-permute-start(bf16[16,64,128]{2,1,0:T(8,128)(2,1)S(1)} %pad_maximum_fusion), channel_id=1, source_target_pairs={{0,4},{4,0},{8,12},{12,8},{16,20},{20,16},{24,28},{28,24},{1,5},{5... | collective-permute-start | bytes 786440 | tf_op jit(solution)/shard_map/ppermute | solution.py:389
  36.9 6.5 %copy-start.5 = (bf16[32,64,128]{2,1,0:T(8,128)(2,1)}, bf16[32,64,128]{2,1,0:T(8,128)(2,1)S(1)}, u32[]{:S(2)}) copy-start(bf16[32,64,128]{2,1,0:T(8,128)(2,1)S(1)} %constant_dynamic-update-slice_fusion.w_ref) | copy-start | bytes 1572868
  43.4 4.5 %copy-start.10 = (bf16[4,256,128]{2,1,0:T(8,128)(2,1)S(1)}, bf16[4,256,128]{2,1,0:T(8,128)(2,1)}, u32[]{:S(2)}) copy-start(bf16[4,256,128]{2,1,0:T(8,128)(2,1)} %get-tuple-element.44) | copy-start | bytes 786436
  43.4 6.4 %copy-start.9 = (bf16[4,256,128]{2,1,0:T(8,128)(2,1)S(1)}, bf16[4,256,128]{2,1,0:T(8,128)(2,1)}, u32[]{:S(2)}) copy-start(bf16[4,256,128]{2,1,0:T(8,128)(2,1)} %get-tuple-element.45) | copy-start | bytes 786436
  43.5 7.9 %copy-start.8 = (bf16[4,256,128]{2,1,0:T(8,128)(2,1)S(1)}, bf16[4,256,128]{2,1,0:T(8,128)(2,1)}, u32[]{:S(2)}) copy-start(bf16[4,256,128]{2,1,0:T(8,128)(2,1)} %get-tuple-element.46) | copy-start | bytes 786436
  48.0 9.4 %copy-start.2 = (bf16[32,128,128]{2,1,0:T(8,128)(2,1)}, bf16[32,128,128]{2,1,0:T(8,128)(2,1)S(1)}, u32[]{:S(2)}) copy-start(bf16[32,128,128]{2,1,0:T(8,128)(2,1)S(1)} %all-to-all-done) | copy-start | bytes 3145732
  48.0 14.9 %collective-permute-start.9 = (bf16[4,256,128]{2,1,0:T(8,128)(2,1)S(1)}, bf16[4,256,128]{2,1,0:T(8,128)(2,1)S(1)}, u32[]{:S(2)}, u32[]{:S(2)}) collective-permute-start(bf16[4,256,128]{2,1,0:T(8,128)(2,1)S(1)} %copy-done.10), channel_id=1, source_target_pairs={{0,8},{4,12},{8,0},{12,4},{16,24},{20,28},{24,16},{28,20},{1,9},{5... | collective-permute-start | bytes 786440 | tf_op jit(solution)/shard_map/ppermute | solution.py:389
  49.8 16.8 %collective-permute-start.10 = (bf16[4,256,128]{2,1,0:T(8,128)(2,1)S(1)}, bf16[4,256,128]{2,1,0:T(8,128)(2,1)S(1)}, u32[]{:S(2)}, u32[]{:S(2)}) collective-permute-start(bf16[4,256,128]{2,1,0:T(8,128)(2,1)S(1)} %copy-done.9), channel_id=1, source_target_pairs={{0,16},{4,20},{8,24},{12,28},{16,0},{20,4},{24,8},{28,12},{1,17},{... | collective-permute-start | bytes 786440 | tf_op jit(solution)/shard_map/ppermute | solution.py:389
  51.3 15.3 %collective-permute-start.11 = (bf16[4,256,128]{2,1,0:T(8,128)(2,1)S(1)}, bf16[4,256,128]{2,1,0:T(8,128)(2,1)S(1)}, u32[]{:S(2)}, u32[]{:S(2)}) collective-permute-start(bf16[4,256,128]{2,1,0:T(8,128)(2,1)S(1)} %copy-done.8), channel_id=1, source_target_pairs={{0,24},{4,28},{8,16},{12,20},{16,8},{20,12},{24,0},{28,4},{1,25},{... | collective-permute-start | bytes 786440 | tf_op jit(solution)/shard_map/ppermute | solution.py:389
  51.6 22.5 %all-to-all-start.1 = ((bf16[32,64,128]{2,1,0:T(8,128)(2,1)}), bf16[32,64,128]{2,1,0:T(8,128)(2,1)S(1)}, u32[]{:S(2)}, u32[]{:S(2)}) async-start(bf16[32,64,128]{2,1,0:T(8,128)(2,1)} %narrow_dpool.1), calls=%async_computation.1 | async-start | bytes 1048576 | tf_op jit(solution)/shard_map/all_to_all | solution.py:421
  57.4 9.2 %copy-start.1 = (f32[4,256,128]{2,1,0:T(8,128)S(1)}, f32[4,256,128]{2,1,0:T(8,128)}, u32[]{:S(2)}) copy-start(f32[4,256,128]{2,1,0:T(8,128)} %get-tuple-element.43.refs_0_.kept_ref) | copy-start | bytes 1572868
  67.8 12.5 %collective-permute-start.12 = (bf16[1,256,128]{2,1,0:T(8,128)(2,1)S(1)}, bf16[1,256,128]{2,1,0:T(8,128)(2,1)S(1)}, u32[]{:S(2)}, u32[]{:S(2)}) collective-permute-start(bf16[1,256,128]{2,1,0:T(8,128)(2,1)S(1)} %get-tuple-element.49), channel_id=1, source_target_pairs={{0,1},{1,0},{2,3},{3,2},{4,5},{5,4},{6,7},{7,6},{8,9},{9,8},{10,11... | collective-permute-start | bytes 196616 | tf_op jit(solution)/shard_map/ppermute | solution.py:389
  69.4 10.8 %collective-permute-start.13 = (bf16[1,256,128]{2,1,0:T(8,128)(2,1)S(1)}, bf16[1,256,128]{2,1,0:T(8,128)(2,1)S(1)}, u32[]{:S(2)}, u32[]{:S(2)}) collective-permute-start(bf16[1,256,128]{2,1,0:T(8,128)(2,1)S(1)} %get-tuple-element.50), channel_id=1, source_target_pairs={{0,2},{1,3},{2,0},{3,1},{4,6},{5,7},{6,4},{7,5},{8,10},{9,11},{10,... | collective-permute-start | bytes 196616 | tf_op jit(solution)/shard_map/ppermute | solution.py:389
  73.0 7.3 %collective-permute-start.14 = (bf16[1,256,128]{2,1,0:T(8,128)(2,1)S(1)}, bf16[1,256,128]{2,1,0:T(8,128)(2,1)S(1)}, u32[]{:S(2)}, u32[]{:S(2)}) collective-permute-start(bf16[1,256,128]{2,1,0:T(8,128)(2,1)S(1)} %get-tuple-element.51), channel_id=1, source_target_pairs={{0,3},{1,2},{2,1},{3,0},{4,7},{5,6},{6,5},{7,4},{8,11},{9,10},{10,... | collective-permute-start | bytes 196616 | tf_op jit(solution)/shard_map/ppermute | solution.py:389
  (4 other events, 3.9 us)
where the time goes:
time: 81.6 us; the launch traced here: 81 us
  Pallas kernels  35.6 us (44%)
  starting transfers between devices  31.5 us (39%)
  local copies, waits for them, and re-layouts  5.41 us (7%)
  waiting for transfers between devices  5.22 us (6%)
  other arithmetic  2.34 us (3%)
  between operations  0.92 us (1%)
    ppermute x15, starting transfers between devices, swap(): return lax.ppermute(x, axis, [(d, d ^ bits) for d in range(size)])  19.6 us
    pallas_call x2, Pallas kernels, partial_proj(): pl.pallas_call(functools.partial(partial_kernel, len(operands), len(other...  8.75 us
    pallas_call x1, Pallas kernels, permute(): pl.pallas_call(functools.partial(permute_kernel, slots, pieces), out_shap...  6.4 us
    all_to_all x1, starting transfers between devices, local(): g3_got = lax.all_to_all(g3, AXES, split_axis=0, concat_axis=0, tiled=True)  6.07 us
    all_to_all x1, starting transfers between devices, local(): lax.all_to_all(narrow, AXES, split_axis=0, concat_axis=0, tiled=True)  5.84 us
    pallas_call x1, Pallas kernels, wide_sum(): pl.pallas_call(wide_kernel, out_shape=jax.ShapeDtypeStruct((ROWS, WSUM),...  5.48 us
    pallas_call x1, Pallas kernels, narrow_sum(): pl.pallas_call(narrow_sum_kernel, out_shape=jax.ShapeDtypeStruct((ROWS, W...  5.39 us
    ppermute x15, waiting for transfers between devices, swap(): return lax.ppermute(x, axis, [(d, d ^ bits) for d in range(size)])  5.21 us
  transfers between devices with their start and end apart: 17, of which 2 were waited for; matrix products, arithmetic and copies ran while one was open for 3% of the time, Pallas kernels for 44%

commit v1 on v0

--- a/solution.py
+++ b/solution.py
@@ -21,8 +21,8 @@
 MIB = 1024 * 1024
 
 
-def params(grid):
-    return pltpu.CompilerParams(dimension_semantics=("arbitrary",) * grid, vmem_limit_bytes=58 * MIB)
+def params(grid, mib=58):
+    return pltpu.CompilerParams(dimension_semantics=("arbitrary",) * grid, vmem_limit_bytes=mib * MIB)
 
 
 HBM = pl.BlockSpec(memory_space=pltpu.HBM)
@@ -107,7 +107,7 @@
     return copies
 
 
-def narrow_kernel(blocks, place_ref, g_ref, w_ref, *refs):
+def narrow_kernel(base, blocks, index_ref, g_ref, w_ref, *refs):
     out_ref, g_held, w_held, out_held, g_sems, w_sems, out_sems = refs[-7:]
     weights = fetch(w_ref, w_held, w_sems, 1)
     loads = fetch(g_ref, g_held, g_sems, blocks)
@@ -120,7 +120,7 @@
     for i, load in enumerate(loads):
         load.wait()
         for s in range(i * step, (i + 1) * step):
-            w = w_held[place_ref[s]]
+            w = w_held[index_ref[base + s]]
             first = lax.dot_general(g_held[s, :, :PD], w, dims, preferred_element_type=jnp.float32)
             second = lax.dot_general(g_held[s, :, PD:], w, dims, preferred_element_type=jnp.float32)
             d = jnp.where(column < W1, first, second)
@@ -132,12 +132,12 @@
         store.wait()
 
 
-def narrow_dpool(place, g12, w12, after=()):
+def narrow_dpool(index, first, g12, w12, after=()):
     slots, count, _ = g12.shape
     blocks = 4
     shape = (slots, count // 2, 2 * W12)
     return pl.pallas_call(
-        functools.partial(narrow_kernel, blocks),
+        functools.partial(narrow_kernel, first, blocks),
         out_shape=jax.ShapeDtypeStruct(shape, jnp.bfloat16),
         grid_spec=pltpu.PrefetchScalarGridSpec(
             num_scalar_prefetch=1,
@@ -156,11 +156,10 @@
         compiler_params=params(1),
         cost_estimate=cost(4e9),
         name="narrow_dpool",
-    )(place, g12, w12, *after)
-
-
-def partial_kernel(ins, added, results, node_ref, line_ref, *refs):
-    blocks, size = node_ref.shape[0], line_ref.shape[0]
+    )(index, g12, w12, *after)
+
+
+def partial_kernel(first, blocks, size, ins, added, results, index_ref, *refs):
     operands, others = refs[:ins], refs[ins : ins + added]
     outs, scratch = refs[-3 - 2 * results - ins - added :][:results], refs[-3 - results - ins - added :]
     held, other_held, out_held = scratch[:ins], scratch[ins : ins + added], scratch[ins + added : -3]
@@ -171,7 +170,7 @@
         return arrays[i // per].at[pl.ds(i % per * size, size)]
 
     loads = [
-        fetch(ref, at, in_sems.at[n], blocks, lambda i: node_ref[i])
+        fetch(ref, at, in_sems.at[n], blocks, lambda i: index_ref[first + i])
         for n, (ref, at) in enumerate(zip(operands, held))
     ]
     if added:
@@ -189,7 +188,7 @@
             copies[i].wait()
         out = block(out_held, i)
         for l in range(size):
-            slot = i * size + line_ref[l]
+            slot = i * size + index_ref[l]
             q = held[0][slot].T
             narrow = jnp.dot(q[:W12], held[1][slot], preferred_element_type=jnp.float32)
             wide = jnp.dot(q[W12:], held[2][slot], preferred_element_type=jnp.float32)
@@ -204,17 +203,16 @@
         store.wait()
 
 
-def partial_proj(nodes, lines, q, g12, g3, results, others=()):
+def partial_proj(index, first, blocks, size, q, g12, g3, results, others=()):
     _, count, _ = q.shape
-    blocks, size = nodes.shape[0], lines.shape[0]
     kinds = [jnp.bfloat16 if others and i else jnp.float32 for i in range(results)]
     shapes = [jax.ShapeDtypeStruct((blocks // results * size, WSUM, PD), kind) for kind in kinds]
     operands = (q, g12, g3)
     return pl.pallas_call(
-        functools.partial(partial_kernel, len(operands), len(others), results),
+        functools.partial(partial_kernel, first, blocks, size, len(operands), len(others), results),
         out_shape=shapes,
         grid_spec=pltpu.PrefetchScalarGridSpec(
-            num_scalar_prefetch=2,
+            num_scalar_prefetch=1,
             grid=(1,),
             in_specs=[HBM] * len(operands) + [ANY] * len(others),
             out_specs=[HBM] * results,
@@ -227,10 +225,10 @@
                 pltpu.SemaphoreType.DMA((blocks,)),
             ],
         ),
-        compiler_params=params(1),
+        compiler_params=params(1, 57),
         cost_estimate=cost(4e9 if others else 1e7),
         name="partial_proj",
-    )(nodes, lines, *operands, *others)
+    )(index, *operands, *others)
 
 
 def count_kernel(index_ref, length_ref, *refs):
@@ -396,26 +394,35 @@
     n_plane = n_node // 2
     node, loc = lax.axis_index("node"), lax.axis_index("local")
 
+    entry = jnp.arange(n_local + 2 * n_plane + slots, dtype=jnp.int32)
+    plane = entry - n_local
+    slot = plane - 2 * n_plane
+    other = slot // n_local ^ node
+    index = jnp.where(
+        plane < 0,
+        entry ^ loc,
+        jnp.where(
+            slot < 0,
+            ((plane % n_plane) ^ (node // 2)) * 2 + (node + 1 + plane // n_plane) % 2,
+            other % 2 * (slots // 2) + other // 2 * n_local + (slot % n_local ^ loc),
+        ),
+    ).astype(jnp.int32)
+
     rows = proj[:, :W12]
     rows = jnp.concatenate([rows] + [swap(rows, "local", n_local, d) for d in range(1, n_local)])
     g12, g3, q = permute(assign, grad_out, pooled)
     rows, g3 = lax.optimization_barrier((rows, g3))
     g3_got = lax.all_to_all(g3, AXES, split_axis=0, concat_axis=0, tiled=True)
 
-    plane = jnp.arange(n_plane, dtype=jnp.int32) ^ (node // 2)
-    lines = jnp.arange(n_local, dtype=jnp.int32) ^ loc
-    sent = partial_proj(plane * 2 + 1 - node % 2, lines, q, g12, g3, 2)
+    sent = partial_proj(index, n_local, n_plane, n_local, q, g12, g3, 2)
     got = [swap(x, "node", n_node, 1) for x in sent]
 
     rows, sent = lax.optimization_barrier((rows, sent))
     rows = jnp.concatenate([rows] + [swap(rows, "node", n_node, 2 * d) for d in range(1, n_plane)])
     hits = count_hits(indices[0].transpose(1, 2, 0), lengths[0].T[:, None, :], after=sent[:1])
-    kept = partial_proj(plane * 2 + node % 2, lines, q, g12, g3, n_plane, got)
+    kept = partial_proj(index, n_local + n_plane, n_plane, n_local, q, g12, g3, n_plane, got)
     rows = jnp.concatenate([rows, swap(rows, "node", n_node, 1)])
-    slot = jnp.arange(slots, dtype=jnp.int32)
-    slot_node = slot // n_local ^ node
-    slot_place = slot_node % 2 * (slots // 2) + slot_node // 2 * n_local + (slot % n_local ^ loc)
-    narrow = narrow_dpool(slot_place, g12, rows, after=kept[:1])
+    narrow = narrow_dpool(index, n_local + 2 * n_plane, g12, rows, after=kept[:1])
 
     narrow, hits, g3_got, kept = lax.optimization_barrier((narrow, hits, g3_got, kept))
     narrow_got = lax.all_to_all(narrow, AXES, split_axis=0, concat_axis=0, tiled=True)

time: 81.6 us -> 80.5 us (0.987)
  other arithmetic: 2.34 us -> 1.27 us
    add x2 -> x0, other arithmetic: 1.02 us -> none  [the longest x1 0.53 us: local(): slot_node % 2 * (slots // 2) + slot_node // 2 * n_local]
  transfers between devices with their start and end apart: 17 -> 17, of which waited for: 2 -> 3; matrix products, arithmetic and copies ran while one was open for 3% -> 2% of each run, Pallas kernels for 44% -> 44%
where the time goes in v1:
time: 80.5 us; the launch traced here: 79.9 us
  Pallas kernels  35.5 us (44%)
  starting transfers between devices  31.4 us (39%)
  local copies, waits for them, and re-layouts  5.43 us (7%)
  waiting for transfers between devices  5.38 us (7%)
  other arithmetic  1.27 us (2%)
  between operations  0.93 us (1%)
    ppermute x15, starting transfers between devices, swap(): return lax.ppermute(x, axis, [(d, d ^ bits) for d in range(size)])  19.6 us
    pallas_call x2, Pallas kernels, partial_proj(): pl.pallas_call(functools.partial(partial_kernel, first, blocks, size, len...  8.73 us
    pallas_call x1, Pallas kernels, permute(): pl.pallas_call(functools.partial(permute_kernel, slots, pieces), out_shap...  6.37 us
    all_to_all x1, starting transfers between devices, local(): g3_got = lax.all_to_all(g3, AXES, split_axis=0, concat_axis=0, tiled=True)  6.07 us
    all_to_all x1, starting transfers between devices, local(): lax.all_to_all(narrow, AXES, split_axis=0, concat_axis=0, tiled=True)  5.7 us
    pallas_call x1, Pallas kernels, wide_sum(): pl.pallas_call(wide_kernel, out_shape=jax.ShapeDtypeStruct((ROWS, WSUM),...  5.48 us
    pallas_call x1, Pallas kernels, narrow_sum(): pl.pallas_call(narrow_sum_kernel, out_shape=jax.ShapeDtypeStruct((ROWS, W...  5.39 us
    ppermute x15, waiting for transfers between devices, swap(): return lax.ppermute(x, axis, [(d, d ^ bits) for d in range(size)])  5.37 us
  transfers between devices with their start and end apart: 17, of which 3 were waited for; matrix products, arithmetic and copies ran while one was open for 2% of the time, Pallas kernels for 44%

profile of v1, /device:TPU:0, one launch (start us, length us, event | category | flops | bytes accessed | tf_op | source)
XLA Modules:
  0.0 79.9 jit_solution(5352199560250462031)
XLA Ops:
  0.6 0.7 slice.3
  1.4 5.0 %collective-permute-start.2 = (bf16[1,64,128]{2,1,0:T(8,128)(2,1)S(1)}, bf16[1,64,128]{2,1,0:T(8,128)(2,1)S(1)}, u32[]{:S(2)}, u32[]{:S(2)}) collective-permute-start(bf16[1,64,128]{2,1,0:T(8,128)(2,1)S(1)} %slice.3), channel_id=1, source_target_pairs={{0,3},{1,2},{2,1},{3,0},{4,7},{5,6},{6,5},{7,4},{8,11},{9,10},{10,... | collective-permute-start | bytes 49160 | tf_op jit(solution)/shard_map/ppermute | solution.py:387
  7.0 6.4 %permute_groups.1 = (bf16[32,128,256]{2,1,0:T(8,128)(2,1)}, bf16[32,128,128]{2,1,0:T(8,128)(2,1)}, bf16[32,128,256]{2,1,0:T(8,128)(2,1)}) custom-call(s32[32]{0:T(128)} %assign_ref.1, bf16[128,32,384]{2,1,0:T(8,128)(2,1)} %grad_ref.1, bf16[128,32,256]{2,1,0:T(8,128)(2,1)} %pool_ref.1), custom_call_target="tpu_custom_call" | custom-call | flops 10000000 | bytes 1024 | tf_op jit(solution)/shard_map/permute_groups/pallas_call | solution.py:78
  13.4 6.1 %all-to-all-start = ((bf16[32,128,128]{2,1,0:T(8,128)(2,1)}), bf16[32,128,128]{2,1,0:T(8,128)(2,1)S(1)}, u32[]{:S(2)}, u32[]{:S(2)}) async-start(bf16[32,128,128]{2,1,0:T(8,128)(2,1)} %get-tuple-element.34.refs_2_), calls=%async_computation | async-start | bytes 2097152 | tf_op jit(solution)/shard_map/all_to_all | solution.py:415
  20.7 4.3 %partial_proj.2 = (f32[8,256,128]{2,1,0:T(8,128)}, f32[8,256,128]{2,1,0:T(8,128)}) custom-call(s32[44]{0:T(128)} %fusion.9.index_ref, bf16[32,128,256]{2,1,0:T(8,128)(2,1)} %get-tuple-element.33.refs_0_, bf16[32,128,256]{2,1,0:T(8,128)(2,1)} %get-tuple-element.30.refs_1_.g_ref, bf16[32,128,128]{2,1,0:T(8,128)(2,1)} %get-tuple-element.34.refs_2_), custom_call_target="tpu_custom_call" | custom-call | flops 10000000 | bytes 1024 | tf_op jit(solution)/shard_map/partial_proj/pallas_call | solution.py:211
  25.1 1.8 %collective-permute-start.3 = (bf16[4,64,128]{2,1,0:T(8,128)(2,1)S(1)}, bf16[4,64,128]{2,1,0:T(8,128)(2,1)S(1)}, u32[]{:S(2)}, u32[]{:S(2)}) collective-permute-start(bf16[4,64,128]{2,1,0:T(8,128)(2,1)S(1)} %pad_maximum_fusion.1), channel_id=1, source_target_pairs={{0,8},{4,12},{8,0},{12,4},{16,24},{20,28},{24,16},{28,20},{1,9},{5... | collective-permute-start | bytes 196616 | tf_op jit(solution)/shard_map/ppermute | solution.py:387
  26.9 1.5 %collective-permute-start.4 = (bf16[4,64,128]{2,1,0:T(8,128)(2,1)S(1)}, bf16[4,64,128]{2,1,0:T(8,128)(2,1)S(1)}, u32[]{:S(2)}, u32[]{:S(2)}) collective-permute-start(bf16[4,64,128]{2,1,0:T(8,128)(2,1)S(1)} %pad_maximum_fusion.1), channel_id=1, source_target_pairs={{0,16},{4,20},{8,24},{12,28},{16,0},{20,4},{24,8},{28,12},{1,17},{... | collective-permute-start | bytes 196616 | tf_op jit(solution)/shard_map/ppermute | solution.py:387
  29.1 4.9 %count_hits.1.hits_ref = s32[3,64,4096]{2,1,0:T(8,128)} custom-call(s32[3,8,4096]{2,1,0:T(8,128)} %bitcast.15, s32[3,1,4096]{2,1,0:T(1,128)} %broadcast_in_dim.6.length_ref, f32[8,256,128]{2,1,0:T(8,128)} %get-tuple-element.39.refs_0_), custom_call_target="tpu_custom_call" | custom-call | flops 5000000000 | bytes 1024 | tf_op jit(solution)/shard_map/count_hits/pallas_call | solution.py:259
  34.4 1.5 %collective-permute-done.6 = bf16[16,64,128]{2,1,0:T(8,128)(2,1)S(1)} collective-permute-done((bf16[16,64,128]{2,1,0:T(8,128)(2,1)S(1)}, bf16[16,64,128]{2,1,0:T(8,128)(2,1)S(1)}, u32[]{:S(2)}, u32[]{:S(2)}) %collective-permute-start.6) | collective-permute-done | bytes 262176 | tf_op jit(solution)/shard_map/ppermute | solution.py:387
  36.0 1.0 %copy-done.6 = f32[8,256,128]{2,1,0:T(8,128)} copy-done((f32[8,256,128]{2,1,0:T(8,128)}, f32[8,256,128]{2,1,0:T(8,128)S(1)}, u32[]{:S(2)}) %copy-start.6) | copy-done | bytes 1048600
  37.0 1.0 %copy-done.7 = f32[8,256,128]{2,1,0:T(8,128)} copy-done((f32[8,256,128]{2,1,0:T(8,128)}, f32[8,256,128]{2,1,0:T(8,128)S(1)}, u32[]{:S(2)}) %copy-start.7) | copy-done | bytes 1048600
  38.0 4.4 %partial_proj.3 = (f32[4,256,128]{2,1,0:T(8,128)}, bf16[4,256,128]{2,1,0:T(8,128)(2,1)}, bf16[4,256,128]{2,1,0:T(8,128)(2,1)}, bf16[4,256,128]{2,1,0:T(8,128)(2,1)}) custom-call(s32[44]{0:T(128)} %fusion.9.index_ref, bf16[32,128,256]{2,1,0:T(8,128)(2,1)} %get-tuple-element.33.refs_0_, bf16[32,128,256]{2,1,0:T(8,128)(2,1)} %get-tuple-element.30.refs_1_.g_ref, ...), custom_call_target="tpu_custom_call" | custom-call | flops 4000000000 | bytes 1024 | tf_op jit(solution)/shard_map/partial_proj/pallas_call | solution.py:211
  42.5 4.5 %narrow_dpool.1 = bf16[32,64,128]{2,1,0:T(8,128)(2,1)} custom-call(s32[44]{0:T(128)} %fusion.9.index_ref, bf16[32,128,256]{2,1,0:T(8,128)(2,1)} %get-tuple-element.30.refs_1_.g_ref, bf16[32,64,128]{2,1,0:T(8,128)(2,1)} %copy-done.5, f32[4,256,128]{2,1,0:T(8,128)} %get-tuple-element.43.refs_0_.kept_ref), custom_call_target="tpu_custom_call" | custom-call | flops 4000000000 | bytes 1024 | tf_op jit(solution)/shard_map/narrow_dpool/pallas_call | solution.py:139
  47.0 1.7 %collective-permute-start.9 = (bf16[4,256,128]{2,1,0:T(8,128)(2,1)S(1)}, bf16[4,256,128]{2,1,0:T(8,128)(2,1)S(1)}, u32[]{:S(2)}, u32[]{:S(2)}) collective-permute-start(bf16[4,256,128]{2,1,0:T(8,128)(2,1)S(1)} %copy-done.10), channel_id=1, source_target_pairs={{0,8},{4,12},{8,0},{12,4},{16,24},{20,28},{24,16},{28,20},{1,9},{5... | collective-permute-start | bytes 786440 | tf_op jit(solution)/shard_map/ppermute | solution.py:387
  48.7 1.5 %collective-permute-start.10 = (bf16[4,256,128]{2,1,0:T(8,128)(2,1)S(1)}, bf16[4,256,128]{2,1,0:T(8,128)(2,1)S(1)}, u32[]{:S(2)}, u32[]{:S(2)}) collective-permute-start(bf16[4,256,128]{2,1,0:T(8,128)(2,1)S(1)} %copy-done.9), channel_id=1, source_target_pairs={{0,16},{4,20},{8,24},{12,28},{16,0},{20,4},{24,8},{28,12},{1,17},{... | collective-permute-start | bytes 786440 | tf_op jit(solution)/shard_map/ppermute | solution.py:387
  50.6 5.7 %all-to-all-start.1 = ((bf16[32,64,128]{2,1,0:T(8,128)(2,1)}), bf16[32,64,128]{2,1,0:T(8,128)(2,1)S(1)}, u32[]{:S(2)}, u32[]{:S(2)}) async-start(bf16[32,64,128]{2,1,0:T(8,128)(2,1)} %narrow_dpool.1), calls=%async_computation.1 | async-start | bytes 1048576 | tf_op jit(solution)/shard_map/all_to_all | solution.py:428
  56.3 5.5 %wide_sum.1.refs_3_.wide_ref = f32[512,256]{1,0:T(8,128)} custom-call(s32[3,64,4096]{2,1,0:T(8,128)} %count_hits.1.hits_ref, bf16[4096,128]{1,0:T(8,128)(2,1)} %bitcast.12, bf16[256,128]{1,0:T(8,128)(2,1)} %bitcast.14), custom_call_target="tpu_custom_call" | custom-call | flops 10000000 | bytes 1024 | tf_op jit(solution)/shard_map/wide_sum/pallas_call | solution.py:297
  61.8 3.7 %collective-permute-done.10.refs_1_ = bf16[4,256,128]{2,1,0:T(8,128)(2,1)S(1)} collective-permute-done((bf16[4,256,128]{2,1,0:T(8,128)(2,1)S(1)}, bf16[4,256,128]{2,1,0:T(8,128)(2,1)S(1)}, u32[]{:S(2)}, u32[]{:S(2)}) %collective-permute-start.10) | collective-permute-done | bytes 262176 | tf_op jit(solution)/shard_map/ppermute | solution.py:387
  65.5 1.0 %copy-done = f32[512,256]{1,0:T(8,128)S(1)} copy-done((f32[512,256]{1,0:T(8,128)S(1)}, f32[512,256]{1,0:T(8,128)}, u32[]{:S(2)}) %copy-start) | copy-done | bytes 524312
  66.7 1.7 %collective-permute-start.12 = (bf16[1,256,128]{2,1,0:T(8,128)(2,1)S(1)}, bf16[1,256,128]{2,1,0:T(8,128)(2,1)S(1)}, u32[]{:S(2)}, u32[]{:S(2)}) collective-permute-start(bf16[1,256,128]{2,1,0:T(8,128)(2,1)S(1)} %get-tuple-element.49), channel_id=1, source_target_pairs={{0,1},{1,0},{2,3},{3,2},{4,5},{5,4},{6,7},{7,6},{8,9},{9,8},{10,11... | collective-permute-start | bytes 196616 | tf_op jit(solution)/shard_map/ppermute | solution.py:387
  68.3 4.0 %collective-permute-start.13 = (bf16[1,256,128]{2,1,0:T(8,128)(2,1)S(1)}, bf16[1,256,128]{2,1,0:T(8,128)(2,1)S(1)}, u32[]{:S(2)}, u32[]{:S(2)}) collective-permute-start(bf16[1,256,128]{2,1,0:T(8,128)(2,1)S(1)} %get-tuple-element.50), channel_id=1, source_target_pairs={{0,2},{1,3},{2,0},{3,1},{4,6},{5,7},{6,4},{7,5},{8,10},{9,11},{10,... | collective-permute-start | bytes 196616 | tf_op jit(solution)/shard_map/ppermute | solution.py:387
  73.0 0.8 copy-done.3
  73.8 5.4 %narrow_sum.1 = f32[512,256]{1,0:T(8,128)} custom-call(s32[3,64,4096]{2,1,0:T(8,128)} %count_hits.1.hits_ref, bf16[32,64,128]{2,1,0:T(8,128)(2,1)} %copy-done.3, f32[512,256]{1,0:T(8,128)} %wide_sum.1.refs_3_.wide_ref), custom_call_target="tpu_custom_call", output_to_operand_aliasing={{}: (2, {})} | custom-call | flops 10000000 | bytes 1024 | tf_op jit(solution)/shard_map/narrow_sum/pallas_call | solution.py:341
  79.2 0.7 add_multiply_fusion
  (52 shorter events, 4.1 us)
Async XLA Ops:
  1.4 12.0 %collective-permute-start.2 = (bf16[1,64,128]{2,1,0:T(8,128)(2,1)S(1)}, bf16[1,64,128]{2,1,0:T(8,128)(2,1)S(1)}, u32[]{:S(2)}, u32[]{:S(2)}) collective-permute-start(bf16[1,64,128]{2,1,0:T(8,128)(2,1)S(1)} %slice.3), channel_id=1, source_target_pairs={{0,3},{1,2},{2,1},{3,0},{4,7},{5,6},{6,5},{7,4},{8,11},{9,10},{10,... | collective-permute-start | bytes 49160 | tf_op jit(solution)/shard_map/ppermute | solution.py:387
  6.4 7.0 %collective-permute-start.1 = (bf16[1,64,128]{2,1,0:T(8,128)(2,1)S(1)}, bf16[1,64,128]{2,1,0:T(8,128)(2,1)S(1)}, u32[]{:S(2)}, u32[]{:S(2)}) collective-permute-start(bf16[1,64,128]{2,1,0:T(8,128)(2,1)S(1)} %slice.3), channel_id=1, source_target_pairs={{0,2},{1,3},{2,0},{3,1},{4,6},{5,7},{6,4},{7,5},{8,10},{9,11},{10,... | collective-permute-start | bytes 49160 | tf_op jit(solution)/shard_map/ppermute | solution.py:387
  6.4 7.0 %collective-permute-start = (bf16[1,64,128]{2,1,0:T(8,128)(2,1)S(1)}, bf16[1,64,128]{2,1,0:T(8,128)(2,1)S(1)}, u32[]{:S(2)}, u32[]{:S(2)}) collective-permute-start(bf16[1,64,128]{2,1,0:T(8,128)(2,1)S(1)} %slice.3), channel_id=1, source_target_pairs={{0,1},{1,0},{2,3},{3,2},{4,5},{5,4},{6,7},{7,6},{8,9},{9,8},{10,11... | collective-permute-start | bytes 49160 | tf_op jit(solution)/shard_map/ppermute | solution.py:387
  13.3 6.2 %copy-start.4 = (s32[1,4096,3]{1,0,2:T(1,128)S(1)}, s32[1,4096,3]{1,0,2:T(1,128)}, u32[]{:S(2)}) copy-start(s32[1,4096,3]{1,0,2:T(1,128)} %param.11) | copy-start | bytes 147460
  13.4 33.6 %all-to-all-start = ((bf16[32,128,128]{2,1,0:T(8,128)(2,1)}), bf16[32,128,128]{2,1,0:T(8,128)(2,1)S(1)}, u32[]{:S(2)}, u32[]{:S(2)}) async-start(bf16[32,128,128]{2,1,0:T(8,128)(2,1)} %get-tuple-element.34.refs_2_), calls=%async_computation | async-start | bytes 2097152 | tf_op jit(solution)/shard_map/all_to_all | solution.py:415
  25.1 9.0 %collective-permute-start.3 = (bf16[4,64,128]{2,1,0:T(8,128)(2,1)S(1)}, bf16[4,64,128]{2,1,0:T(8,128)(2,1)S(1)}, u32[]{:S(2)}, u32[]{:S(2)}) collective-permute-start(bf16[4,64,128]{2,1,0:T(8,128)(2,1)S(1)} %pad_maximum_fusion.1), channel_id=1, source_target_pairs={{0,8},{4,12},{8,0},{12,4},{16,24},{20,28},{24,16},{28,20},{1,9},{5... | collective-permute-start | bytes 196616 | tf_op jit(solution)/shard_map/ppermute | solution.py:387
  26.9 7.2 %collective-permute-start.4 = (bf16[4,64,128]{2,1,0:T(8,128)(2,1)S(1)}, bf16[4,64,128]{2,1,0:T(8,128)(2,1)S(1)}, u32[]{:S(2)}, u32[]{:S(2)}) collective-permute-start(bf16[4,64,128]{2,1,0:T(8,128)(2,1)S(1)} %pad_maximum_fusion.1), channel_id=1, source_target_pairs={{0,16},{4,20},{8,24},{12,28},{16,0},{20,4},{24,8},{28,12},{1,17},{... | collective-permute-start | bytes 196616 | tf_op jit(solution)/shard_map/ppermute | solution.py:387
  28.4 5.9 %collective-permute-start.5 = (bf16[4,64,128]{2,1,0:T(8,128)(2,1)S(1)}, bf16[4,64,128]{2,1,0:T(8,128)(2,1)S(1)}, u32[]{:S(2)}, u32[]{:S(2)}) collective-permute-start(bf16[4,64,128]{2,1,0:T(8,128)(2,1)S(1)} %pad_maximum_fusion.1), channel_id=1, source_target_pairs={{0,24},{4,28},{8,16},{12,20},{16,8},{20,12},{24,0},{28,4},{1,25},{... | collective-permute-start | bytes 196616 | tf_op jit(solution)/shard_map/ppermute | solution.py:387
  28.6 7.3 %collective-permute-start.7 = (f32[8,256,128]{2,1,0:T(8,128)}, f32[8,256,128]{2,1,0:T(8,128)S(1)}, u32[]{:S(2)}, u32[]{:S(2)}) collective-permute-start(f32[8,256,128]{2,1,0:T(8,128)} %get-tuple-element.39.refs_0_), channel_id=1, source_target_pairs={{0,4},{4,0},{8,12},{12,8},{16,20},{20,16},{24,28},{28,24},{1,5},{5... | collective-permute-start | bytes 3145736 | tf_op jit(solution)/shard_map/ppermute | solution.py:387
  28.6 7.3 %collective-permute-start.8 = (f32[8,256,128]{2,1,0:T(8,128)}, f32[8,256,128]{2,1,0:T(8,128)S(1)}, u32[]{:S(2)}, u32[]{:S(2)}) collective-permute-start(f32[8,256,128]{2,1,0:T(8,128)} %get-tuple-element.36), channel_id=1, source_target_pairs={{0,4},{4,0},{8,12},{12,8},{16,20},{20,16},{24,28},{28,24},{1,5},{5... | collective-permute-start | bytes 3145736 | tf_op jit(solution)/shard_map/ppermute | solution.py:387
  34.3 1.6 %collective-permute-start.6 = (bf16[16,64,128]{2,1,0:T(8,128)(2,1)S(1)}, bf16[16,64,128]{2,1,0:T(8,128)(2,1)S(1)}, u32[]{:S(2)}, u32[]{:S(2)}) collective-permute-start(bf16[16,64,128]{2,1,0:T(8,128)(2,1)S(1)} %pad_maximum_fusion), channel_id=1, source_target_pairs={{0,4},{4,0},{8,12},{12,8},{16,20},{20,16},{24,28},{28,24},{1,5},{5... | collective-permute-start | bytes 786440 | tf_op jit(solution)/shard_map/ppermute | solution.py:387
  35.9 6.5 %copy-start.5 = (bf16[32,64,128]{2,1,0:T(8,128)(2,1)}, bf16[32,64,128]{2,1,0:T(8,128)(2,1)S(1)}, u32[]{:S(2)}) copy-start(bf16[32,64,128]{2,1,0:T(8,128)(2,1)S(1)} %constant_dynamic-update-slice_fusion.w_ref) | copy-start | bytes 1572868
  42.5 4.5 %copy-start.10 = (bf16[4,256,128]{2,1,0:T(8,128)(2,1)S(1)}, bf16[4,256,128]{2,1,0:T(8,128)(2,1)}, u32[]{:S(2)}) copy-start(bf16[4,256,128]{2,1,0:T(8,128)(2,1)} %get-tuple-element.44) | copy-start | bytes 786436
  42.5 6.2 %copy-start.9 = (bf16[4,256,128]{2,1,0:T(8,128)(2,1)S(1)}, bf16[4,256,128]{2,1,0:T(8,128)(2,1)}, u32[]{:S(2)}) copy-start(bf16[4,256,128]{2,1,0:T(8,128)(2,1)} %get-tuple-element.45) | copy-start | bytes 786436
  42.5 7.7 %copy-start.8 = (bf16[4,256,128]{2,1,0:T(8,128)(2,1)S(1)}, bf16[4,256,128]{2,1,0:T(8,128)(2,1)}, u32[]{:S(2)}) copy-start(bf16[4,256,128]{2,1,0:T(8,128)(2,1)} %get-tuple-element.46) | copy-start | bytes 786436
  47.0 9.3 %copy-start.2 = (bf16[32,128,128]{2,1,0:T(8,128)(2,1)}, bf16[32,128,128]{2,1,0:T(8,128)(2,1)S(1)}, u32[]{:S(2)}) copy-start(bf16[32,128,128]{2,1,0:T(8,128)(2,1)S(1)} %all-to-all-done) | copy-start | bytes 3145732
  47.0 14.8 %collective-permute-start.9 = (bf16[4,256,128]{2,1,0:T(8,128)(2,1)S(1)}, bf16[4,256,128]{2,1,0:T(8,128)(2,1)S(1)}, u32[]{:S(2)}, u32[]{:S(2)}) collective-permute-start(bf16[4,256,128]{2,1,0:T(8,128)(2,1)S(1)} %copy-done.10), channel_id=1, source_target_pairs={{0,8},{4,12},{8,0},{12,4},{16,24},{20,28},{24,16},{28,20},{1,9},{5... | collective-permute-start | bytes 786440 | tf_op jit(solution)/shard_map/ppermute | solution.py:387
  48.7 16.8 %collective-permute-start.10 = (bf16[4,256,128]{2,1,0:T(8,128)(2,1)S(1)}, bf16[4,256,128]{2,1,0:T(8,128)(2,1)S(1)}, u32[]{:S(2)}, u32[]{:S(2)}) collective-permute-start(bf16[4,256,128]{2,1,0:T(8,128)(2,1)S(1)} %copy-done.9), channel_id=1, source_target_pairs={{0,16},{4,20},{8,24},{12,28},{16,0},{20,4},{24,8},{28,12},{1,17},{... | collective-permute-start | bytes 786440 | tf_op jit(solution)/shard_map/ppermute | solution.py:387
  50.2 15.3 %collective-permute-start.11 = (bf16[4,256,128]{2,1,0:T(8,128)(2,1)S(1)}, bf16[4,256,128]{2,1,0:T(8,128)(2,1)S(1)}, u32[]{:S(2)}, u32[]{:S(2)}) collective-permute-start(bf16[4,256,128]{2,1,0:T(8,128)(2,1)S(1)} %copy-done.8), channel_id=1, source_target_pairs={{0,24},{4,28},{8,16},{12,20},{16,8},{20,12},{24,0},{28,4},{1,25},{... | collective-permute-start | bytes 786440 | tf_op jit(solution)/shard_map/ppermute | solution.py:387
  50.6 22.4 %all-to-all-start.1 = ((bf16[32,64,128]{2,1,0:T(8,128)(2,1)}), bf16[32,64,128]{2,1,0:T(8,128)(2,1)S(1)}, u32[]{:S(2)}, u32[]{:S(2)}) async-start(bf16[32,64,128]{2,1,0:T(8,128)(2,1)} %narrow_dpool.1), calls=%async_computation.1 | async-start | bytes 1048576 | tf_op jit(solution)/shard_map/all_to_all | solution.py:428
  56.3 9.2 %copy-start.1 = (f32[4,256,128]{2,1,0:T(8,128)S(1)}, f32[4,256,128]{2,1,0:T(8,128)}, u32[]{:S(2)}) copy-start(f32[4,256,128]{2,1,0:T(8,128)} %get-tuple-element.43.refs_0_.kept_ref) | copy-start | bytes 1572868
  66.7 12.5 %collective-permute-start.12 = (bf16[1,256,128]{2,1,0:T(8,128)(2,1)S(1)}, bf16[1,256,128]{2,1,0:T(8,128)(2,1)S(1)}, u32[]{:S(2)}, u32[]{:S(2)}) collective-permute-start(bf16[1,256,128]{2,1,0:T(8,128)(2,1)S(1)} %get-tuple-element.49), channel_id=1, source_target_pairs={{0,1},{1,0},{2,3},{3,2},{4,5},{5,4},{6,7},{7,6},{8,9},{9,8},{10,11... | collective-permute-start | bytes 196616 | tf_op jit(solution)/shard_map/ppermute | solution.py:387
  68.3 10.8 %collective-permute-start.13 = (bf16[1,256,128]{2,1,0:T(8,128)(2,1)S(1)}, bf16[1,256,128]{2,1,0:T(8,128)(2,1)S(1)}, u32[]{:S(2)}, u32[]{:S(2)}) collective-permute-start(bf16[1,256,128]{2,1,0:T(8,128)(2,1)S(1)} %get-tuple-element.50), channel_id=1, source_target_pairs={{0,2},{1,3},{2,0},{3,1},{4,6},{5,7},{6,4},{7,5},{8,10},{9,11},{10,... | collective-permute-start | bytes 196616 | tf_op jit(solution)/shard_map/ppermute | solution.py:387
  72.4 6.8 %collective-permute-start.14 = (bf16[1,256,128]{2,1,0:T(8,128)(2,1)S(1)}, bf16[1,256,128]{2,1,0:T(8,128)(2,1)S(1)}, u32[]{:S(2)}, u32[]{:S(2)}) collective-permute-start(bf16[1,256,128]{2,1,0:T(8,128)(2,1)S(1)} %get-tuple-element.51), channel_id=1, source_target_pairs={{0,3},{1,2},{2,1},{3,0},{4,7},{5,6},{6,5},{7,4},{8,11},{9,10},{10,... | collective-permute-start | bytes 196616 | tf_op jit(solution)/shard_map/ppermute | solution.py:387
  (4 other events, 3.9 us)

commit v2 on v1

--- a/solution.py
+++ b/solution.py
@@ -225,7 +225,7 @@
                 pltpu.SemaphoreType.DMA((blocks,)),
             ],
         ),
-        compiler_params=params(1, 57),
+        compiler_params=params(1),
         cost_estimate=cost(4e9 if others else 1e7),
         name="partial_proj",
     )(index, *operands, *others)
@@ -266,7 +266,7 @@
         ]
         + [ANY] * len(after),
         out_specs=pl.BlockSpec((1, ROWS // 8, block), lambda k, i: (k, 0, i)),
-        compiler_params=params(2),
+        compiler_params=params(2, 60),
         cost_estimate=cost(5e9),
         name="count_hits",
     )(lookups, counts, *after)
@@ -305,7 +305,7 @@
         ]
         + [ANY] * len(after),
         out_specs=pl.BlockSpec((ROWS, WSUM), lambda i: (0, 0)),
-        compiler_params=params(1),
+        compiler_params=params(1, 52),
         cost_estimate=cost(1e7),
         name="wide_sum",
     )(hits, g3, weights, *after)
@@ -419,7 +419,7 @@
 
     rows, sent = lax.optimization_barrier((rows, sent))
     rows = jnp.concatenate([rows] + [swap(rows, "node", n_node, 2 * d) for d in range(1, n_plane)])
-    hits = count_hits(indices[0].transpose(1, 2, 0), lengths[0].T[:, None, :], after=sent[:1])
+    hits = count_hits(indices[0].transpose(1, 2, 0), lengths.transpose(2, 0, 1), after=sent[:1])
     kept = partial_proj(index, n_local + n_plane, n_plane, n_local, q, g12, g3, n_plane, got)
     rows = jnp.concatenate([rows, swap(rows, "node", n_node, 1)])
     narrow = narrow_dpool(index, n_local + 2 * n_plane, g12, rows, after=kept[:1])

time: 80.5 us -> 79.8 us (level)
    unnamed x27 -> x24, local copies, waits for them, and re-layouts: 4.02 us -> 3.97 us
  transfers between devices with their start and end apart: 17 -> 17, of which waited for: 3 -> 3; matrix products, arithmetic and copies ran while one was open for 2% -> 1% of each run, Pallas kernels for 44% -> 45%
where the time goes in v2:
time: 79.8 us; the launch traced here: 79.1 us
  Pallas kernels  35.5 us (44%)
  starting transfers between devices  30.7 us (38%)
  waiting for transfers between devices  6.06 us (8%)
  local copies, waits for them, and re-layouts  4.73 us (6%)
  other arithmetic  1.27 us (2%)
  between operations  0.9 us (1%)
    ppermute x15, starting transfers between devices, swap(): return lax.ppermute(x, axis, [(d, d ^ bits) for d in range(size)])  19.4 us
    pallas_call x2, Pallas kernels, partial_proj(): pl.pallas_call(functools.partial(partial_kernel, first, blocks, size, len...  8.74 us
    pallas_call x1, Pallas kernels, permute(): pl.pallas_call(functools.partial(permute_kernel, slots, pieces), out_shap...  6.5 us
    all_to_all x1, starting transfers between devices, local(): g3_got = lax.all_to_all(g3, AXES, split_axis=0, concat_axis=0, tiled=True)  6.07 us
    ppermute x15, waiting for transfers between devices, swap(): return lax.ppermute(x, axis, [(d, d ^ bits) for d in range(size)])  6.06 us
    pallas_call x1, Pallas kernels, narrow_sum(): pl.pallas_call(narrow_sum_kernel, out_shape=jax.ShapeDtypeStruct((ROWS, W...  5.39 us
    pallas_call x1, Pallas kernels, wide_sum(): pl.pallas_call(wide_kernel, out_shape=jax.ShapeDtypeStruct((ROWS, WSUM),...  5.28 us
    all_to_all x1, starting transfers between devices, local(): lax.all_to_all(narrow, AXES, split_axis=0, concat_axis=0, tiled=True)  5.22 us
  transfers between devices with their start and end apart: 17, of which 3 were waited for; matrix products, arithmetic and copies ran while one was open for 1% of the time, Pallas kernels for 45%

profile of v2, /device:TPU:0, one launch (start us, length us, event | category | flops | bytes accessed | tf_op | source)
XLA Modules:
  0.0 79.1 jit_solution(10230489367245660137)
XLA Ops:
  0.6 0.7 slice.3
  1.4 5.0 %collective-permute-start.2 = (bf16[1,64,128]{2,1,0:T(8,128)(2,1)S(1)}, bf16[1,64,128]{2,1,0:T(8,128)(2,1)S(1)}, u32[]{:S(2)}, u32[]{:S(2)}) collective-permute-start(bf16[1,64,128]{2,1,0:T(8,128)(2,1)S(1)} %slice.3), channel_id=1, source_target_pairs={{0,3},{1,2},{2,1},{3,0},{4,7},{5,6},{6,5},{7,4},{8,11},{9,10},{10,... | collective-permute-start | bytes 49160 | tf_op jit(solution)/shard_map/ppermute | solution.py:387
  7.0 6.5 %permute_groups.1 = (bf16[32,128,256]{2,1,0:T(8,128)(2,1)}, bf16[32,128,128]{2,1,0:T(8,128)(2,1)}, bf16[32,128,256]{2,1,0:T(8,128)(2,1)}) custom-call(s32[32]{0:T(128)} %assign_ref.1, bf16[128,32,384]{2,1,0:T(8,128)(2,1)} %grad_ref.1, bf16[128,32,256]{2,1,0:T(8,128)(2,1)} %pool_ref.1), custom_call_target="tpu_custom_call" | custom-call | flops 10000000 | bytes 1024 | tf_op jit(solution)/shard_map/permute_groups/pallas_call | solution.py:78
  13.5 6.1 %all-to-all-start = ((bf16[32,128,128]{2,1,0:T(8,128)(2,1)}), bf16[32,128,128]{2,1,0:T(8,128)(2,1)S(1)}, u32[]{:S(2)}, u32[]{:S(2)}) async-start(bf16[32,128,128]{2,1,0:T(8,128)(2,1)} %get-tuple-element.34.refs_2_), calls=%async_computation | async-start | bytes 2097152 | tf_op jit(solution)/shard_map/all_to_all | solution.py:415
  20.2 4.3 %partial_proj.2 = (f32[8,256,128]{2,1,0:T(8,128)}, f32[8,256,128]{2,1,0:T(8,128)}) custom-call(s32[44]{0:T(128)} %fusion.9.index_ref, bf16[32,128,256]{2,1,0:T(8,128)(2,1)} %get-tuple-element.33.refs_0_, bf16[32,128,256]{2,1,0:T(8,128)(2,1)} %get-tuple-element.30.refs_1_.g_ref, bf16[32,128,128]{2,1,0:T(8,128)(2,1)} %get-tuple-element.34.refs_2_), custom_call_target="tpu_custom_call" | custom-call | flops 10000000 | bytes 1024 | tf_op jit(solution)/shard_map/partial_proj/pallas_call | solution.py:211
  24.5 1.8 %collective-permute-start.3 = (bf16[4,64,128]{2,1,0:T(8,128)(2,1)S(1)}, bf16[4,64,128]{2,1,0:T(8,128)(2,1)S(1)}, u32[]{:S(2)}, u32[]{:S(2)}) collective-permute-start(bf16[4,64,128]{2,1,0:T(8,128)(2,1)S(1)} %pad_maximum_fusion.1), channel_id=1, source_target_pairs={{0,8},{4,12},{8,0},{12,4},{16,24},{20,28},{24,16},{28,20},{1,9},{5... | collective-permute-start | bytes 196616 | tf_op jit(solution)/shard_map/ppermute | solution.py:387
  26.3 1.5 %collective-permute-start.4 = (bf16[4,64,128]{2,1,0:T(8,128)(2,1)S(1)}, bf16[4,64,128]{2,1,0:T(8,128)(2,1)S(1)}, u32[]{:S(2)}, u32[]{:S(2)}) collective-permute-start(bf16[4,64,128]{2,1,0:T(8,128)(2,1)S(1)} %pad_maximum_fusion.1), channel_id=1, source_target_pairs={{0,16},{4,20},{8,24},{12,28},{16,0},{20,4},{24,8},{28,12},{1,17},{... | collective-permute-start | bytes 196616 | tf_op jit(solution)/shard_map/ppermute | solution.py:387
  28.6 4.9 %count_hits.1.hits_ref = s32[3,64,4096]{2,1,0:T(8,128)} custom-call(s32[3,8,4096]{2,1,0:T(8,128)} %bitcast.10, s32[3,1,4096]{2,1,0:T(1,128)} %bitcast.11, f32[8,256,128]{2,1,0:T(8,128)} %get-tuple-element.39.refs_0_), custom_call_target="tpu_custom_call" | custom-call | flops 5000000000 | bytes 1024 | tf_op jit(solution)/shard_map/count_hits/pallas_call | solution.py:259
  34.4 1.5 %collective-permute-done.6 = bf16[16,64,128]{2,1,0:T(8,128)(2,1)S(1)} collective-permute-done((bf16[16,64,128]{2,1,0:T(8,128)(2,1)S(1)}, bf16[16,64,128]{2,1,0:T(8,128)(2,1)S(1)}, u32[]{:S(2)}, u32[]{:S(2)}) %collective-permute-start.6) | collective-permute-done | bytes 262176 | tf_op jit(solution)/shard_map/ppermute | solution.py:387
  36.0 1.0 %copy-done.5 = f32[8,256,128]{2,1,0:T(8,128)} copy-done((f32[8,256,128]{2,1,0:T(8,128)}, f32[8,256,128]{2,1,0:T(8,128)S(1)}, u32[]{:S(2)}) %copy-start.5) | copy-done | bytes 1048600
  37.0 1.0 %copy-done.6 = f32[8,256,128]{2,1,0:T(8,128)} copy-done((f32[8,256,128]{2,1,0:T(8,128)}, f32[8,256,128]{2,1,0:T(8,128)S(1)}, u32[]{:S(2)}) %copy-start.6) | copy-done | bytes 1048600
  38.0 4.4 %partial_proj.3 = (f32[4,256,128]{2,1,0:T(8,128)}, bf16[4,256,128]{2,1,0:T(8,128)(2,1)}, bf16[4,256,128]{2,1,0:T(8,128)(2,1)}, bf16[4,256,128]{2,1,0:T(8,128)(2,1)}) custom-call(s32[44]{0:T(128)} %fusion.9.index_ref, bf16[32,128,256]{2,1,0:T(8,128)(2,1)} %get-tuple-element.33.refs_0_, bf16[32,128,256]{2,1,0:T(8,128)(2,1)} %get-tuple-element.30.refs_1_.g_ref, ...), custom_call_target="tpu_custom_call" | custom-call | flops 4000000000 | bytes 1024 | tf_op jit(solution)/shard_map/partial_proj/pallas_call | solution.py:211
  42.5 4.5 %narrow_dpool.1 = bf16[32,64,128]{2,1,0:T(8,128)(2,1)} custom-call(s32[44]{0:T(128)} %fusion.9.index_ref, bf16[32,128,256]{2,1,0:T(8,128)(2,1)} %get-tuple-element.30.refs_1_.g_ref, bf16[32,64,128]{2,1,0:T(8,128)(2,1)} %copy-done.4, f32[4,256,128]{2,1,0:T(8,128)} %get-tuple-element.43.refs_0_.kept_ref), custom_call_target="tpu_custom_call" | custom-call | flops 4000000000 | bytes 1024 | tf_op jit(solution)/shard_map/narrow_dpool/pallas_call | solution.py:139
  47.0 1.2 %collective-permute-start.9 = (bf16[4,256,128]{2,1,0:T(8,128)(2,1)S(1)}, bf16[4,256,128]{2,1,0:T(8,128)(2,1)S(1)}, u32[]{:S(2)}, u32[]{:S(2)}) collective-permute-start(bf16[4,256,128]{2,1,0:T(8,128)(2,1)S(1)} %copy-done.9), channel_id=1, source_target_pairs={{0,8},{4,12},{8,0},{12,4},{16,24},{20,28},{24,16},{28,20},{1,9},{5... | collective-permute-start | bytes 786440 | tf_op jit(solution)/shard_map/ppermute | solution.py:387
  48.1 1.5 %collective-permute-start.10 = (bf16[4,256,128]{2,1,0:T(8,128)(2,1)S(1)}, bf16[4,256,128]{2,1,0:T(8,128)(2,1)S(1)}, u32[]{:S(2)}, u32[]{:S(2)}) collective-permute-start(bf16[4,256,128]{2,1,0:T(8,128)(2,1)S(1)} %copy-done.8), channel_id=1, source_target_pairs={{0,16},{4,20},{8,24},{12,28},{16,0},{20,4},{24,8},{28,12},{1,17},{... | collective-permute-start | bytes 786440 | tf_op jit(solution)/shard_map/ppermute | solution.py:387
  49.6 0.9 %collective-permute-start.11 = (bf16[4,256,128]{2,1,0:T(8,128)(2,1)S(1)}, bf16[4,256,128]{2,1,0:T(8,128)(2,1)S(1)}, u32[]{:S(2)}, u32[]{:S(2)}) collective-permute-start(bf16[4,256,128]{2,1,0:T(8,128)(2,1)S(1)} %copy-done.7), channel_id=1, source_target_pairs={{0,24},{4,28},{8,16},{12,20},{16,8},{20,12},{24,0},{28,4},{1,25},{... | collective-permute-start | bytes 786440 | tf_op jit(solution)/shard_map/ppermute | solution.py:387
  50.5 5.2 %all-to-all-start.1 = ((bf16[32,64,128]{2,1,0:T(8,128)(2,1)}), bf16[32,64,128]{2,1,0:T(8,128)(2,1)S(1)}, u32[]{:S(2)}, u32[]{:S(2)}) async-start(bf16[32,64,128]{2,1,0:T(8,128)(2,1)} %narrow_dpool.1), calls=%async_computation.1 | async-start | bytes 1048576 | tf_op jit(solution)/shard_map/all_to_all | solution.py:428
  55.8 5.3 %wide_sum.1.refs_3_.wide_ref = f32[512,256]{1,0:T(8,128)} custom-call(s32[3,64,4096]{2,1,0:T(8,128)} %count_hits.1.hits_ref, bf16[4096,128]{1,0:T(8,128)(2,1)S(1)} %bitcast.7, bf16[256,128]{1,0:T(8,128)(2,1)S(1)} %bitcast.9), custom_call_target="tpu_custom_call" | custom-call | flops 10000000 | bytes 1024 | tf_op jit(solution)/shard_map/wide_sum/pallas_call | solution.py:297
  61.1 3.9 %collective-permute-done.10.refs_1_ = bf16[4,256,128]{2,1,0:T(8,128)(2,1)S(1)} collective-permute-done((bf16[4,256,128]{2,1,0:T(8,128)(2,1)S(1)}, bf16[4,256,128]{2,1,0:T(8,128)(2,1)S(1)}, u32[]{:S(2)}, u32[]{:S(2)}) %collective-permute-start.10) | collective-permute-done | bytes 262176 | tf_op jit(solution)/shard_map/ppermute | solution.py:387
  64.9 1.0 %copy-done = f32[512,256]{1,0:T(8,128)S(1)} copy-done((f32[512,256]{1,0:T(8,128)S(1)}, f32[512,256]{1,0:T(8,128)}, u32[]{:S(2)}) %copy-start) | copy-done | bytes 524312
  66.1 1.4 %collective-permute-start.12 = (bf16[1,256,128]{2,1,0:T(8,128)(2,1)S(1)}, bf16[1,256,128]{2,1,0:T(8,128)(2,1)S(1)}, u32[]{:S(2)}, u32[]{:S(2)}) collective-permute-start(bf16[1,256,128]{2,1,0:T(8,128)(2,1)S(1)} %get-tuple-element.49), channel_id=1, source_target_pairs={{0,1},{1,0},{2,3},{3,2},{4,5},{5,4},{6,7},{7,6},{8,9},{9,8},{10,11... | collective-permute-start | bytes 196616 | tf_op jit(solution)/shard_map/ppermute | solution.py:387
  67.6 4.3 %collective-permute-start.13 = (bf16[1,256,128]{2,1,0:T(8,128)(2,1)S(1)}, bf16[1,256,128]{2,1,0:T(8,128)(2,1)S(1)}, u32[]{:S(2)}, u32[]{:S(2)}) collective-permute-start(bf16[1,256,128]{2,1,0:T(8,128)(2,1)S(1)} %get-tuple-element.50), channel_id=1, source_target_pairs={{0,2},{1,3},{2,0},{3,1},{4,6},{5,7},{6,4},{7,5},{8,10},{9,11},{10,... | collective-permute-start | bytes 196616 | tf_op jit(solution)/shard_map/ppermute | solution.py:387
  72.2 0.8 %copy-done.3 = bf16[32,64,128]{2,1,0:T(8,128)(2,1)} copy-done((bf16[32,64,128]{2,1,0:T(8,128)(2,1)}, bf16[32,64,128]{2,1,0:T(8,128)(2,1)S(1)}, u32[]{:S(2)}) %copy-start.3) | copy-done | bytes 524312
  73.1 5.4 %narrow_sum.1 = f32[512,256]{1,0:T(8,128)} custom-call(s32[3,64,4096]{2,1,0:T(8,128)} %count_hits.1.hits_ref, bf16[32,64,128]{2,1,0:T(8,128)(2,1)} %copy-done.3, f32[512,256]{1,0:T(8,128)} %wide_sum.1.refs_3_.wide_ref), custom_call_target="tpu_custom_call", output_to_operand_aliasing={{}: (2, {})} | custom-call | flops 10000000 | bytes 1024 | tf_op jit(solution)/shard_map/narrow_sum/pallas_call | solution.py:341
  (48 shorter events, 4.1 us)
Async XLA Ops:
  1.4 12.1 %collective-permute-start.2 = (bf16[1,64,128]{2,1,0:T(8,128)(2,1)S(1)}, bf16[1,64,128]{2,1,0:T(8,128)(2,1)S(1)}, u32[]{:S(2)}, u32[]{:S(2)}) collective-permute-start(bf16[1,64,128]{2,1,0:T(8,128)(2,1)S(1)} %slice.3), channel_id=1, source_target_pairs={{0,3},{1,2},{2,1},{3,0},{4,7},{5,6},{6,5},{7,4},{8,11},{9,10},{10,... | collective-permute-start | bytes 49160 | tf_op jit(solution)/shard_map/ppermute | solution.py:387
  6.4 7.1 %collective-permute-start.1 = (bf16[1,64,128]{2,1,0:T(8,128)(2,1)S(1)}, bf16[1,64,128]{2,1,0:T(8,128)(2,1)S(1)}, u32[]{:S(2)}, u32[]{:S(2)}) collective-permute-start(bf16[1,64,128]{2,1,0:T(8,128)(2,1)S(1)} %slice.3), channel_id=1, source_target_pairs={{0,2},{1,3},{2,0},{3,1},{4,6},{5,7},{6,4},{7,5},{8,10},{9,11},{10,... | collective-permute-start | bytes 49160 | tf_op jit(solution)/shard_map/ppermute | solution.py:387
  6.4 7.1 %collective-permute-start = (bf16[1,64,128]{2,1,0:T(8,128)(2,1)S(1)}, bf16[1,64,128]{2,1,0:T(8,128)(2,1)S(1)}, u32[]{:S(2)}, u32[]{:S(2)}) collective-permute-start(bf16[1,64,128]{2,1,0:T(8,128)(2,1)S(1)} %slice.3), channel_id=1, source_target_pairs={{0,1},{1,0},{2,3},{3,2},{4,5},{5,4},{6,7},{7,6},{8,9},{9,8},{10,11... | collective-permute-start | bytes 49160 | tf_op jit(solution)/shard_map/ppermute | solution.py:387
  13.5 33.4 %all-to-all-start = ((bf16[32,128,128]{2,1,0:T(8,128)(2,1)}), bf16[32,128,128]{2,1,0:T(8,128)(2,1)S(1)}, u32[]{:S(2)}, u32[]{:S(2)}) async-start(bf16[32,128,128]{2,1,0:T(8,128)(2,1)} %get-tuple-element.34.refs_2_), calls=%async_computation | async-start | bytes 2097152 | tf_op jit(solution)/shard_map/all_to_all | solution.py:415
  24.5 9.0 %collective-permute-start.3 = (bf16[4,64,128]{2,1,0:T(8,128)(2,1)S(1)}, bf16[4,64,128]{2,1,0:T(8,128)(2,1)S(1)}, u32[]{:S(2)}, u32[]{:S(2)}) collective-permute-start(bf16[4,64,128]{2,1,0:T(8,128)(2,1)S(1)} %pad_maximum_fusion.1), channel_id=1, source_target_pairs={{0,8},{4,12},{8,0},{12,4},{16,24},{20,28},{24,16},{28,20},{1,9},{5... | collective-permute-start | bytes 196616 | tf_op jit(solution)/shard_map/ppermute | solution.py:387
  26.3 7.9 %collective-permute-start.4 = (bf16[4,64,128]{2,1,0:T(8,128)(2,1)S(1)}, bf16[4,64,128]{2,1,0:T(8,128)(2,1)S(1)}, u32[]{:S(2)}, u32[]{:S(2)}) collective-permute-start(bf16[4,64,128]{2,1,0:T(8,128)(2,1)S(1)} %pad_maximum_fusion.1), channel_id=1, source_target_pairs={{0,16},{4,20},{8,24},{12,28},{16,0},{20,4},{24,8},{28,12},{1,17},{... | collective-permute-start | bytes 196616 | tf_op jit(solution)/shard_map/ppermute | solution.py:387
  27.8 6.4 %collective-permute-start.5 = (bf16[4,64,128]{2,1,0:T(8,128)(2,1)S(1)}, bf16[4,64,128]{2,1,0:T(8,128)(2,1)S(1)}, u32[]{:S(2)}, u32[]{:S(2)}) collective-permute-start(bf16[4,64,128]{2,1,0:T(8,128)(2,1)S(1)} %pad_maximum_fusion.1), channel_id=1, source_target_pairs={{0,24},{4,28},{8,16},{12,20},{16,8},{20,12},{24,0},{28,4},{1,25},{... | collective-permute-start | bytes 196616 | tf_op jit(solution)/shard_map/ppermute | solution.py:387
  28.1 7.9 %collective-permute-start.7 = (f32[8,256,128]{2,1,0:T(8,128)}, f32[8,256,128]{2,1,0:T(8,128)S(1)}, u32[]{:S(2)}, u32[]{:S(2)}) collective-permute-start(f32[8,256,128]{2,1,0:T(8,128)} %get-tuple-element.39.refs_0_), channel_id=1, source_target_pairs={{0,4},{4,0},{8,12},{12,8},{16,20},{20,16},{24,28},{28,24},{1,5},{5... | collective-permute-start | bytes 3145736 | tf_op jit(solution)/shard_map/ppermute | solution.py:387
  28.1 7.9 %collective-permute-start.8 = (f32[8,256,128]{2,1,0:T(8,128)}, f32[8,256,128]{2,1,0:T(8,128)S(1)}, u32[]{:S(2)}, u32[]{:S(2)}) collective-permute-start(f32[8,256,128]{2,1,0:T(8,128)} %get-tuple-element.36), channel_id=1, source_target_pairs={{0,4},{4,0},{8,12},{12,8},{16,20},{20,16},{24,28},{28,24},{1,5},{5... | collective-permute-start | bytes 3145736 | tf_op jit(solution)/shard_map/ppermute | solution.py:387
  34.3 1.6 %collective-permute-start.6 = (bf16[16,64,128]{2,1,0:T(8,128)(2,1)S(1)}, bf16[16,64,128]{2,1,0:T(8,128)(2,1)S(1)}, u32[]{:S(2)}, u32[]{:S(2)}) collective-permute-start(bf16[16,64,128]{2,1,0:T(8,128)(2,1)S(1)} %pad_maximum_fusion), channel_id=1, source_target_pairs={{0,4},{4,0},{8,12},{12,8},{16,20},{20,16},{24,28},{28,24},{1,5},{5... | collective-permute-start | bytes 786440 | tf_op jit(solution)/shard_map/ppermute | solution.py:387
  35.9 6.5 %copy-start.4 = (bf16[32,64,128]{2,1,0:T(8,128)(2,1)}, bf16[32,64,128]{2,1,0:T(8,128)(2,1)S(1)}, u32[]{:S(2)}) copy-start(bf16[32,64,128]{2,1,0:T(8,128)(2,1)S(1)} %constant_dynamic-update-slice_fusion.w_ref) | copy-start | bytes 1572868
  35.9 1.1 %copy-start.5 = (f32[8,256,128]{2,1,0:T(8,128)}, f32[8,256,128]{2,1,0:T(8,128)S(1)}, u32[]{:S(2)}) copy-start(f32[8,256,128]{2,1,0:T(8,128)S(1)} %collective-permute-done.7.refs_3_) | copy-start | bytes 3145732
  42.4 4.5 %copy-start.9 = (bf16[4,256,128]{2,1,0:T(8,128)(2,1)S(1)}, bf16[4,256,128]{2,1,0:T(8,128)(2,1)}, u32[]{:S(2)}) copy-start(bf16[4,256,128]{2,1,0:T(8,128)(2,1)} %get-tuple-element.44) | copy-start | bytes 786436
  42.4 5.7 %copy-start.8 = (bf16[4,256,128]{2,1,0:T(8,128)(2,1)S(1)}, bf16[4,256,128]{2,1,0:T(8,128)(2,1)}, u32[]{:S(2)}) copy-start(bf16[4,256,128]{2,1,0:T(8,128)(2,1)} %get-tuple-element.45) | copy-start | bytes 786436
  42.4 7.2 %copy-start.7 = (bf16[4,256,128]{2,1,0:T(8,128)(2,1)S(1)}, bf16[4,256,128]{2,1,0:T(8,128)(2,1)}, u32[]{:S(2)}) copy-start(bf16[4,256,128]{2,1,0:T(8,128)(2,1)} %get-tuple-element.46) | copy-start | bytes 786436
  42.5 13.3 %copy-start.1 = (bf16[1,256,128]{2,1,0:T(8,128)(2,1)S(1)}, bf16[1,256,128]{2,1,0:T(8,128)(2,1)}, u32[]{:S(2)}) copy-start(bf16[1,256,128]{2,1,0:T(8,128)(2,1)} %param.8) | copy-start | bytes 196612
  47.0 14.1 %collective-permute-start.9 = (bf16[4,256,128]{2,1,0:T(8,128)(2,1)S(1)}, bf16[4,256,128]{2,1,0:T(8,128)(2,1)S(1)}, u32[]{:S(2)}, u32[]{:S(2)}) collective-permute-start(bf16[4,256,128]{2,1,0:T(8,128)(2,1)S(1)} %copy-done.9), channel_id=1, source_target_pairs={{0,8},{4,12},{8,0},{12,4},{16,24},{20,28},{24,16},{28,20},{1,9},{5... | collective-permute-start | bytes 786440 | tf_op jit(solution)/shard_map/ppermute | solution.py:387
  48.1 16.8 %collective-permute-start.10 = (bf16[4,256,128]{2,1,0:T(8,128)(2,1)S(1)}, bf16[4,256,128]{2,1,0:T(8,128)(2,1)S(1)}, u32[]{:S(2)}, u32[]{:S(2)}) collective-permute-start(bf16[4,256,128]{2,1,0:T(8,128)(2,1)S(1)} %copy-done.8), channel_id=1, source_target_pairs={{0,16},{4,20},{8,24},{12,28},{16,0},{20,4},{24,8},{28,12},{1,17},{... | collective-permute-start | bytes 786440 | tf_op jit(solution)/shard_map/ppermute | solution.py:387
  49.6 15.3 %collective-permute-start.11 = (bf16[4,256,128]{2,1,0:T(8,128)(2,1)S(1)}, bf16[4,256,128]{2,1,0:T(8,128)(2,1)S(1)}, u32[]{:S(2)}, u32[]{:S(2)}) collective-permute-start(bf16[4,256,128]{2,1,0:T(8,128)(2,1)S(1)} %copy-done.7), channel_id=1, source_target_pairs={{0,24},{4,28},{8,16},{12,20},{16,8},{20,12},{24,0},{28,4},{1,25},{... | collective-permute-start | bytes 786440 | tf_op jit(solution)/shard_map/ppermute | solution.py:387
  50.5 21.7 %all-to-all-start.1 = ((bf16[32,64,128]{2,1,0:T(8,128)(2,1)}), bf16[32,64,128]{2,1,0:T(8,128)(2,1)S(1)}, u32[]{:S(2)}, u32[]{:S(2)}) async-start(bf16[32,64,128]{2,1,0:T(8,128)(2,1)} %narrow_dpool.1), calls=%async_computation.1 | async-start | bytes 1048576 | tf_op jit(solution)/shard_map/all_to_all | solution.py:428
  55.8 9.2 %copy-start.2 = (f32[4,256,128]{2,1,0:T(8,128)S(1)}, f32[4,256,128]{2,1,0:T(8,128)}, u32[]{:S(2)}) copy-start(f32[4,256,128]{2,1,0:T(8,128)} %get-tuple-element.43.refs_0_.kept_ref) | copy-start | bytes 1572868
  66.1 12.3 %collective-permute-start.12 = (bf16[1,256,128]{2,1,0:T(8,128)(2,1)S(1)}, bf16[1,256,128]{2,1,0:T(8,128)(2,1)S(1)}, u32[]{:S(2)}, u32[]{:S(2)}) collective-permute-start(bf16[1,256,128]{2,1,0:T(8,128)(2,1)S(1)} %get-tuple-element.49), channel_id=1, source_target_pairs={{0,1},{1,0},{2,3},{3,2},{4,5},{5,4},{6,7},{7,6},{8,9},{9,8},{10,11... | collective-permute-start | bytes 196616 | tf_op jit(solution)/shard_map/ppermute | solution.py:387
  67.6 10.9 %collective-permute-start.13 = (bf16[1,256,128]{2,1,0:T(8,128)(2,1)S(1)}, bf16[1,256,128]{2,1,0:T(8,128)(2,1)S(1)}, u32[]{:S(2)}, u32[]{:S(2)}) collective-permute-start(bf16[1,256,128]{2,1,0:T(8,128)(2,1)S(1)} %get-tuple-element.50), channel_id=1, source_target_pairs={{0,2},{1,3},{2,0},{3,1},{4,6},{5,7},{6,4},{7,5},{8,10},{9,11},{10,... | collective-permute-start | bytes 196616 | tf_op jit(solution)/shard_map/ppermute | solution.py:387
  71.8 6.6 %collective-permute-start.14 = (bf16[1,256,128]{2,1,0:T(8,128)(2,1)S(1)}, bf16[1,256,128]{2,1,0:T(8,128)(2,1)S(1)}, u32[]{:S(2)}, u32[]{:S(2)}) collective-permute-start(bf16[1,256,128]{2,1,0:T(8,128)(2,1)S(1)} %get-tuple-element.51), channel_id=1, source_target_pairs={{0,3},{1,2},{2,1},{3,0},{4,7},{5,6},{6,5},{7,4},{8,11},{9,10},{10,... | collective-permute-start | bytes 196616 | tf_op jit(solution)/shard_map/ppermute | solution.py:387
  (3 other events, 2.9 us)

commit v3 on v2

--- a/solution.py
+++ b/solution.py
@@ -160,10 +160,8 @@
 
 
 def partial_kernel(first, blocks, size, ins, added, results, index_ref, *refs):
-    operands, others = refs[:ins], refs[ins : ins + added]
-    outs, scratch = refs[-3 - 2 * results - ins - added :][:results], refs[-3 - results - ins - added :]
-    held, other_held, out_held = scratch[:ins], scratch[ins : ins + added], scratch[ins + added : -3]
-    in_sems, other_sems, out_sems = scratch[-3:]
+    operands, others, outs = refs[:ins], refs[ins : ins + added], refs[ins + added : ins + added + results]
+    held, out_held, (in_sems, out_sems) = refs[-2 - results - ins : -2 - results], refs[-2 - results : -2], refs[-2:]
 
     def block(arrays, i):
         per = blocks // len(arrays)
@@ -173,15 +171,6 @@
         fetch(ref, at, in_sems.at[n], blocks, lambda i: index_ref[first + i])
         for n, (ref, at) in enumerate(zip(operands, held))
     ]
-    if added:
-        loads.append(
-            [
-                pltpu.make_async_copy(block(others, i), block(other_held, i), other_sems.at[i])
-                for i in range(blocks)
-            ]
-        )
-        for copy in loads[-1]:
-            copy.start()
     stores = []
     for i in range(blocks):
         for copies in loads:
@@ -195,7 +184,7 @@
             pieces = ((0, W1, narrow[:W1, :PD]), (W1, W12, narrow[W1:, PD:]), (W12, WSUM, wide))
             for start, end, piece in pieces:
                 if added:
-                    piece = piece + block(other_held, i)[l, start:end]
+                    piece = piece + block(others, i)[l, start:end]
                 out[l, start:end] = piece.astype(out.dtype)
         stores.append(pltpu.make_async_copy(out, block(outs, i), out_sems.at[i]))
         stores[-1].start()
@@ -208,24 +197,18 @@
     kinds = [jnp.bfloat16 if others and i else jnp.float32 for i in range(results)]
     shapes = [jax.ShapeDtypeStruct((blocks // results * size, WSUM, PD), kind) for kind in kinds]
     operands = (q, g12, g3)
+    beside = sum(4 * x.size for x in others) // MIB
     return pl.pallas_call(
         functools.partial(partial_kernel, first, blocks, size, len(operands), len(others), results),
         out_shape=shapes,
-        grid_spec=pltpu.PrefetchScalarGridSpec(
-            num_scalar_prefetch=1,
-            grid=(1,),
-            in_specs=[HBM] * len(operands) + [ANY] * len(others),
-            out_specs=[HBM] * results,
-            scratch_shapes=[pltpu.VMEM((blocks * size, count, x.shape[2]), jnp.bfloat16) for x in operands]
-            + [pltpu.VMEM(x.shape, x.dtype) for x in others]
-            + [pltpu.VMEM(x.shape, x.dtype) for x in shapes]
-            + [
-                pltpu.SemaphoreType.DMA((len(operands), blocks)),
-                pltpu.SemaphoreType.DMA((blocks,)),
-                pltpu.SemaphoreType.DMA((blocks,)),
-            ],
-        ),
-        compiler_params=params(1),
+        in_specs=[pl.BlockSpec(memory_space=pltpu.SMEM)]
+        + [HBM] * len(operands)
+        + [pl.BlockSpec(memory_space=pltpu.VMEM)] * len(others),
+        out_specs=[HBM] * results,
+        scratch_shapes=[pltpu.VMEM((blocks * size, count, x.shape[2]), jnp.bfloat16) for x in operands]
+        + [pltpu.VMEM(x.shape, x.dtype) for x in shapes]
+        + [pltpu.SemaphoreType.DMA((len(operands), blocks)), pltpu.SemaphoreType.DMA((blocks,))],
+        compiler_params=params(0, 58 - beside),
         cost_estimate=cost(4e9 if others else 1e7),
         name="partial_proj",
     )(index, *operands, *others)

time: 79.8 us -> 80.5 us (level)
  no operation moved by 1% of the time
where the time goes in v3:
time: 80.5 us; the launch traced here: 79.8 us
  Pallas kernels  36.1 us (45%)
  starting transfers between devices  30.7 us (38%)
  waiting for transfers between devices  6.1 us (8%)
  local copies, waits for them, and re-layouts  4.73 us (6%)
  other arithmetic  1.27 us (2%)
  between operations  0.9 us (1%)
    ppermute x15, starting transfers between devices, swap(): return lax.ppermute(x, axis, [(d, d ^ bits) for d in range(size)])  19.4 us
    pallas_call x2, Pallas kernels, partial_proj(): pl.pallas_call(functools.partial(partial_kernel, first, blocks, size, len...  9.38 us
    pallas_call x1, Pallas kernels, permute(): pl.pallas_call(functools.partial(permute_kernel, slots, pieces), out_shap...  6.5 us
    ppermute x15, waiting for transfers between devices, swap(): return lax.ppermute(x, axis, [(d, d ^ bits) for d in range(size)])  6.09 us
    all_to_all x1, starting transfers between devices, local(): g3_got = lax.all_to_all(g3, AXES, split_axis=0, concat_axis=0, tiled=True)  6.07 us
    pallas_call x1, Pallas kernels, narrow_sum(): pl.pallas_call(narrow_sum_kernel, out_shape=jax.ShapeDtypeStruct((ROWS, W...  5.39 us
    pallas_call x1, Pallas kernels, wide_sum(): pl.pallas_call(wide_kernel, out_shape=jax.ShapeDtypeStruct((ROWS, WSUM),...  5.28 us
    all_to_all x1, starting transfers between devices, local(): lax.all_to_all(narrow, AXES, split_axis=0, concat_axis=0, tiled=True)  5.17 us
  transfers between devices with their start and end apart: 17, of which 3 were waited for; matrix products, arithmetic and copies ran while one was open for 1% of the time, Pallas kernels for 45%

profile of v3, /device:TPU:0, one launch (start us, length us, event | category | flops | bytes accessed | tf_op | source)
XLA Modules:
  0.0 79.8 jit_solution(7680147877526005587)
XLA Ops:
  1.4 5.0 %collective-permute-start.2 = (bf16[1,64,128]{2,1,0:T(8,128)(2,1)S(1)}, bf16[1,64,128]{2,1,0:T(8,128)(2,1)S(1)}, u32[]{:S(2)}, u32[]{:S(2)}) collective-permute-start(bf16[1,64,128]{2,1,0:T(8,128)(2,1)S(1)} %slice.3), channel_id=1, source_target_pairs={{0,3},{1,2},{2,1},{3,0},{4,7},{5,6},{6,5},{7,4},{8,11},{9,10},{10,... | collective-permute-start | bytes 49160 | tf_op jit(solution)/shard_map/ppermute | solution.py:370
  7.0 6.5 %permute_groups.1 = (bf16[32,128,256]{2,1,0:T(8,128)(2,1)}, bf16[32,128,128]{2,1,0:T(8,128)(2,1)}, bf16[32,128,256]{2,1,0:T(8,128)(2,1)}) custom-call(s32[32]{0:T(128)} %assign_ref.1, bf16[128,32,384]{2,1,0:T(8,128)(2,1)} %grad_ref.1, bf16[128,32,256]{2,1,0:T(8,128)(2,1)} %pool_ref.1), custom_call_target="tpu_custom_call" | custom-call | flops 10000000 | bytes 1024 | tf_op jit(solution)/shard_map/permute_groups/pallas_call | solution.py:78
  13.5 6.1 %all-to-all-start = ((bf16[32,128,128]{2,1,0:T(8,128)(2,1)}), bf16[32,128,128]{2,1,0:T(8,128)(2,1)S(1)}, u32[]{:S(2)}, u32[]{:S(2)}) async-start(bf16[32,128,128]{2,1,0:T(8,128)(2,1)} %get-tuple-element.34.refs_2_), calls=%async_computation | async-start | bytes 2097152 | tf_op jit(solution)/shard_map/all_to_all | solution.py:398
  20.2 4.3 %partial_proj.2 = (f32[8,256,128]{2,1,0:T(8,128)}, f32[8,256,128]{2,1,0:T(8,128)}) custom-call(s32[44]{0:T(128)} %fusion.9.index_ref, bf16[32,128,256]{2,1,0:T(8,128)(2,1)} %get-tuple-element.33.refs_0_, bf16[32,128,256]{2,1,0:T(8,128)(2,1)} %get-tuple-element.30.refs_1_.g_ref, bf16[32,128,128]{2,1,0:T(8,128)(2,1)} %get-tuple-element.34.refs_2_), custom_call_target="tpu_custom_call" | custom-call | flops 10000000 | bytes 1024 | tf_op jit(solution)/shard_map/partial_proj/pallas_call | solution.py:201
  24.5 1.8 %collective-permute-start.3 = (bf16[4,64,128]{2,1,0:T(8,128)(2,1)S(1)}, bf16[4,64,128]{2,1,0:T(8,128)(2,1)S(1)}, u32[]{:S(2)}, u32[]{:S(2)}) collective-permute-start(bf16[4,64,128]{2,1,0:T(8,128)(2,1)S(1)} %pad_maximum_fusion.1), channel_id=1, source_target_pairs={{0,8},{4,12},{8,0},{12,4},{16,24},{20,28},{24,16},{28,20},{1,9},{5... | collective-permute-start | bytes 196616 | tf_op jit(solution)/shard_map/ppermute | solution.py:370
  26.3 1.5 %collective-permute-start.4 = (bf16[4,64,128]{2,1,0:T(8,128)(2,1)S(1)}, bf16[4,64,128]{2,1,0:T(8,128)(2,1)S(1)}, u32[]{:S(2)}, u32[]{:S(2)}) collective-permute-start(bf16[4,64,128]{2,1,0:T(8,128)(2,1)S(1)} %pad_maximum_fusion.1), channel_id=1, source_target_pairs={{0,16},{4,20},{8,24},{12,28},{16,0},{20,4},{24,8},{28,12},{1,17},{... | collective-permute-start | bytes 196616 | tf_op jit(solution)/shard_map/ppermute | solution.py:370
  28.5 4.9 %count_hits.1.hits_ref = s32[3,64,4096]{2,1,0:T(8,128)} custom-call(s32[3,8,4096]{2,1,0:T(8,128)} %bitcast.10, s32[3,1,4096]{2,1,0:T(1,128)} %bitcast.11, f32[8,256,128]{2,1,0:T(8,128)} %get-tuple-element.39.refs_0_), custom_call_target="tpu_custom_call" | custom-call | flops 5000000000 | bytes 1024 | tf_op jit(solution)/shard_map/count_hits/pallas_call | solution.py:242
  33.5 0.7 collective-permute-done.4
  34.4 1.5 %collective-permute-done.6 = bf16[16,64,128]{2,1,0:T(8,128)(2,1)S(1)} collective-permute-done((bf16[16,64,128]{2,1,0:T(8,128)(2,1)S(1)}, bf16[16,64,128]{2,1,0:T(8,128)(2,1)S(1)}, u32[]{:S(2)}, u32[]{:S(2)}) %collective-permute-start.6) | collective-permute-done | bytes 262176 | tf_op jit(solution)/shard_map/ppermute | solution.py:370
  36.0 1.0 %copy-done.5 = f32[8,256,128]{2,1,0:T(8,128)} copy-done((f32[8,256,128]{2,1,0:T(8,128)}, f32[8,256,128]{2,1,0:T(8,128)S(1)}, u32[]{:S(2)}) %copy-start.5) | copy-done | bytes 1048600
  37.0 1.0 %copy-done.6 = f32[8,256,128]{2,1,0:T(8,128)} copy-done((f32[8,256,128]{2,1,0:T(8,128)}, f32[8,256,128]{2,1,0:T(8,128)S(1)}, u32[]{:S(2)}) %copy-start.6) | copy-done | bytes 1048600
  38.0 5.1 %partial_proj.3 = (f32[4,256,128]{2,1,0:T(8,128)}, bf16[4,256,128]{2,1,0:T(8,128)(2,1)}, bf16[4,256,128]{2,1,0:T(8,128)(2,1)}, bf16[4,256,128]{2,1,0:T(8,128)(2,1)}) custom-call(s32[44]{0:T(128)} %fusion.9.index_ref, bf16[32,128,256]{2,1,0:T(8,128)(2,1)} %get-tuple-element.33.refs_0_, bf16[32,128,256]{2,1,0:T(8,128)(2,1)} %get-tuple-element.30.refs_1_.g_ref, ...), custom_call_target="tpu_custom_call" | custom-call | flops 4000000000 | bytes 1024 | tf_op jit(solution)/shard_map/partial_proj/pallas_call | solution.py:201
  43.1 4.5 %narrow_dpool.1 = bf16[32,64,128]{2,1,0:T(8,128)(2,1)} custom-call(s32[44]{0:T(128)} %fusion.9.index_ref, bf16[32,128,256]{2,1,0:T(8,128)(2,1)} %get-tuple-element.30.refs_1_.g_ref, bf16[32,64,128]{2,1,0:T(8,128)(2,1)} %copy-done.4, f32[4,256,128]{2,1,0:T(8,128)} %get-tuple-element.43.refs_0_.kept_ref), custom_call_target="tpu_custom_call" | custom-call | flops 4000000000 | bytes 1024 | tf_op jit(solution)/shard_map/narrow_dpool/pallas_call | solution.py:139
  47.6 1.1 %collective-permute-start.9 = (bf16[4,256,128]{2,1,0:T(8,128)(2,1)S(1)}, bf16[4,256,128]{2,1,0:T(8,128)(2,1)S(1)}, u32[]{:S(2)}, u32[]{:S(2)}) collective-permute-start(bf16[4,256,128]{2,1,0:T(8,128)(2,1)S(1)} %copy-done.9), channel_id=1, source_target_pairs={{0,8},{4,12},{8,0},{12,4},{16,24},{20,28},{24,16},{28,20},{1,9},{5... | collective-permute-start | bytes 786440 | tf_op jit(solution)/shard_map/ppermute | solution.py:370
  48.8 1.5 %collective-permute-start.10 = (bf16[4,256,128]{2,1,0:T(8,128)(2,1)S(1)}, bf16[4,256,128]{2,1,0:T(8,128)(2,1)S(1)}, u32[]{:S(2)}, u32[]{:S(2)}) collective-permute-start(bf16[4,256,128]{2,1,0:T(8,128)(2,1)S(1)} %copy-done.8), channel_id=1, source_target_pairs={{0,16},{4,20},{8,24},{12,28},{16,0},{20,4},{24,8},{28,12},{1,17},{... | collective-permute-start | bytes 786440 | tf_op jit(solution)/shard_map/ppermute | solution.py:370
  50.2 1.0 %collective-permute-start.11 = (bf16[4,256,128]{2,1,0:T(8,128)(2,1)S(1)}, bf16[4,256,128]{2,1,0:T(8,128)(2,1)S(1)}, u32[]{:S(2)}, u32[]{:S(2)}) collective-permute-start(bf16[4,256,128]{2,1,0:T(8,128)(2,1)S(1)} %copy-done.7), channel_id=1, source_target_pairs={{0,24},{4,28},{8,16},{12,20},{16,8},{20,12},{24,0},{28,4},{1,25},{... | collective-permute-start | bytes 786440 | tf_op jit(solution)/shard_map/ppermute | solution.py:370
  51.2 5.2 %all-to-all-start.1 = ((bf16[32,64,128]{2,1,0:T(8,128)(2,1)}), bf16[32,64,128]{2,1,0:T(8,128)(2,1)S(1)}, u32[]{:S(2)}, u32[]{:S(2)}) async-start(bf16[32,64,128]{2,1,0:T(8,128)(2,1)} %narrow_dpool.1), calls=%async_computation.1 | async-start | bytes 1048576 | tf_op jit(solution)/shard_map/all_to_all | solution.py:411
  56.4 5.3 %wide_sum.1.refs_3_.wide_ref = f32[512,256]{1,0:T(8,128)} custom-call(s32[3,64,4096]{2,1,0:T(8,128)} %count_hits.1.hits_ref, bf16[4096,128]{1,0:T(8,128)(2,1)S(1)} %bitcast.7, bf16[256,128]{1,0:T(8,128)(2,1)S(1)} %bitcast.9), custom_call_target="tpu_custom_call" | custom-call | flops 10000000 | bytes 1024 | tf_op jit(solution)/shard_map/wide_sum/pallas_call | solution.py:280
  61.7 3.9 %collective-permute-done.10.refs_1_ = bf16[4,256,128]{2,1,0:T(8,128)(2,1)S(1)} collective-permute-done((bf16[4,256,128]{2,1,0:T(8,128)(2,1)S(1)}, bf16[4,256,128]{2,1,0:T(8,128)(2,1)S(1)}, u32[]{:S(2)}, u32[]{:S(2)}) %collective-permute-start.10) | collective-permute-done | bytes 262176 | tf_op jit(solution)/shard_map/ppermute | solution.py:370
  65.6 1.0 %copy-done = f32[512,256]{1,0:T(8,128)S(1)} copy-done((f32[512,256]{1,0:T(8,128)S(1)}, f32[512,256]{1,0:T(8,128)}, u32[]{:S(2)}) %copy-start) | copy-done | bytes 524312
  66.7 1.5 %collective-permute-start.12 = (bf16[1,256,128]{2,1,0:T(8,128)(2,1)S(1)}, bf16[1,256,128]{2,1,0:T(8,128)(2,1)S(1)}, u32[]{:S(2)}, u32[]{:S(2)}) collective-permute-start(bf16[1,256,128]{2,1,0:T(8,128)(2,1)S(1)} %get-tuple-element.49), channel_id=1, source_target_pairs={{0,1},{1,0},{2,3},{3,2},{4,5},{5,4},{6,7},{7,6},{8,9},{9,8},{10,11... | collective-permute-start | bytes 196616 | tf_op jit(solution)/shard_map/ppermute | solution.py:370
  68.2 4.2 %collective-permute-start.13 = (bf16[1,256,128]{2,1,0:T(8,128)(2,1)S(1)}, bf16[1,256,128]{2,1,0:T(8,128)(2,1)S(1)}, u32[]{:S(2)}, u32[]{:S(2)}) collective-permute-start(bf16[1,256,128]{2,1,0:T(8,128)(2,1)S(1)} %get-tuple-element.50), channel_id=1, source_target_pairs={{0,2},{1,3},{2,0},{3,1},{4,6},{5,7},{6,4},{7,5},{8,10},{9,11},{10,... | collective-permute-start | bytes 196616 | tf_op jit(solution)/shard_map/ppermute | solution.py:370
  72.9 0.8 %copy-done.3 = bf16[32,64,128]{2,1,0:T(8,128)(2,1)} copy-done((bf16[32,64,128]{2,1,0:T(8,128)(2,1)}, bf16[32,64,128]{2,1,0:T(8,128)(2,1)S(1)}, u32[]{:S(2)}) %copy-start.3) | copy-done | bytes 524312
  73.7 5.4 %narrow_sum.1 = f32[512,256]{1,0:T(8,128)} custom-call(s32[3,64,4096]{2,1,0:T(8,128)} %count_hits.1.hits_ref, bf16[32,64,128]{2,1,0:T(8,128)(2,1)} %copy-done.3, f32[512,256]{1,0:T(8,128)} %wide_sum.1.refs_3_.wide_ref), custom_call_target="tpu_custom_call", output_to_operand_aliasing={{}: (2, {})} | custom-call | flops 10000000 | bytes 1024 | tf_op jit(solution)/shard_map/narrow_sum/pallas_call | solution.py:324
  (48 shorter events, 4.1 us)
Async XLA Ops:
  1.4 12.1 %collective-permute-start.2 = (bf16[1,64,128]{2,1,0:T(8,128)(2,1)S(1)}, bf16[1,64,128]{2,1,0:T(8,128)(2,1)S(1)}, u32[]{:S(2)}, u32[]{:S(2)}) collective-permute-start(bf16[1,64,128]{2,1,0:T(8,128)(2,1)S(1)} %slice.3), channel_id=1, source_target_pairs={{0,3},{1,2},{2,1},{3,0},{4,7},{5,6},{6,5},{7,4},{8,11},{9,10},{10,... | collective-permute-start | bytes 49160 | tf_op jit(solution)/shard_map/ppermute | solution.py:370
  6.4 7.1 %collective-permute-start.1 = (bf16[1,64,128]{2,1,0:T(8,128)(2,1)S(1)}, bf16[1,64,128]{2,1,0:T(8,128)(2,1)S(1)}, u32[]{:S(2)}, u32[]{:S(2)}) collective-permute-start(bf16[1,64,128]{2,1,0:T(8,128)(2,1)S(1)} %slice.3), channel_id=1, source_target_pairs={{0,2},{1,3},{2,0},{3,1},{4,6},{5,7},{6,4},{7,5},{8,10},{9,11},{10,... | collective-permute-start | bytes 49160 | tf_op jit(solution)/shard_map/ppermute | solution.py:370
  6.4 7.1 %collective-permute-start = (bf16[1,64,128]{2,1,0:T(8,128)(2,1)S(1)}, bf16[1,64,128]{2,1,0:T(8,128)(2,1)S(1)}, u32[]{:S(2)}, u32[]{:S(2)}) collective-permute-start(bf16[1,64,128]{2,1,0:T(8,128)(2,1)S(1)} %slice.3), channel_id=1, source_target_pairs={{0,1},{1,0},{2,3},{3,2},{4,5},{5,4},{6,7},{7,6},{8,9},{9,8},{10,11... | collective-permute-start | bytes 49160 | tf_op jit(solution)/shard_map/ppermute | solution.py:370
  13.5 34.1 %all-to-all-start = ((bf16[32,128,128]{2,1,0:T(8,128)(2,1)}), bf16[32,128,128]{2,1,0:T(8,128)(2,1)S(1)}, u32[]{:S(2)}, u32[]{:S(2)}) async-start(bf16[32,128,128]{2,1,0:T(8,128)(2,1)} %get-tuple-element.34.refs_2_), calls=%async_computation | async-start | bytes 2097152 | tf_op jit(solution)/shard_map/all_to_all | solution.py:398
  24.5 9.0 %collective-permute-start.3 = (bf16[4,64,128]{2,1,0:T(8,128)(2,1)S(1)}, bf16[4,64,128]{2,1,0:T(8,128)(2,1)S(1)}, u32[]{:S(2)}, u32[]{:S(2)}) collective-permute-start(bf16[4,64,128]{2,1,0:T(8,128)(2,1)S(1)} %pad_maximum_fusion.1), channel_id=1, source_target_pairs={{0,8},{4,12},{8,0},{12,4},{16,24},{20,28},{24,16},{28,20},{1,9},{5... | collective-permute-start | bytes 196616 | tf_op jit(solution)/shard_map/ppermute | solution.py:370
  26.3 7.9 %collective-permute-start.4 = (bf16[4,64,128]{2,1,0:T(8,128)(2,1)S(1)}, bf16[4,64,128]{2,1,0:T(8,128)(2,1)S(1)}, u32[]{:S(2)}, u32[]{:S(2)}) collective-permute-start(bf16[4,64,128]{2,1,0:T(8,128)(2,1)S(1)} %pad_maximum_fusion.1), channel_id=1, source_target_pairs={{0,16},{4,20},{8,24},{12,28},{16,0},{20,4},{24,8},{28,12},{1,17},{... | collective-permute-start | bytes 196616 | tf_op jit(solution)/shard_map/ppermute | solution.py:370
  27.8 6.5 %collective-permute-start.5 = (bf16[4,64,128]{2,1,0:T(8,128)(2,1)S(1)}, bf16[4,64,128]{2,1,0:T(8,128)(2,1)S(1)}, u32[]{:S(2)}, u32[]{:S(2)}) collective-permute-start(bf16[4,64,128]{2,1,0:T(8,128)(2,1)S(1)} %pad_maximum_fusion.1), channel_id=1, source_target_pairs={{0,24},{4,28},{8,16},{12,20},{16,8},{20,12},{24,0},{28,4},{1,25},{... | collective-permute-start | bytes 196616 | tf_op jit(solution)/shard_map/ppermute | solution.py:370
  28.0 7.9 %collective-permute-start.7 = (f32[8,256,128]{2,1,0:T(8,128)}, f32[8,256,128]{2,1,0:T(8,128)S(1)}, u32[]{:S(2)}, u32[]{:S(2)}) collective-permute-start(f32[8,256,128]{2,1,0:T(8,128)} %get-tuple-element.39.refs_0_), channel_id=1, source_target_pairs={{0,4},{4,0},{8,12},{12,8},{16,20},{20,16},{24,28},{28,24},{1,5},{5... | collective-permute-start | bytes 3145736 | tf_op jit(solution)/shard_map/ppermute | solution.py:370
  28.0 7.9 %collective-permute-start.8 = (f32[8,256,128]{2,1,0:T(8,128)}, f32[8,256,128]{2,1,0:T(8,128)S(1)}, u32[]{:S(2)}, u32[]{:S(2)}) collective-permute-start(f32[8,256,128]{2,1,0:T(8,128)} %get-tuple-element.36), channel_id=1, source_target_pairs={{0,4},{4,0},{8,12},{12,8},{16,20},{20,16},{24,28},{28,24},{1,5},{5... | collective-permute-start | bytes 3145736 | tf_op jit(solution)/shard_map/ppermute | solution.py:370
  34.3 1.6 %collective-permute-start.6 = (bf16[16,64,128]{2,1,0:T(8,128)(2,1)S(1)}, bf16[16,64,128]{2,1,0:T(8,128)(2,1)S(1)}, u32[]{:S(2)}, u32[]{:S(2)}) collective-permute-start(bf16[16,64,128]{2,1,0:T(8,128)(2,1)S(1)} %pad_maximum_fusion), channel_id=1, source_target_pairs={{0,4},{4,0},{8,12},{12,8},{16,20},{20,16},{24,28},{28,24},{1,5},{5... | collective-permute-start | bytes 786440 | tf_op jit(solution)/shard_map/ppermute | solution.py:370
  35.9 7.2 %copy-start.4 = (bf16[32,64,128]{2,1,0:T(8,128)(2,1)}, bf16[32,64,128]{2,1,0:T(8,128)(2,1)S(1)}, u32[]{:S(2)}) copy-start(bf16[32,64,128]{2,1,0:T(8,128)(2,1)S(1)} %constant_dynamic-update-slice_fusion.w_ref) | copy-start | bytes 1572868
  35.9 1.1 %copy-start.5 = (f32[8,256,128]{2,1,0:T(8,128)}, f32[8,256,128]{2,1,0:T(8,128)S(1)}, u32[]{:S(2)}) copy-start(f32[8,256,128]{2,1,0:T(8,128)S(1)} %collective-permute-done.7.refs_3_) | copy-start | bytes 3145732
  43.1 4.5 %copy-start.9 = (bf16[4,256,128]{2,1,0:T(8,128)(2,1)S(1)}, bf16[4,256,128]{2,1,0:T(8,128)(2,1)}, u32[]{:S(2)}) copy-start(bf16[4,256,128]{2,1,0:T(8,128)(2,1)} %get-tuple-element.44) | copy-start | bytes 786436
  43.1 5.7 %copy-start.8 = (bf16[4,256,128]{2,1,0:T(8,128)(2,1)S(1)}, bf16[4,256,128]{2,1,0:T(8,128)(2,1)}, u32[]{:S(2)}) copy-start(bf16[4,256,128]{2,1,0:T(8,128)(2,1)} %get-tuple-element.45) | copy-start | bytes 786436
  43.1 7.1 %copy-start.7 = (bf16[4,256,128]{2,1,0:T(8,128)(2,1)S(1)}, bf16[4,256,128]{2,1,0:T(8,128)(2,1)}, u32[]{:S(2)}) copy-start(bf16[4,256,128]{2,1,0:T(8,128)(2,1)} %get-tuple-element.46) | copy-start | bytes 786436
  43.1 13.3 %copy-start.1 = (bf16[1,256,128]{2,1,0:T(8,128)(2,1)S(1)}, bf16[1,256,128]{2,1,0:T(8,128)(2,1)}, u32[]{:S(2)}) copy-start(bf16[1,256,128]{2,1,0:T(8,128)(2,1)} %param.8) | copy-start | bytes 196612
  47.6 14.0 %collective-permute-start.9 = (bf16[4,256,128]{2,1,0:T(8,128)(2,1)S(1)}, bf16[4,256,128]{2,1,0:T(8,128)(2,1)S(1)}, u32[]{:S(2)}, u32[]{:S(2)}) collective-permute-start(bf16[4,256,128]{2,1,0:T(8,128)(2,1)S(1)} %copy-done.9), channel_id=1, source_target_pairs={{0,8},{4,12},{8,0},{12,4},{16,24},{20,28},{24,16},{28,20},{1,9},{5... | collective-permute-start | bytes 786440 | tf_op jit(solution)/shard_map/ppermute | solution.py:370
  48.8 16.8 %collective-permute-start.10 = (bf16[4,256,128]{2,1,0:T(8,128)(2,1)S(1)}, bf16[4,256,128]{2,1,0:T(8,128)(2,1)S(1)}, u32[]{:S(2)}, u32[]{:S(2)}) collective-permute-start(bf16[4,256,128]{2,1,0:T(8,128)(2,1)S(1)} %copy-done.8), channel_id=1, source_target_pairs={{0,16},{4,20},{8,24},{12,28},{16,0},{20,4},{24,8},{28,12},{1,17},{... | collective-permute-start | bytes 786440 | tf_op jit(solution)/shard_map/ppermute | solution.py:370
  50.2 15.3 %collective-permute-start.11 = (bf16[4,256,128]{2,1,0:T(8,128)(2,1)S(1)}, bf16[4,256,128]{2,1,0:T(8,128)(2,1)S(1)}, u32[]{:S(2)}, u32[]{:S(2)}) collective-permute-start(bf16[4,256,128]{2,1,0:T(8,128)(2,1)S(1)} %copy-done.7), channel_id=1, source_target_pairs={{0,24},{4,28},{8,16},{12,20},{16,8},{20,12},{24,0},{28,4},{1,25},{... | collective-permute-start | bytes 786440 | tf_op jit(solution)/shard_map/ppermute | solution.py:370
  51.2 21.7 %all-to-all-start.1 = ((bf16[32,64,128]{2,1,0:T(8,128)(2,1)}), bf16[32,64,128]{2,1,0:T(8,128)(2,1)S(1)}, u32[]{:S(2)}, u32[]{:S(2)}) async-start(bf16[32,64,128]{2,1,0:T(8,128)(2,1)} %narrow_dpool.1), calls=%async_computation.1 | async-start | bytes 1048576 | tf_op jit(solution)/shard_map/all_to_all | solution.py:411
  56.4 9.2 %copy-start.2 = (f32[4,256,128]{2,1,0:T(8,128)S(1)}, f32[4,256,128]{2,1,0:T(8,128)}, u32[]{:S(2)}) copy-start(f32[4,256,128]{2,1,0:T(8,128)} %get-tuple-element.43.refs_0_.kept_ref) | copy-start | bytes 1572868
  66.7 12.3 %collective-permute-start.12 = (bf16[1,256,128]{2,1,0:T(8,128)(2,1)S(1)}, bf16[1,256,128]{2,1,0:T(8,128)(2,1)S(1)}, u32[]{:S(2)}, u32[]{:S(2)}) collective-permute-start(bf16[1,256,128]{2,1,0:T(8,128)(2,1)S(1)} %get-tuple-element.49), channel_id=1, source_target_pairs={{0,1},{1,0},{2,3},{3,2},{4,5},{5,4},{6,7},{7,6},{8,9},{9,8},{10,11... | collective-permute-start | bytes 196616 | tf_op jit(solution)/shard_map/ppermute | solution.py:370
  68.2 10.8 %collective-permute-start.13 = (bf16[1,256,128]{2,1,0:T(8,128)(2,1)S(1)}, bf16[1,256,128]{2,1,0:T(8,128)(2,1)S(1)}, u32[]{:S(2)}, u32[]{:S(2)}) collective-permute-start(bf16[1,256,128]{2,1,0:T(8,128)(2,1)S(1)} %get-tuple-element.50), channel_id=1, source_target_pairs={{0,2},{1,3},{2,0},{3,1},{4,6},{5,7},{6,4},{7,5},{8,10},{9,11},{10,... | collective-permute-start | bytes 196616 | tf_op jit(solution)/shard_map/ppermute | solution.py:370
  72.4 6.6 %collective-permute-start.14 = (bf16[1,256,128]{2,1,0:T(8,128)(2,1)S(1)}, bf16[1,256,128]{2,1,0:T(8,128)(2,1)S(1)}, u32[]{:S(2)}, u32[]{:S(2)}) collective-permute-start(bf16[1,256,128]{2,1,0:T(8,128)(2,1)S(1)} %get-tuple-element.51), channel_id=1, source_target_pairs={{0,3},{1,2},{2,1},{3,0},{4,7},{5,6},{6,5},{7,4},{8,11},{9,10},{10,... | collective-permute-start | bytes 196616 | tf_op jit(solution)/shard_map/ppermute | solution.py:370
  (3 other events, 2.9 us)

commit v4 on v2

--- a/solution.py
+++ b/solution.py
@@ -225,7 +225,7 @@
                 pltpu.SemaphoreType.DMA((blocks,)),
             ],
         ),
-        compiler_params=params(1),
+        compiler_params=params(1, 50),
         cost_estimate=cost(4e9 if others else 1e7),
         name="partial_proj",
     )(index, *operands, *others)

time: 79.8 us -> 77.7 us (0.974)
  waiting for transfers between devices: 6.06 us -> 8.16 us
  Pallas kernels: 35.5 us -> 33.8 us
  local copies, waits for them, and re-layouts: 4.73 us -> 3.47 us
    ppermute x15, waiting for transfers between devices: 6.06 us -> 8.15 us  [swap(): return lax.ppermute(x, axis, [(d, d ^ bits) for d in range(size)])]
    pallas_call x2, Pallas kernels: 8.74 us -> 7.22 us  [partial_proj(): pl.pallas_call(functools.partial(partial_kernel, first, blocks, size, len...]
    unnamed x24 -> x20, local copies, waits for them, and re-layouts: 3.97 us -> 2.72 us
  transfers between devices with their start and end apart: 17 -> 17, of which waited for: 3 -> 3; matrix products, arithmetic and copies ran while one was open for 1% -> 0% of each run, Pallas kernels for 45% -> 44%
where the time goes in v4:
time: 77.7 us; the launch traced here: 77 us
  Pallas kernels  33.8 us (44%)
  starting transfers between devices  30 us (39%)
  waiting for transfers between devices  8.16 us (11%)
  local copies, waits for them, and re-layouts  3.47 us (4%)
  between operations  0.89 us (1%)
    ppermute x15, starting transfers between devices, swap(): return lax.ppermute(x, axis, [(d, d ^ bits) for d in range(size)])  19 us
    ppermute x15, waiting for transfers between devices, swap(): return lax.ppermute(x, axis, [(d, d ^ bits) for d in range(size)])  8.15 us
    pallas_call x2, Pallas kernels, partial_proj(): pl.pallas_call(functools.partial(partial_kernel, first, blocks, size, len...  7.22 us
    pallas_call x1, Pallas kernels, permute(): pl.pallas_call(functools.partial(permute_kernel, slots, pieces), out_shap...  6.34 us
    all_to_all x1, starting transfers between devices, local(): g3_got = lax.all_to_all(g3, AXES, split_axis=0, concat_axis=0, tiled=True)  6.07 us
    pallas_call x1, Pallas kernels, narrow_sum(): pl.pallas_call(narrow_sum_kernel, out_shape=jax.ShapeDtypeStruct((ROWS, W...  5.39 us
    pallas_call x1, Pallas kernels, wide_sum(): pl.pallas_call(wide_kernel, out_shape=jax.ShapeDtypeStruct((ROWS, WSUM),...  5.28 us
    pallas_call x1, Pallas kernels, count_hits(): pl.pallas_call(count_kernel, out_shape=jax.ShapeDtypeStruct((tables, ROWS...  4.93 us
  transfers between devices with their start and end apart: 17, of which 3 were waited for; matrix products, arithmetic and copies ran while one was open for 0% of the time, Pallas kernels for 44%

profile of v4, /device:TPU:0, one launch (start us, length us, event | category | flops | bytes accessed | tf_op | source)
XLA Modules:
  0.0 77.0 jit_solution(4358341850807051830)
XLA Ops:
  0.6 0.7 slice.3
  1.4 5.0 %collective-permute-start.2 = (bf16[1,64,128]{2,1,0:T(8,128)(2,1)S(1)}, bf16[1,64,128]{2,1,0:T(8,128)(2,1)S(1)}, u32[]{:S(2)}, u32[]{:S(2)}) collective-permute-start(bf16[1,64,128]{2,1,0:T(8,128)(2,1)S(1)} %slice.3), channel_id=1, source_target_pairs={{0,3},{1,2},{2,1},{3,0},{4,7},{5,6},{6,5},{7,4},{8,11},{9,10},{10,... | collective-permute-start | bytes 49160 | tf_op jit(solution)/shard_map/ppermute | solution.py:387
  7.0 6.3 %permute_groups.1 = (bf16[32,128,256]{2,1,0:T(8,128)(2,1)}, bf16[32,128,128]{2,1,0:T(8,128)(2,1)}, bf16[32,128,256]{2,1,0:T(8,128)(2,1)}) custom-call(s32[32]{0:T(128)} %assign_ref.1, bf16[128,32,384]{2,1,0:T(8,128)(2,1)} %grad_ref.1, bf16[128,32,256]{2,1,0:T(8,128)(2,1)} %pool_ref.1), custom_call_target="tpu_custom_call" | custom-call | flops 10000000 | bytes 1024 | tf_op jit(solution)/shard_map/permute_groups/pallas_call | solution.py:78
  13.4 6.1 %all-to-all-start = ((bf16[32,128,128]{2,1,0:T(8,128)(2,1)}), bf16[32,128,128]{2,1,0:T(8,128)(2,1)S(1)}, u32[]{:S(2)}, u32[]{:S(2)}) async-start(bf16[32,128,128]{2,1,0:T(8,128)(2,1)} %get-tuple-element.34.refs_2_), calls=%async_computation | async-start | bytes 2097152 | tf_op jit(solution)/shard_map/all_to_all | solution.py:415
  19.5 3.4 %partial_proj.2 = (f32[8,256,128]{2,1,0:T(8,128)}, f32[8,256,128]{2,1,0:T(8,128)S(1)}) custom-call(s32[44]{0:T(128)S(1)} %fusion.9.index_ref, bf16[32,128,256]{2,1,0:T(8,128)(2,1)} %get-tuple-element.33.refs_0_, bf16[32,128,256]{2,1,0:T(8,128)(2,1)} %get-tuple-element.30.refs_1_.g_ref, bf16[32,128,128]{2,1,0:T(8,128)(2,1)S(1)} %copy-done), custom_call_target="tpu_custom_call" | custom-call | flops 10000000 | bytes 1024 | tf_op jit(solution)/shard_map/partial_proj/pallas_call | solution.py:211
  22.9 1.8 %collective-permute-start.3 = (bf16[4,64,128]{2,1,0:T(8,128)(2,1)S(1)}, bf16[4,64,128]{2,1,0:T(8,128)(2,1)S(1)}, u32[]{:S(2)}, u32[]{:S(2)}) collective-permute-start(bf16[4,64,128]{2,1,0:T(8,128)(2,1)S(1)} %pad_maximum_fusion.1), channel_id=1, source_target_pairs={{0,8},{4,12},{8,0},{12,4},{16,24},{20,28},{24,16},{28,20},{1,9},{5... | collective-permute-start | bytes 196616 | tf_op jit(solution)/shard_map/ppermute | solution.py:387
  24.7 1.5 %collective-permute-start.4 = (bf16[4,64,128]{2,1,0:T(8,128)(2,1)S(1)}, bf16[4,64,128]{2,1,0:T(8,128)(2,1)S(1)}, u32[]{:S(2)}, u32[]{:S(2)}) collective-permute-start(bf16[4,64,128]{2,1,0:T(8,128)(2,1)S(1)} %pad_maximum_fusion.1), channel_id=1, source_target_pairs={{0,16},{4,20},{8,24},{12,28},{16,0},{20,4},{24,8},{28,12},{1,17},{... | collective-permute-start | bytes 196616 | tf_op jit(solution)/shard_map/ppermute | solution.py:387
  27.0 4.9 %count_hits.1.hits_ref = s32[3,64,4096]{2,1,0:T(8,128)} custom-call(s32[3,8,4096]{2,1,0:T(8,128)} %bitcast.10, s32[3,1,4096]{2,1,0:T(1,128)} %bitcast.11, f32[8,256,128]{2,1,0:T(8,128)} %get-tuple-element.39.refs_0_), custom_call_target="tpu_custom_call" | custom-call | flops 5000000000 | bytes 1024 | tf_op jit(solution)/shard_map/count_hits/pallas_call | solution.py:259
  31.9 2.2 %collective-permute-done.4 = bf16[4,64,128]{2,1,0:T(8,128)(2,1)S(1)} collective-permute-done((bf16[4,64,128]{2,1,0:T(8,128)(2,1)S(1)}, bf16[4,64,128]{2,1,0:T(8,128)(2,1)S(1)}, u32[]{:S(2)}, u32[]{:S(2)}) %collective-permute-start.4) | collective-permute-done | bytes 65568 | tf_op jit(solution)/shard_map/ppermute | solution.py:387
  34.4 1.4 %collective-permute-done.6 = bf16[16,64,128]{2,1,0:T(8,128)(2,1)S(1)} collective-permute-done((bf16[16,64,128]{2,1,0:T(8,128)(2,1)S(1)}, bf16[16,64,128]{2,1,0:T(8,128)(2,1)S(1)}, u32[]{:S(2)}, u32[]{:S(2)}) %collective-permute-start.6) | collective-permute-done | bytes 262176 | tf_op jit(solution)/shard_map/ppermute | solution.py:387
  35.8 3.9 %partial_proj.3 = (f32[4,256,128]{2,1,0:T(8,128)S(1)}, bf16[4,256,128]{2,1,0:T(8,128)(2,1)S(1)}, bf16[4,256,128]{2,1,0:T(8,128)(2,1)S(1)}, bf16[4,256,128]{2,1,0:T(8,128)(2,1)S(1)}) custom-call(s32[44]{0:T(128)S(1)} %fusion.9.index_ref, bf16[32,128,256]{2,1,0:T(8,128)(2,1)} %get-tuple-element.33.refs_0_, ...), custom_call_target="tpu_custom_call" | custom-call | flops 4000000000 | bytes 1024 | tf_op jit(solution)/shard_map/partial_proj/pallas_call | solution.py:211
  39.7 0.8 %copy-done.4 = f32[4,256,128]{2,1,0:T(8,128)} copy-done((f32[4,256,128]{2,1,0:T(8,128)}, f32[4,256,128]{2,1,0:T(8,128)S(1)}, u32[]{:S(2)}) %copy-start.4) | copy-done | bytes 524312
  40.5 4.5 %narrow_dpool.1 = bf16[32,64,128]{2,1,0:T(8,128)(2,1)} custom-call(s32[44]{0:T(128)} %copy-done.3, bf16[32,128,256]{2,1,0:T(8,128)(2,1)} %get-tuple-element.30.refs_1_.g_ref, bf16[32,64,128]{2,1,0:T(8,128)(2,1)} %copy-done.7, f32[4,256,128]{2,1,0:T(8,128)} %copy-done.4), custom_call_target="tpu_custom_call" | custom-call | flops 4000000000 | bytes 1024 | tf_op jit(solution)/shard_map/narrow_dpool/pallas_call | solution.py:139
  45.0 1.0 %collective-permute-start.9 = (bf16[4,256,128]{2,1,0:T(8,128)(2,1)S(1)}, bf16[4,256,128]{2,1,0:T(8,128)(2,1)S(1)}, u32[]{:S(2)}, u32[]{:S(2)}) collective-permute-start(bf16[4,256,128]{2,1,0:T(8,128)(2,1)S(1)} %get-tuple-element.44), channel_id=1, source_target_pairs={{0,8},{4,12},{8,0},{12,4},{16,24},{20,28},{24,16},{28,20},{1,9},{5... | collective-permute-start | bytes 786440 | tf_op jit(solution)/shard_map/ppermute | solution.py:387
  46.0 1.5 %collective-permute-start.10 = (bf16[4,256,128]{2,1,0:T(8,128)(2,1)S(1)}, bf16[4,256,128]{2,1,0:T(8,128)(2,1)S(1)}, u32[]{:S(2)}, u32[]{:S(2)}) collective-permute-start(bf16[4,256,128]{2,1,0:T(8,128)(2,1)S(1)} %get-tuple-element.45), channel_id=1, source_target_pairs={{0,16},{4,20},{8,24},{12,28},{16,0},{20,4},{24,8},{28,12},{1,17},{... | collective-permute-start | bytes 786440 | tf_op jit(solution)/shard_map/ppermute | solution.py:387
  47.5 1.1 %collective-permute-start.11 = (bf16[4,256,128]{2,1,0:T(8,128)(2,1)S(1)}, bf16[4,256,128]{2,1,0:T(8,128)(2,1)S(1)}, u32[]{:S(2)}, u32[]{:S(2)}) collective-permute-start(bf16[4,256,128]{2,1,0:T(8,128)(2,1)S(1)} %get-tuple-element.46), channel_id=1, source_target_pairs={{0,24},{4,28},{8,16},{12,20},{16,8},{20,12},{24,0},{28,4},{1,25},{... | collective-permute-start | bytes 786440 | tf_op jit(solution)/shard_map/ppermute | solution.py:387
  48.5 4.9 %all-to-all-start.1 = ((bf16[32,64,128]{2,1,0:T(8,128)(2,1)}), bf16[32,64,128]{2,1,0:T(8,128)(2,1)S(1)}, u32[]{:S(2)}, u32[]{:S(2)}) async-start(bf16[32,64,128]{2,1,0:T(8,128)(2,1)} %narrow_dpool.1), calls=%async_computation.1 | async-start | bytes 1048576 | tf_op jit(solution)/shard_map/all_to_all | solution.py:428
  53.5 5.3 %wide_sum.1.refs_3_.wide_ref = f32[512,256]{1,0:T(8,128)} custom-call(s32[3,64,4096]{2,1,0:T(8,128)} %count_hits.1.hits_ref, bf16[4096,128]{1,0:T(8,128)(2,1)S(1)} %bitcast.7, bf16[256,128]{1,0:T(8,128)(2,1)S(1)} %bitcast.9), custom_call_target="tpu_custom_call" | custom-call | flops 10000000 | bytes 1024 | tf_op jit(solution)/shard_map/wide_sum/pallas_call | solution.py:297
  58.8 4.6 %collective-permute-done.10.refs_1_ = bf16[4,256,128]{2,1,0:T(8,128)(2,1)S(1)} collective-permute-done((bf16[4,256,128]{2,1,0:T(8,128)(2,1)S(1)}, bf16[4,256,128]{2,1,0:T(8,128)(2,1)S(1)}, u32[]{:S(2)}, u32[]{:S(2)}) %collective-permute-start.10) | collective-permute-done | bytes 262176 | tf_op jit(solution)/shard_map/ppermute | solution.py:387
  63.4 1.0 %copy-done.1 = f32[512,256]{1,0:T(8,128)S(1)} copy-done((f32[512,256]{1,0:T(8,128)S(1)}, f32[512,256]{1,0:T(8,128)}, u32[]{:S(2)}) %copy-start.1) | copy-done | bytes 524312
  64.5 1.1 %collective-permute-start.12 = (bf16[1,256,128]{2,1,0:T(8,128)(2,1)S(1)}, bf16[1,256,128]{2,1,0:T(8,128)(2,1)S(1)}, u32[]{:S(2)}, u32[]{:S(2)}) collective-permute-start(bf16[1,256,128]{2,1,0:T(8,128)(2,1)S(1)} %get-tuple-element.49), channel_id=1, source_target_pairs={{0,1},{1,0},{2,3},{3,2},{4,5},{5,4},{6,7},{7,6},{8,9},{9,8},{10,11... | collective-permute-start | bytes 196616 | tf_op jit(solution)/shard_map/ppermute | solution.py:387
  65.6 4.5 %collective-permute-start.13 = (bf16[1,256,128]{2,1,0:T(8,128)(2,1)S(1)}, bf16[1,256,128]{2,1,0:T(8,128)(2,1)S(1)}, u32[]{:S(2)}, u32[]{:S(2)}) collective-permute-start(bf16[1,256,128]{2,1,0:T(8,128)(2,1)S(1)} %get-tuple-element.50), channel_id=1, source_target_pairs={{0,2},{1,3},{2,0},{3,1},{4,6},{5,7},{6,4},{7,5},{8,10},{9,11},{10,... | collective-permute-start | bytes 196616 | tf_op jit(solution)/shard_map/ppermute | solution.py:387
  70.1 0.8 %copy-done.6 = bf16[32,64,128]{2,1,0:T(8,128)(2,1)} copy-done((bf16[32,64,128]{2,1,0:T(8,128)(2,1)}, bf16[32,64,128]{2,1,0:T(8,128)(2,1)S(1)}, u32[]{:S(2)}) %copy-start.6) | copy-done | bytes 524312
  70.9 5.4 %narrow_sum.1 = f32[512,256]{1,0:T(8,128)} custom-call(s32[3,64,4096]{2,1,0:T(8,128)} %count_hits.1.hits_ref, bf16[32,64,128]{2,1,0:T(8,128)(2,1)} %copy-done.6, f32[512,256]{1,0:T(8,128)} %wide_sum.1.refs_3_.wide_ref), custom_call_target="tpu_custom_call", output_to_operand_aliasing={{}: (2, {})} | custom-call | flops 10000000 | bytes 1024 | tf_op jit(solution)/shard_map/narrow_sum/pallas_call | solution.py:341
  (44 shorter events, 2.5 us)
Async XLA Ops:
  1.4 12.0 %collective-permute-start.2 = (bf16[1,64,128]{2,1,0:T(8,128)(2,1)S(1)}, bf16[1,64,128]{2,1,0:T(8,128)(2,1)S(1)}, u32[]{:S(2)}, u32[]{:S(2)}) collective-permute-start(bf16[1,64,128]{2,1,0:T(8,128)(2,1)S(1)} %slice.3), channel_id=1, source_target_pairs={{0,3},{1,2},{2,1},{3,0},{4,7},{5,6},{6,5},{7,4},{8,11},{9,10},{10,... | collective-permute-start | bytes 49160 | tf_op jit(solution)/shard_map/ppermute | solution.py:387
  6.4 6.9 %collective-permute-start.1 = (bf16[1,64,128]{2,1,0:T(8,128)(2,1)S(1)}, bf16[1,64,128]{2,1,0:T(8,128)(2,1)S(1)}, u32[]{:S(2)}, u32[]{:S(2)}) collective-permute-start(bf16[1,64,128]{2,1,0:T(8,128)(2,1)S(1)} %slice.3), channel_id=1, source_target_pairs={{0,2},{1,3},{2,0},{3,1},{4,6},{5,7},{6,4},{7,5},{8,10},{9,11},{10,... | collective-permute-start | bytes 49160 | tf_op jit(solution)/shard_map/ppermute | solution.py:387
  6.4 6.9 %collective-permute-start = (bf16[1,64,128]{2,1,0:T(8,128)(2,1)S(1)}, bf16[1,64,128]{2,1,0:T(8,128)(2,1)S(1)}, u32[]{:S(2)}, u32[]{:S(2)}) collective-permute-start(bf16[1,64,128]{2,1,0:T(8,128)(2,1)S(1)} %slice.3), channel_id=1, source_target_pairs={{0,1},{1,0},{2,3},{3,2},{4,5},{5,4},{6,7},{7,6},{8,9},{9,8},{10,11... | collective-permute-start | bytes 49160 | tf_op jit(solution)/shard_map/ppermute | solution.py:387
  13.3 6.2 %copy-start = (bf16[32,128,128]{2,1,0:T(8,128)(2,1)S(1)}, bf16[32,128,128]{2,1,0:T(8,128)(2,1)}, u32[]{:S(2)}) copy-start(bf16[32,128,128]{2,1,0:T(8,128)(2,1)} %get-tuple-element.34.refs_2_) | copy-start | bytes 3145732
  13.4 31.6 %all-to-all-start = ((bf16[32,128,128]{2,1,0:T(8,128)(2,1)}), bf16[32,128,128]{2,1,0:T(8,128)(2,1)S(1)}, u32[]{:S(2)}, u32[]{:S(2)}) async-start(bf16[32,128,128]{2,1,0:T(8,128)(2,1)} %get-tuple-element.34.refs_2_), calls=%async_computation | async-start | bytes 2097152 | tf_op jit(solution)/shard_map/all_to_all | solution.py:415
  19.5 16.3 %copy-start.3 = (s32[44]{0:T(128)}, s32[44]{0:T(128)S(1)}, u32[]{:S(2)}) copy-start(s32[44]{0:T(128)S(1)} %fusion.9.index_ref) | copy-start | bytes 532
  22.9 9.0 %collective-permute-start.3 = (bf16[4,64,128]{2,1,0:T(8,128)(2,1)S(1)}, bf16[4,64,128]{2,1,0:T(8,128)(2,1)S(1)}, u32[]{:S(2)}, u32[]{:S(2)}) collective-permute-start(bf16[4,64,128]{2,1,0:T(8,128)(2,1)S(1)} %pad_maximum_fusion.1), channel_id=1, source_target_pairs={{0,8},{4,12},{8,0},{12,4},{16,24},{20,28},{24,16},{28,20},{1,9},{5... | collective-permute-start | bytes 196616 | tf_op jit(solution)/shard_map/ppermute | solution.py:387
  24.7 9.3 %collective-permute-start.4 = (bf16[4,64,128]{2,1,0:T(8,128)(2,1)S(1)}, bf16[4,64,128]{2,1,0:T(8,128)(2,1)S(1)}, u32[]{:S(2)}, u32[]{:S(2)}) collective-permute-start(bf16[4,64,128]{2,1,0:T(8,128)(2,1)S(1)} %pad_maximum_fusion.1), channel_id=1, source_target_pairs={{0,16},{4,20},{8,24},{12,28},{16,0},{20,4},{24,8},{28,12},{1,17},{... | collective-permute-start | bytes 196616 | tf_op jit(solution)/shard_map/ppermute | solution.py:387
  26.2 7.9 %collective-permute-start.5 = (bf16[4,64,128]{2,1,0:T(8,128)(2,1)S(1)}, bf16[4,64,128]{2,1,0:T(8,128)(2,1)S(1)}, u32[]{:S(2)}, u32[]{:S(2)}) collective-permute-start(bf16[4,64,128]{2,1,0:T(8,128)(2,1)S(1)} %pad_maximum_fusion.1), channel_id=1, source_target_pairs={{0,24},{4,28},{8,16},{12,20},{16,8},{20,12},{24,0},{28,4},{1,25},{... | collective-permute-start | bytes 196616 | tf_op jit(solution)/shard_map/ppermute | solution.py:387
  26.5 9.3 %collective-permute-start.7 = (f32[8,256,128]{2,1,0:T(8,128)}, f32[8,256,128]{2,1,0:T(8,128)}, u32[]{:S(2)}, u32[]{:S(2)}) collective-permute-start(f32[8,256,128]{2,1,0:T(8,128)} %get-tuple-element.39.refs_0_), channel_id=1, source_target_pairs={{0,4},{4,0},{8,12},{12,8},{16,20},{20,16},{24,28},{28,24},{1,5},{5... | collective-permute-start | bytes 3145736 | tf_op jit(solution)/shard_map/ppermute | solution.py:387
  26.5 9.3 %collective-permute-start.8 = (f32[8,256,128]{2,1,0:T(8,128)S(1)}, f32[8,256,128]{2,1,0:T(8,128)}, u32[]{:S(2)}, u32[]{:S(2)}) collective-permute-start(f32[8,256,128]{2,1,0:T(8,128)S(1)} %get-tuple-element.36), channel_id=1, source_target_pairs={{0,4},{4,0},{8,12},{12,8},{16,20},{20,16},{24,28},{28,24},{1,5},{5... | collective-permute-start | bytes 3145736 | tf_op jit(solution)/shard_map/ppermute | solution.py:387
  34.1 1.6 %collective-permute-start.6 = (bf16[16,64,128]{2,1,0:T(8,128)(2,1)S(1)}, bf16[16,64,128]{2,1,0:T(8,128)(2,1)S(1)}, u32[]{:S(2)}, u32[]{:S(2)}) collective-permute-start(bf16[16,64,128]{2,1,0:T(8,128)(2,1)S(1)} %pad_maximum_fusion), channel_id=1, source_target_pairs={{0,4},{4,0},{8,12},{12,8},{16,20},{20,16},{24,28},{28,24},{1,5},{5... | collective-permute-start | bytes 786440 | tf_op jit(solution)/shard_map/ppermute | solution.py:387
  35.8 3.9 %copy-start.7 = (bf16[32,64,128]{2,1,0:T(8,128)(2,1)}, bf16[32,64,128]{2,1,0:T(8,128)(2,1)S(1)}, u32[]{:S(2)}) copy-start(bf16[32,64,128]{2,1,0:T(8,128)(2,1)S(1)} %constant_dynamic-update-slice_fusion.w_ref) | copy-start | bytes 1572868
  40.5 13.0 %copy-start.2 = (bf16[1,256,128]{2,1,0:T(8,128)(2,1)S(1)}, bf16[1,256,128]{2,1,0:T(8,128)(2,1)}, u32[]{:S(2)}) copy-start(bf16[1,256,128]{2,1,0:T(8,128)(2,1)} %param.8) | copy-start | bytes 196612
  45.0 13.8 %collective-permute-start.9 = (bf16[4,256,128]{2,1,0:T(8,128)(2,1)S(1)}, bf16[4,256,128]{2,1,0:T(8,128)(2,1)S(1)}, u32[]{:S(2)}, u32[]{:S(2)}) collective-permute-start(bf16[4,256,128]{2,1,0:T(8,128)(2,1)S(1)} %get-tuple-element.44), channel_id=1, source_target_pairs={{0,8},{4,12},{8,0},{12,4},{16,24},{20,28},{24,16},{28,20},{1,9},{5... | collective-permute-start | bytes 786440 | tf_op jit(solution)/shard_map/ppermute | solution.py:387
  46.0 17.4 %collective-permute-start.10 = (bf16[4,256,128]{2,1,0:T(8,128)(2,1)S(1)}, bf16[4,256,128]{2,1,0:T(8,128)(2,1)S(1)}, u32[]{:S(2)}, u32[]{:S(2)}) collective-permute-start(bf16[4,256,128]{2,1,0:T(8,128)(2,1)S(1)} %get-tuple-element.45), channel_id=1, source_target_pairs={{0,16},{4,20},{8,24},{12,28},{16,0},{20,4},{24,8},{28,12},{1,17},{... | collective-permute-start | bytes 786440 | tf_op jit(solution)/shard_map/ppermute | solution.py:387
  47.5 15.9 %collective-permute-start.11 = (bf16[4,256,128]{2,1,0:T(8,128)(2,1)S(1)}, bf16[4,256,128]{2,1,0:T(8,128)(2,1)S(1)}, u32[]{:S(2)}, u32[]{:S(2)}) collective-permute-start(bf16[4,256,128]{2,1,0:T(8,128)(2,1)S(1)} %get-tuple-element.46), channel_id=1, source_target_pairs={{0,24},{4,28},{8,16},{12,20},{16,8},{20,12},{24,0},{28,4},{1,25},{... | collective-permute-start | bytes 786440 | tf_op jit(solution)/shard_map/ppermute | solution.py:387
  48.5 21.6 %all-to-all-start.1 = ((bf16[32,64,128]{2,1,0:T(8,128)(2,1)}), bf16[32,64,128]{2,1,0:T(8,128)(2,1)S(1)}, u32[]{:S(2)}, u32[]{:S(2)}) async-start(bf16[32,64,128]{2,1,0:T(8,128)(2,1)} %narrow_dpool.1), calls=%async_computation.1 | async-start | bytes 1048576 | tf_op jit(solution)/shard_map/all_to_all | solution.py:428
  53.5 9.9 %copy-start.5 = (f32[4,256,128]{2,1,0:T(8,128)S(1)}, f32[4,256,128]{2,1,0:T(8,128)}, u32[]{:S(2)}) copy-start(f32[4,256,128]{2,1,0:T(8,128)} %copy-done.4) | copy-start | bytes 1572868
  63.4 1.0 %copy-start.1 = (f32[512,256]{1,0:T(8,128)S(1)}, f32[512,256]{1,0:T(8,128)}, u32[]{:S(2)}) copy-start(f32[512,256]{1,0:T(8,128)} %wide_sum.1.refs_3_.wide_ref) | copy-start | bytes 1572868
  64.5 11.8 %collective-permute-start.12 = (bf16[1,256,128]{2,1,0:T(8,128)(2,1)S(1)}, bf16[1,256,128]{2,1,0:T(8,128)(2,1)S(1)}, u32[]{:S(2)}, u32[]{:S(2)}) collective-permute-start(bf16[1,256,128]{2,1,0:T(8,128)(2,1)S(1)} %get-tuple-element.49), channel_id=1, source_target_pairs={{0,1},{1,0},{2,3},{3,2},{4,5},{5,4},{6,7},{7,6},{8,9},{9,8},{10,11... | collective-permute-start | bytes 196616 | tf_op jit(solution)/shard_map/ppermute | solution.py:387
  65.6 10.8 %collective-permute-start.13 = (bf16[1,256,128]{2,1,0:T(8,128)(2,1)S(1)}, bf16[1,256,128]{2,1,0:T(8,128)(2,1)S(1)}, u32[]{:S(2)}, u32[]{:S(2)}) collective-permute-start(bf16[1,256,128]{2,1,0:T(8,128)(2,1)S(1)} %get-tuple-element.50), channel_id=1, source_target_pairs={{0,2},{1,3},{2,0},{3,1},{4,6},{5,7},{6,4},{7,5},{8,10},{9,11},{10,... | collective-permute-start | bytes 196616 | tf_op jit(solution)/shard_map/ppermute | solution.py:387
  70.1 6.2 %collective-permute-start.14 = (bf16[1,256,128]{2,1,0:T(8,128)(2,1)S(1)}, bf16[1,256,128]{2,1,0:T(8,128)(2,1)S(1)}, u32[]{:S(2)}, u32[]{:S(2)}) collective-permute-start(bf16[1,256,128]{2,1,0:T(8,128)(2,1)S(1)} %get-tuple-element.51), channel_id=1, source_target_pairs={{0,3},{1,2},{2,1},{3,0},{4,7},{5,6},{6,5},{7,4},{8,11},{9,10},{10,... | collective-permute-start | bytes 196616 | tf_op jit(solution)/shard_map/ppermute | solution.py:387
  70.1 0.8 %copy-start.6 = (bf16[32,64,128]{2,1,0:T(8,128)(2,1)}, bf16[32,64,128]{2,1,0:T(8,128)(2,1)S(1)}, u32[]{:S(2)}) copy-start(bf16[32,64,128]{2,1,0:T(8,128)(2,1)S(1)} %all-to-all-done.1.d_ref) | copy-start | bytes 1572868
  (1 other events, 0.8 us)

commit v5 on v4

--- a/solution.py
+++ b/solution.py
@@ -153,7 +153,7 @@
                 pltpu.SemaphoreType.DMA((blocks,)),
             ],
         ),
-        compiler_params=params(1),
+        compiler_params=params(1, 50),
         cost_estimate=cost(4e9),
         name="narrow_dpool",
     )(index, g12, w12, *after)
@@ -350,7 +350,7 @@
         + [ANY] * len(after),
         out_specs=pl.BlockSpec((ROWS, PD), lambda i: (0, 0)),
         input_output_aliases={2: 0},
-        compiler_params=params(1),
+        compiler_params=params(1, 54),
         cost_estimate=cost(1e7),
         name="narrow_sum",
     )(hits, narrow, wide, *after)

time: 77.7 us -> 76.1 us (0.979)
  waiting for transfers between devices: 8.16 us -> 11.4 us
  local copies, waits for them, and re-layouts: 3.47 us -> 1.86 us
  Pallas kernels: 33.8 us -> 32.2 us
  starting transfers between devices: 30 us -> 28.5 us
    all_to_all x1, waiting for transfers between devices: 0.01 us -> 1.92 us  [local(): g3_got = lax.all_to_all(g3, AXES, split_axis=0, concat_axis=0, tiled=True)]
    unnamed x20 -> x12, local copies, waits for them, and re-layouts: 2.72 us -> 1.1 us
    pallas_call x1, Pallas kernels: 4.48 us -> 2.91 us  [narrow_dpool(): pl.pallas_call(functools.partial(narrow_kernel, first, blocks), out_shape...]
    ppermute x15, waiting for transfers between devices: 8.15 us -> 9.46 us  [swap(): return lax.ppermute(x, axis, [(d, d ^ bits) for d in range(size)])]
    ppermute x15, starting transfers between devices: 19 us -> 17.8 us  [swap(): return lax.ppermute(x, axis, [(d, d ^ bits) for d in range(size)])]
  transfers between devices with their start and end apart: 17 -> 17, of which waited for: 3 -> 4; matrix products, arithmetic and copies ran while one was open for 0% -> 0% of each run, Pallas kernels for 44% -> 43%
where the time goes in v5:
time: 76.1 us; the launch traced here: 75.5 us
  Pallas kernels  32.2 us (42%)
  starting transfers between devices  28.5 us (37%)
  waiting for transfers between devices  11.4 us (15%)
  local copies, waits for them, and re-layouts  1.86 us (2%)
  between operations  0.85 us (1%)
    ppermute x15, starting transfers between devices, swap(): return lax.ppermute(x, axis, [(d, d ^ bits) for d in range(size)])  17.8 us
    ppermute x15, waiting for transfers between devices, swap(): return lax.ppermute(x, axis, [(d, d ^ bits) for d in range(size)])  9.46 us
    pallas_call x2, Pallas kernels, partial_proj(): pl.pallas_call(functools.partial(partial_kernel, first, blocks, size, len...  7.22 us
    pallas_call x1, Pallas kernels, permute(): pl.pallas_call(functools.partial(permute_kernel, slots, pieces), out_shap...  6.38 us
    all_to_all x1, starting transfers between devices, local(): g3_got = lax.all_to_all(g3, AXES, split_axis=0, concat_axis=0, tiled=True)  6.07 us
    pallas_call x1, Pallas kernels, narrow_sum(): pl.pallas_call(narrow_sum_kernel, out_shape=jax.ShapeDtypeStruct((ROWS, W...  5.39 us
    pallas_call x1, Pallas kernels, wide_sum(): pl.pallas_call(wide_kernel, out_shape=jax.ShapeDtypeStruct((ROWS, WSUM),...  5.23 us
    pallas_call x1, Pallas kernels, count_hits(): pl.pallas_call(count_kernel, out_shape=jax.ShapeDtypeStruct((tables, ROWS...  4.94 us
  transfers between devices with their start and end apart: 17, of which 4 were waited for; matrix products, arithmetic and copies ran while one was open for 0% of the time, Pallas kernels for 43%

profile of v5, /device:TPU:0, one launch (start us, length us, event | category | flops | bytes accessed | tf_op | source)
XLA Modules:
  0.0 75.5 jit_solution(14389598676383100132)
XLA Ops:
  0.6 0.7 slice.3
  1.4 5.0 %collective-permute-start.2 = (bf16[1,64,128]{2,1,0:T(8,128)(2,1)S(1)}, bf16[1,64,128]{2,1,0:T(8,128)(2,1)S(1)}, u32[]{:S(2)}, u32[]{:S(2)}) collective-permute-start(bf16[1,64,128]{2,1,0:T(8,128)(2,1)S(1)} %slice.3), channel_id=1, source_target_pairs={{0,3},{1,2},{2,1},{3,0},{4,7},{5,6},{6,5},{7,4},{8,11},{9,10},{10,... | collective-permute-start | bytes 49160 | tf_op jit(solution)/shard_map/ppermute | solution.py:387
  7.0 6.4 %permute_groups.1 = (bf16[32,128,256]{2,1,0:T(8,128)(2,1)}, bf16[32,128,128]{2,1,0:T(8,128)(2,1)}, bf16[32,128,256]{2,1,0:T(8,128)(2,1)}) custom-call(s32[32]{0:T(128)} %assign_ref.1, bf16[128,32,384]{2,1,0:T(8,128)(2,1)} %grad_ref.1, bf16[128,32,256]{2,1,0:T(8,128)(2,1)} %pool_ref.1), custom_call_target="tpu_custom_call" | custom-call | flops 10000000 | bytes 1024 | tf_op jit(solution)/shard_map/permute_groups/pallas_call | solution.py:78
  13.4 6.1 %all-to-all-start = ((bf16[32,128,128]{2,1,0:T(8,128)(2,1)}), bf16[32,128,128]{2,1,0:T(8,128)(2,1)S(1)}, u32[]{:S(2)}, u32[]{:S(2)}) async-start(bf16[32,128,128]{2,1,0:T(8,128)(2,1)} %get-tuple-element.34.refs_2_), calls=%async_computation | async-start | bytes 2097152 | tf_op jit(solution)/shard_map/all_to_all | solution.py:415
  19.6 3.4 %partial_proj.2 = (f32[8,256,128]{2,1,0:T(8,128)}, f32[8,256,128]{2,1,0:T(8,128)S(1)}) custom-call(s32[44]{0:T(128)S(1)} %fusion.9.index_ref, bf16[32,128,256]{2,1,0:T(8,128)(2,1)} %get-tuple-element.33.refs_0_, bf16[32,128,256]{2,1,0:T(8,128)(2,1)} %get-tuple-element.30.refs_1_.g_ref, bf16[32,128,128]{2,1,0:T(8,128)(2,1)S(1)} %copy-done), custom_call_target="tpu_custom_call" | custom-call | flops 10000000 | bytes 1024 | tf_op jit(solution)/shard_map/partial_proj/pallas_call | solution.py:211
  22.9 1.8 %collective-permute-start.3 = (bf16[4,64,128]{2,1,0:T(8,128)(2,1)S(1)}, bf16[4,64,128]{2,1,0:T(8,128)(2,1)S(1)}, u32[]{:S(2)}, u32[]{:S(2)}) collective-permute-start(bf16[4,64,128]{2,1,0:T(8,128)(2,1)S(1)} %pad_maximum_fusion.1), channel_id=1, source_target_pairs={{0,8},{4,12},{8,0},{12,4},{16,24},{20,28},{24,16},{28,20},{1,9},{5... | collective-permute-start | bytes 196616 | tf_op jit(solution)/shard_map/ppermute | solution.py:387
  24.8 1.5 %collective-permute-start.4 = (bf16[4,64,128]{2,1,0:T(8,128)(2,1)S(1)}, bf16[4,64,128]{2,1,0:T(8,128)(2,1)S(1)}, u32[]{:S(2)}, u32[]{:S(2)}) collective-permute-start(bf16[4,64,128]{2,1,0:T(8,128)(2,1)S(1)} %pad_maximum_fusion.1), channel_id=1, source_target_pairs={{0,16},{4,20},{8,24},{12,28},{16,0},{20,4},{24,8},{28,12},{1,17},{... | collective-permute-start | bytes 196616 | tf_op jit(solution)/shard_map/ppermute | solution.py:387
  27.0 4.9 %count_hits.1.hits_ref = s32[3,64,4096]{2,1,0:T(8,128)} custom-call(s32[3,8,4096]{2,1,0:T(8,128)} %bitcast.10, s32[3,1,4096]{2,1,0:T(1,128)} %bitcast.11, f32[8,256,128]{2,1,0:T(8,128)} %get-tuple-element.39.refs_0_), custom_call_target="tpu_custom_call" | custom-call | flops 5000000000 | bytes 1024 | tf_op jit(solution)/shard_map/count_hits/pallas_call | solution.py:259
  31.9 2.2 %collective-permute-done.4 = bf16[4,64,128]{2,1,0:T(8,128)(2,1)S(1)} collective-permute-done((bf16[4,64,128]{2,1,0:T(8,128)(2,1)S(1)}, bf16[4,64,128]{2,1,0:T(8,128)(2,1)S(1)}, u32[]{:S(2)}, u32[]{:S(2)}) %collective-permute-start.4) | collective-permute-done | bytes 65568 | tf_op jit(solution)/shard_map/ppermute | solution.py:387
  34.4 1.4 %collective-permute-done.6 = bf16[16,64,128]{2,1,0:T(8,128)(2,1)S(1)} collective-permute-done((bf16[16,64,128]{2,1,0:T(8,128)(2,1)S(1)}, bf16[16,64,128]{2,1,0:T(8,128)(2,1)S(1)}, u32[]{:S(2)}, u32[]{:S(2)}) %collective-permute-start.6) | collective-permute-done | bytes 262176 | tf_op jit(solution)/shard_map/ppermute | solution.py:387
  35.8 3.9 %partial_proj.3 = (f32[4,256,128]{2,1,0:T(8,128)S(1)}, bf16[4,256,128]{2,1,0:T(8,128)(2,1)S(1)}, bf16[4,256,128]{2,1,0:T(8,128)(2,1)S(1)}, bf16[4,256,128]{2,1,0:T(8,128)(2,1)S(1)}) custom-call(s32[44]{0:T(128)S(1)} %fusion.9.index_ref, bf16[32,128,256]{2,1,0:T(8,128)(2,1)} %get-tuple-element.33.refs_0_, ...), custom_call_target="tpu_custom_call" | custom-call | flops 4000000000 | bytes 1024 | tf_op jit(solution)/shard_map/partial_proj/pallas_call | solution.py:211
  39.7 2.9 %narrow_dpool.1 = bf16[32,64,128]{2,1,0:T(8,128)(2,1)} custom-call(s32[44]{0:T(128)S(1)} %fusion.9.index_ref, bf16[32,128,256]{2,1,0:T(8,128)(2,1)S(1)} %copy-done.2, bf16[32,64,128]{2,1,0:T(8,128)(2,1)S(1)} %constant_dynamic-update-slice_fusion.w_ref, f32[4,256,128]{2,1,0:T(8,128)S(1)} %get-tuple-element.43.refs_0_.kept_ref), custom_call_target="tpu_custom_call" | custom-call | flops 4000000000 | bytes 1024 | tf_op jit(solution)/shard_map/narrow_dpool/pallas_call | solution.py:139
  42.6 1.9 %all-to-all-done = bf16[32,128,128]{2,1,0:T(8,128)(2,1)S(1)} async-done(((bf16[32,128,128]{2,1,0:T(8,128)(2,1)}), bf16[32,128,128]{2,1,0:T(8,128)(2,1)S(1)}, u32[]{:S(2)}, u32[]{:S(2)}) %all-to-all-start) | async-done | bytes 1048608 | tf_op jit(solution)/shard_map/all_to_all | solution.py:415
  44.6 1.5 %collective-permute-start.9 = (bf16[4,256,128]{2,1,0:T(8,128)(2,1)S(1)}, bf16[4,256,128]{2,1,0:T(8,128)(2,1)S(1)}, u32[]{:S(2)}, u32[]{:S(2)}) collective-permute-start(bf16[4,256,128]{2,1,0:T(8,128)(2,1)S(1)} %get-tuple-element.44), channel_id=1, source_target_pairs={{0,8},{4,12},{8,0},{12,4},{16,24},{20,28},{24,16},{28,20},{1,9},{5... | collective-permute-start | bytes 786440 | tf_op jit(solution)/shard_map/ppermute | solution.py:387
  46.0 1.5 %collective-permute-start.10 = (bf16[4,256,128]{2,1,0:T(8,128)(2,1)S(1)}, bf16[4,256,128]{2,1,0:T(8,128)(2,1)S(1)}, u32[]{:S(2)}, u32[]{:S(2)}) collective-permute-start(bf16[4,256,128]{2,1,0:T(8,128)(2,1)S(1)} %get-tuple-element.45), channel_id=1, source_target_pairs={{0,16},{4,20},{8,24},{12,28},{16,0},{20,4},{24,8},{28,12},{1,17},{... | collective-permute-start | bytes 786440 | tf_op jit(solution)/shard_map/ppermute | solution.py:387
  48.0 4.6 %all-to-all-start.1 = ((bf16[32,64,128]{2,1,0:T(8,128)(2,1)}), bf16[32,64,128]{2,1,0:T(8,128)(2,1)}, u32[]{:S(2)}, u32[]{:S(2)}) async-start(bf16[32,64,128]{2,1,0:T(8,128)(2,1)} %narrow_dpool.1), calls=%async_computation.1 | async-start | bytes 1048576 | tf_op jit(solution)/shard_map/all_to_all | solution.py:428
  52.6 5.2 %wide_sum.1.refs_3_.wide_ref = f32[512,256]{1,0:T(8,128)} custom-call(s32[3,64,4096]{2,1,0:T(8,128)} %count_hits.1.hits_ref, bf16[4096,128]{1,0:T(8,128)(2,1)S(1)} %bitcast.7, bf16[256,128]{1,0:T(8,128)(2,1)S(1)} %bitcast.9), custom_call_target="tpu_custom_call" | custom-call | flops 10000000 | bytes 1024 | tf_op jit(solution)/shard_map/wide_sum/pallas_call | solution.py:297
  57.9 5.9 %collective-permute-done.10.refs_1_ = bf16[4,256,128]{2,1,0:T(8,128)(2,1)S(1)} collective-permute-done((bf16[4,256,128]{2,1,0:T(8,128)(2,1)S(1)}, bf16[4,256,128]{2,1,0:T(8,128)(2,1)S(1)}, u32[]{:S(2)}, u32[]{:S(2)}) %collective-permute-start.10) | collective-permute-done | bytes 262176 | tf_op jit(solution)/shard_map/ppermute | solution.py:387
  63.8 1.0 %copy-done.1 = f32[512,256]{1,0:T(8,128)S(1)} copy-done((f32[512,256]{1,0:T(8,128)S(1)}, f32[512,256]{1,0:T(8,128)}, u32[]{:S(2)}) %copy-start.1) | copy-done | bytes 524312
  64.9 1.5 %collective-permute-start.12 = (bf16[1,256,128]{2,1,0:T(8,128)(2,1)S(1)}, bf16[1,256,128]{2,1,0:T(8,128)(2,1)S(1)}, u32[]{:S(2)}, u32[]{:S(2)}) collective-permute-start(bf16[1,256,128]{2,1,0:T(8,128)(2,1)S(1)} %get-tuple-element.49), channel_id=1, source_target_pairs={{0,1},{1,0},{2,3},{3,2},{4,5},{5,4},{6,7},{7,6},{8,9},{9,8},{10,11... | collective-permute-start | bytes 196616 | tf_op jit(solution)/shard_map/ppermute | solution.py:387
  66.5 1.3 %collective-permute-start.13 = (bf16[1,256,128]{2,1,0:T(8,128)(2,1)S(1)}, bf16[1,256,128]{2,1,0:T(8,128)(2,1)S(1)}, u32[]{:S(2)}, u32[]{:S(2)}) collective-permute-start(bf16[1,256,128]{2,1,0:T(8,128)(2,1)S(1)} %get-tuple-element.50), channel_id=1, source_target_pairs={{0,2},{1,3},{2,0},{3,1},{4,6},{5,7},{6,4},{7,5},{8,10},{9,11},{10,... | collective-permute-start | bytes 196616 | tf_op jit(solution)/shard_map/ppermute | solution.py:387
  67.8 1.6 %collective-permute-start.14 = (bf16[1,256,128]{2,1,0:T(8,128)(2,1)S(1)}, bf16[1,256,128]{2,1,0:T(8,128)(2,1)S(1)}, u32[]{:S(2)}, u32[]{:S(2)}) collective-permute-start(bf16[1,256,128]{2,1,0:T(8,128)(2,1)S(1)} %get-tuple-element.51), channel_id=1, source_target_pairs={{0,3},{1,2},{2,1},{3,0},{4,7},{5,6},{6,5},{7,4},{8,11},{9,10},{10,... | collective-permute-start | bytes 196616 | tf_op jit(solution)/shard_map/ppermute | solution.py:387
  69.4 5.4 %narrow_sum.1 = f32[512,256]{1,0:T(8,128)} custom-call(s32[3,64,4096]{2,1,0:T(8,128)} %count_hits.1.hits_ref, bf16[32,64,128]{2,1,0:T(8,128)(2,1)} %all-to-all-done.1.d_ref, f32[512,256]{1,0:T(8,128)} %wide_sum.1.refs_3_.wide_ref), custom_call_target="tpu_custom_call", output_to_operand_aliasing={{}: (2, {})} | custom-call | flops 10000000 | bytes 1024 | tf_op jit(solution)/shard_map/narrow_sum/pallas_call | solution.py:341
  74.8 0.7 add_multiply_fusion
  (36 shorter events, 2.4 us)
Async XLA Ops:
  1.4 12.0 %collective-permute-start.2 = (bf16[1,64,128]{2,1,0:T(8,128)(2,1)S(1)}, bf16[1,64,128]{2,1,0:T(8,128)(2,1)S(1)}, u32[]{:S(2)}, u32[]{:S(2)}) collective-permute-start(bf16[1,64,128]{2,1,0:T(8,128)(2,1)S(1)} %slice.3), channel_id=1, source_target_pairs={{0,3},{1,2},{2,1},{3,0},{4,7},{5,6},{6,5},{7,4},{8,11},{9,10},{10,... | collective-permute-start | bytes 49160 | tf_op jit(solution)/shard_map/ppermute | solution.py:387
  6.4 7.0 %collective-permute-start.1 = (bf16[1,64,128]{2,1,0:T(8,128)(2,1)S(1)}, bf16[1,64,128]{2,1,0:T(8,128)(2,1)S(1)}, u32[]{:S(2)}, u32[]{:S(2)}) collective-permute-start(bf16[1,64,128]{2,1,0:T(8,128)(2,1)S(1)} %slice.3), channel_id=1, source_target_pairs={{0,2},{1,3},{2,0},{3,1},{4,6},{5,7},{6,4},{7,5},{8,10},{9,11},{10,... | collective-permute-start | bytes 49160 | tf_op jit(solution)/shard_map/ppermute | solution.py:387
  6.4 7.0 %collective-permute-start = (bf16[1,64,128]{2,1,0:T(8,128)(2,1)S(1)}, bf16[1,64,128]{2,1,0:T(8,128)(2,1)S(1)}, u32[]{:S(2)}, u32[]{:S(2)}) collective-permute-start(bf16[1,64,128]{2,1,0:T(8,128)(2,1)S(1)} %slice.3), channel_id=1, source_target_pairs={{0,1},{1,0},{2,3},{3,2},{4,5},{5,4},{6,7},{7,6},{8,9},{9,8},{10,11... | collective-permute-start | bytes 49160 | tf_op jit(solution)/shard_map/ppermute | solution.py:387
  13.4 6.2 %copy-start = (bf16[32,128,128]{2,1,0:T(8,128)(2,1)S(1)}, bf16[32,128,128]{2,1,0:T(8,128)(2,1)}, u32[]{:S(2)}) copy-start(bf16[32,128,128]{2,1,0:T(8,128)(2,1)} %get-tuple-element.34.refs_2_) | copy-start | bytes 3145732
  13.4 31.1 %all-to-all-start = ((bf16[32,128,128]{2,1,0:T(8,128)(2,1)}), bf16[32,128,128]{2,1,0:T(8,128)(2,1)S(1)}, u32[]{:S(2)}, u32[]{:S(2)}) async-start(bf16[32,128,128]{2,1,0:T(8,128)(2,1)} %get-tuple-element.34.refs_2_), calls=%async_computation | async-start | bytes 2097152 | tf_op jit(solution)/shard_map/all_to_all | solution.py:415
  22.9 9.0 %collective-permute-start.3 = (bf16[4,64,128]{2,1,0:T(8,128)(2,1)S(1)}, bf16[4,64,128]{2,1,0:T(8,128)(2,1)S(1)}, u32[]{:S(2)}, u32[]{:S(2)}) collective-permute-start(bf16[4,64,128]{2,1,0:T(8,128)(2,1)S(1)} %pad_maximum_fusion.1), channel_id=1, source_target_pairs={{0,8},{4,12},{8,0},{12,4},{16,24},{20,28},{24,16},{28,20},{1,9},{5... | collective-permute-start | bytes 196616 | tf_op jit(solution)/shard_map/ppermute | solution.py:387
  24.8 9.4 %collective-permute-start.4 = (bf16[4,64,128]{2,1,0:T(8,128)(2,1)S(1)}, bf16[4,64,128]{2,1,0:T(8,128)(2,1)S(1)}, u32[]{:S(2)}, u32[]{:S(2)}) collective-permute-start(bf16[4,64,128]{2,1,0:T(8,128)(2,1)S(1)} %pad_maximum_fusion.1), channel_id=1, source_target_pairs={{0,16},{4,20},{8,24},{12,28},{16,0},{20,4},{24,8},{28,12},{1,17},{... | collective-permute-start | bytes 196616 | tf_op jit(solution)/shard_map/ppermute | solution.py:387
  26.2 7.9 %collective-permute-start.5 = (bf16[4,64,128]{2,1,0:T(8,128)(2,1)S(1)}, bf16[4,64,128]{2,1,0:T(8,128)(2,1)S(1)}, u32[]{:S(2)}, u32[]{:S(2)}) collective-permute-start(bf16[4,64,128]{2,1,0:T(8,128)(2,1)S(1)} %pad_maximum_fusion.1), channel_id=1, source_target_pairs={{0,24},{4,28},{8,16},{12,20},{16,8},{20,12},{24,0},{28,4},{1,25},{... | collective-permute-start | bytes 196616 | tf_op jit(solution)/shard_map/ppermute | solution.py:387
  26.5 9.3 %collective-permute-start.7 = (f32[8,256,128]{2,1,0:T(8,128)}, f32[8,256,128]{2,1,0:T(8,128)}, u32[]{:S(2)}, u32[]{:S(2)}) collective-permute-start(f32[8,256,128]{2,1,0:T(8,128)} %get-tuple-element.39.refs_0_), channel_id=1, source_target_pairs={{0,4},{4,0},{8,12},{12,8},{16,20},{20,16},{24,28},{28,24},{1,5},{5... | collective-permute-start | bytes 3145736 | tf_op jit(solution)/shard_map/ppermute | solution.py:387
  26.5 9.3 %collective-permute-start.8 = (f32[8,256,128]{2,1,0:T(8,128)S(1)}, f32[8,256,128]{2,1,0:T(8,128)}, u32[]{:S(2)}, u32[]{:S(2)}) collective-permute-start(f32[8,256,128]{2,1,0:T(8,128)S(1)} %get-tuple-element.36), channel_id=1, source_target_pairs={{0,4},{4,0},{8,12},{12,8},{16,20},{20,16},{24,28},{28,24},{1,5},{5... | collective-permute-start | bytes 3145736 | tf_op jit(solution)/shard_map/ppermute | solution.py:387
  34.2 1.6 %collective-permute-start.6 = (bf16[16,64,128]{2,1,0:T(8,128)(2,1)S(1)}, bf16[16,64,128]{2,1,0:T(8,128)(2,1)S(1)}, u32[]{:S(2)}, u32[]{:S(2)}) collective-permute-start(bf16[16,64,128]{2,1,0:T(8,128)(2,1)S(1)} %pad_maximum_fusion), channel_id=1, source_target_pairs={{0,4},{4,0},{8,12},{12,8},{16,20},{20,16},{24,28},{28,24},{1,5},{5... | collective-permute-start | bytes 786440 | tf_op jit(solution)/shard_map/ppermute | solution.py:387
  35.8 3.9 %copy-start.2 = (bf16[32,128,256]{2,1,0:T(8,128)(2,1)S(1)}, bf16[32,128,256]{2,1,0:T(8,128)(2,1)}, u32[]{:S(2)}) copy-start(bf16[32,128,256]{2,1,0:T(8,128)(2,1)} %get-tuple-element.30.refs_1_.g_ref) | copy-start | bytes 6291460
  39.7 12.9 %copy-start.3 = (bf16[1,256,128]{2,1,0:T(8,128)(2,1)S(1)}, bf16[1,256,128]{2,1,0:T(8,128)(2,1)}, u32[]{:S(2)}) copy-start(bf16[1,256,128]{2,1,0:T(8,128)(2,1)} %param.8) | copy-start | bytes 196612
  44.6 13.3 %collective-permute-start.9 = (bf16[4,256,128]{2,1,0:T(8,128)(2,1)S(1)}, bf16[4,256,128]{2,1,0:T(8,128)(2,1)S(1)}, u32[]{:S(2)}, u32[]{:S(2)}) collective-permute-start(bf16[4,256,128]{2,1,0:T(8,128)(2,1)S(1)} %get-tuple-element.44), channel_id=1, source_target_pairs={{0,8},{4,12},{8,0},{12,4},{16,24},{20,28},{24,16},{28,20},{1,9},{5... | collective-permute-start | bytes 786440 | tf_op jit(solution)/shard_map/ppermute | solution.py:387
  46.0 17.7 %collective-permute-start.10 = (bf16[4,256,128]{2,1,0:T(8,128)(2,1)S(1)}, bf16[4,256,128]{2,1,0:T(8,128)(2,1)S(1)}, u32[]{:S(2)}, u32[]{:S(2)}) collective-permute-start(bf16[4,256,128]{2,1,0:T(8,128)(2,1)S(1)} %get-tuple-element.45), channel_id=1, source_target_pairs={{0,16},{4,20},{8,24},{12,28},{16,0},{20,4},{24,8},{28,12},{1,17},{... | collective-permute-start | bytes 786440 | tf_op jit(solution)/shard_map/ppermute | solution.py:387
  47.5 16.3 %collective-permute-start.11 = (bf16[4,256,128]{2,1,0:T(8,128)(2,1)S(1)}, bf16[4,256,128]{2,1,0:T(8,128)(2,1)S(1)}, u32[]{:S(2)}, u32[]{:S(2)}) collective-permute-start(bf16[4,256,128]{2,1,0:T(8,128)(2,1)S(1)} %get-tuple-element.46), channel_id=1, source_target_pairs={{0,24},{4,28},{8,16},{12,20},{16,8},{20,12},{24,0},{28,4},{1,25},{... | collective-permute-start | bytes 786440 | tf_op jit(solution)/shard_map/ppermute | solution.py:387
  48.0 21.3 %all-to-all-start.1 = ((bf16[32,64,128]{2,1,0:T(8,128)(2,1)}), bf16[32,64,128]{2,1,0:T(8,128)(2,1)}, u32[]{:S(2)}, u32[]{:S(2)}) async-start(bf16[32,64,128]{2,1,0:T(8,128)(2,1)} %narrow_dpool.1), calls=%async_computation.1 | async-start | bytes 1048576 | tf_op jit(solution)/shard_map/all_to_all | solution.py:428
  63.8 1.0 %copy-start.1 = (f32[512,256]{1,0:T(8,128)S(1)}, f32[512,256]{1,0:T(8,128)}, u32[]{:S(2)}) copy-start(f32[512,256]{1,0:T(8,128)} %wide_sum.1.refs_3_.wide_ref) | copy-start | bytes 1572868
  64.9 9.8 %collective-permute-start.12 = (bf16[1,256,128]{2,1,0:T(8,128)(2,1)S(1)}, bf16[1,256,128]{2,1,0:T(8,128)(2,1)S(1)}, u32[]{:S(2)}, u32[]{:S(2)}) collective-permute-start(bf16[1,256,128]{2,1,0:T(8,128)(2,1)S(1)} %get-tuple-element.49), channel_id=1, source_target_pairs={{0,1},{1,0},{2,3},{3,2},{4,5},{5,4},{6,7},{7,6},{8,9},{9,8},{10,11... | collective-permute-start | bytes 196616 | tf_op jit(solution)/shard_map/ppermute | solution.py:387
  66.5 8.3 %collective-permute-start.13 = (bf16[1,256,128]{2,1,0:T(8,128)(2,1)S(1)}, bf16[1,256,128]{2,1,0:T(8,128)(2,1)S(1)}, u32[]{:S(2)}, u32[]{:S(2)}) collective-permute-start(bf16[1,256,128]{2,1,0:T(8,128)(2,1)S(1)} %get-tuple-element.50), channel_id=1, source_target_pairs={{0,2},{1,3},{2,0},{3,1},{4,6},{5,7},{6,4},{7,5},{8,10},{9,11},{10,... | collective-permute-start | bytes 196616 | tf_op jit(solution)/shard_map/ppermute | solution.py:387
  67.8 7.0 %collective-permute-start.14 = (bf16[1,256,128]{2,1,0:T(8,128)(2,1)S(1)}, bf16[1,256,128]{2,1,0:T(8,128)(2,1)S(1)}, u32[]{:S(2)}, u32[]{:S(2)}) collective-permute-start(bf16[1,256,128]{2,1,0:T(8,128)(2,1)S(1)} %get-tuple-element.51), channel_id=1, source_target_pairs={{0,3},{1,2},{2,1},{3,0},{4,7},{5,6},{6,5},{7,4},{8,11},{9,10},{10,... | collective-permute-start | bytes 196616 | tf_op jit(solution)/shard_map/ppermute | solution.py:387

commit v6 on v5

--- a/solution.py
+++ b/solution.py
@@ -424,7 +424,7 @@
     rows = jnp.concatenate([rows, swap(rows, "node", n_node, 1)])
     narrow = narrow_dpool(index, n_local + 2 * n_plane, g12, rows, after=kept[:1])
 
-    narrow, hits, g3_got, kept = lax.optimization_barrier((narrow, hits, g3_got, kept))
+    narrow, hits, g3_got, _ = lax.optimization_barrier((narrow, hits, g3_got, kept))
     narrow_got = lax.all_to_all(narrow, AXES, split_axis=0, concat_axis=0, tiled=True)
     wide = wide_sum(hits, g3_got.reshape(-1, PD), proj[0])
     arrived = [swap(kept[d], "node", n_node, 2 * d) for d in range(1, n_plane)]

time: 76.1 us -> 75.3 us (0.989)
  the two profiles are of different devices: /device:TPU:0 before, /device:TPU:1 now
where the time goes in v6:
time: 75.3 us; the launch traced here: 74.7 us
  Pallas kernels  32.2 us (43%)
  starting transfers between devices  27.2 us (36%)
  waiting for transfers between devices  11.9 us (16%)
  local copies, waits for them, and re-layouts  1.85 us (2%)
  between operations  0.84 us (1%)
  other arithmetic  0.76 us (1%)
    ppermute x15, starting transfers between devices, swap(): return lax.ppermute(x, axis, [(d, d ^ bits) for d in range(size)])  15 us
    all_to_all x1, waiting for transfers between devices, local(): lax.all_to_all(narrow, AXES, split_axis=0, concat_axis=0, tiled=True)  7.72 us
    pallas_call x2, Pallas kernels, partial_proj(): pl.pallas_call(functools.partial(partial_kernel, first, blocks, size, len...  7.22 us
    all_to_all x1, starting transfers between devices, local(): g3_got = lax.all_to_all(g3, AXES, split_axis=0, concat_axis=0, tiled=True)  7.06 us
    pallas_call x1, Pallas kernels, permute(): pl.pallas_call(functools.partial(permute_kernel, slots, pieces), out_shap...  6.39 us
    pallas_call x1, Pallas kernels, narrow_sum(): pl.pallas_call(narrow_sum_kernel, out_shape=jax.ShapeDtypeStruct((ROWS, W...  5.39 us
    pallas_call x1, Pallas kernels, wide_sum(): pl.pallas_call(wide_kernel, out_shape=jax.ShapeDtypeStruct((ROWS, WSUM),...  5.23 us
    all_to_all x1, starting transfers between devices, local(): lax.all_to_all(narrow, AXES, split_axis=0, concat_axis=0, tiled=True)  5.07 us
  transfers between devices with their start and end apart: 17, of which 5 were waited for; matrix products, arithmetic and copies ran while one was open for 0% of the time, Pallas kernels for 43%

profile of v6, /device:TPU:1, one launch (start us, length us, event | category | flops | bytes accessed | tf_op | source)
XLA Modules:
  0.0 74.7 jit_solution(1700884104862214884)
XLA Ops:
  0.6 0.7 slice.3
  1.4 2.1 %collective-permute-start = (bf16[1,64,128]{2,1,0:T(8,128)(2,1)S(1)}, bf16[1,64,128]{2,1,0:T(8,128)(2,1)S(1)}, u32[]{:S(2)}, u32[]{:S(2)}) collective-permute-start(bf16[1,64,128]{2,1,0:T(8,128)(2,1)S(1)} %slice.3), channel_id=1, source_target_pairs={{0,1},{1,0},{2,3},{3,2},{4,5},{5,4},{6,7},{7,6},{8,9},{9,8},{10,11... | collective-permute-start | bytes 49160 | tf_op jit(solution)/shard_map/ppermute | solution.py:387
  3.5 2.3 %collective-permute-start.1 = (bf16[1,64,128]{2,1,0:T(8,128)(2,1)S(1)}, bf16[1,64,128]{2,1,0:T(8,128)(2,1)S(1)}, u32[]{:S(2)}, u32[]{:S(2)}) collective-permute-start(bf16[1,64,128]{2,1,0:T(8,128)(2,1)S(1)} %slice.3), channel_id=1, source_target_pairs={{0,2},{1,3},{2,0},{3,1},{4,6},{5,7},{6,4},{7,5},{8,10},{9,11},{10,... | collective-permute-start | bytes 49160 | tf_op jit(solution)/shard_map/ppermute | solution.py:387
  5.8 6.4 %permute_groups.1 = (bf16[32,128,256]{2,1,0:T(8,128)(2,1)}, bf16[32,128,128]{2,1,0:T(8,128)(2,1)}, bf16[32,128,256]{2,1,0:T(8,128)(2,1)}) custom-call(s32[32]{0:T(128)} %assign_ref.1, bf16[128,32,384]{2,1,0:T(8,128)(2,1)} %grad_ref.1, bf16[128,32,256]{2,1,0:T(8,128)(2,1)} %pool_ref.1), custom_call_target="tpu_custom_call" | custom-call | flops 10000000 | bytes 1024 | tf_op jit(solution)/shard_map/permute_groups/pallas_call | solution.py:78
  12.2 7.1 %all-to-all-start = ((bf16[32,128,128]{2,1,0:T(8,128)(2,1)}), bf16[32,128,128]{2,1,0:T(8,128)(2,1)S(1)}, u32[]{:S(2)}, u32[]{:S(2)}) async-start(bf16[32,128,128]{2,1,0:T(8,128)(2,1)} %get-tuple-element.29.refs_2_), calls=%async_computation | async-start | bytes 2097152 | tf_op jit(solution)/shard_map/all_to_all | solution.py:415
  19.4 3.4 %partial_proj.2 = (f32[8,256,128]{2,1,0:T(8,128)}, f32[8,256,128]{2,1,0:T(8,128)S(1)}) custom-call(s32[44]{0:T(128)S(1)} %fusion.9.index_ref, bf16[32,128,256]{2,1,0:T(8,128)(2,1)} %get-tuple-element.26.refs_0_, bf16[32,128,256]{2,1,0:T(8,128)(2,1)} %get-tuple-element.27.refs_1_.g_ref, bf16[32,128,128]{2,1,0:T(8,128)(2,1)S(1)} %copy-done), custom_call_target="tpu_custom_call" | custom-call | flops 10000000 | bytes 1024 | tf_op jit(solution)/shard_map/partial_proj/pallas_call | solution.py:211
  22.7 2.4 %collective-permute-start.10 = (bf16[4,64,128]{2,1,0:T(8,128)(2,1)S(1)}, bf16[4,64,128]{2,1,0:T(8,128)(2,1)S(1)}, u32[]{:S(2)}, u32[]{:S(2)}) collective-permute-start(bf16[4,64,128]{2,1,0:T(8,128)(2,1)S(1)} %pad_maximum_fusion.1), channel_id=1, source_target_pairs={{0,24},{4,28},{8,16},{12,20},{16,8},{20,12},{24,0},{28,4},{1,25},{... | collective-permute-start | bytes 196616 | tf_op jit(solution)/shard_map/ppermute | solution.py:387
  25.5 1.1 %collective-permute-start.3 = (f32[8,256,128]{2,1,0:T(8,128)}, f32[8,256,128]{2,1,0:T(8,128)}, u32[]{:S(2)}, u32[]{:S(2)}) collective-permute-start(f32[8,256,128]{2,1,0:T(8,128)} %get-tuple-element.38.refs_0_), channel_id=1, source_target_pairs={{0,4},{4,0},{8,12},{12,8},{16,20},{20,16},{24,28},{28,24},{1,5},{5... | collective-permute-start | bytes 3145736 | tf_op jit(solution)/shard_map/ppermute | solution.py:387
  26.6 4.9 %count_hits.1.hits_ref = s32[3,64,4096]{2,1,0:T(8,128)} custom-call(s32[3,8,4096]{2,1,0:T(8,128)} %bitcast.10, s32[3,1,4096]{2,1,0:T(1,128)} %bitcast.11, f32[8,256,128]{2,1,0:T(8,128)} %get-tuple-element.38.refs_0_), custom_call_target="tpu_custom_call" | custom-call | flops 5000000000 | bytes 1024 | tf_op jit(solution)/shard_map/count_hits/pallas_call | solution.py:259
  32.2 1.6 %collective-permute-done.9 = bf16[4,64,128]{2,1,0:T(8,128)(2,1)S(1)} collective-permute-done((bf16[4,64,128]{2,1,0:T(8,128)(2,1)S(1)}, bf16[4,64,128]{2,1,0:T(8,128)(2,1)S(1)}, u32[]{:S(2)}, u32[]{:S(2)}) %collective-permute-start.9) | collective-permute-done | bytes 65568 | tf_op jit(solution)/shard_map/ppermute | solution.py:387
  34.3 1.1 %collective-permute-done.11 = bf16[16,64,128]{2,1,0:T(8,128)(2,1)S(1)} collective-permute-done((bf16[16,64,128]{2,1,0:T(8,128)(2,1)S(1)}, bf16[16,64,128]{2,1,0:T(8,128)(2,1)S(1)}, u32[]{:S(2)}, u32[]{:S(2)}) %collective-permute-start.11) | collective-permute-done | bytes 262176 | tf_op jit(solution)/shard_map/ppermute | solution.py:387
  35.5 3.9 %partial_proj.3 = (f32[4,256,128]{2,1,0:T(8,128)S(1)}, bf16[4,256,128]{2,1,0:T(8,128)(2,1)S(1)}, bf16[4,256,128]{2,1,0:T(8,128)(2,1)S(1)}, bf16[4,256,128]{2,1,0:T(8,128)(2,1)S(1)}) custom-call(s32[44]{0:T(128)S(1)} %fusion.9.index_ref, bf16[32,128,256]{2,1,0:T(8,128)(2,1)} %get-tuple-element.26.refs_0_, ...), custom_call_target="tpu_custom_call" | custom-call | flops 4000000000 | bytes 1024 | tf_op jit(solution)/shard_map/partial_proj/pallas_call | solution.py:211
  39.6 1.2 %collective-permute-start.6 = (bf16[4,256,128]{2,1,0:T(8,128)(2,1)S(1)}, bf16[4,256,128]{2,1,0:T(8,128)(2,1)S(1)}, u32[]{:S(2)}, u32[]{:S(2)}) collective-permute-start(bf16[4,256,128]{2,1,0:T(8,128)(2,1)S(1)} %get-tuple-element.34), channel_id=1, source_target_pairs={{0,16},{4,20},{8,24},{12,28},{16,0},{20,4},{24,8},{28,12},{1,17},{... | collective-permute-start | bytes 786440 | tf_op jit(solution)/shard_map/ppermute | solution.py:387
  40.8 1.3 %collective-permute-start.7 = (bf16[4,256,128]{2,1,0:T(8,128)(2,1)S(1)}, bf16[4,256,128]{2,1,0:T(8,128)(2,1)S(1)}, u32[]{:S(2)}, u32[]{:S(2)}) collective-permute-start(bf16[4,256,128]{2,1,0:T(8,128)(2,1)S(1)} %get-tuple-element.35), channel_id=1, source_target_pairs={{0,24},{4,28},{8,16},{12,20},{16,8},{20,12},{24,0},{28,4},{1,25},{... | collective-permute-start | bytes 786440 | tf_op jit(solution)/shard_map/ppermute | solution.py:387
  42.1 2.9 %narrow_dpool.1 = bf16[32,64,128]{2,1,0:T(8,128)(2,1)} custom-call(s32[44]{0:T(128)S(1)} %fusion.9.index_ref, bf16[32,128,256]{2,1,0:T(8,128)(2,1)S(1)} %copy-done.2, bf16[32,64,128]{2,1,0:T(8,128)(2,1)S(1)} %constant_dynamic-update-slice_fusion.w_ref, f32[4,256,128]{2,1,0:T(8,128)S(1)} %get-tuple-element.32.refs_0_.kept_ref), custom_call_target="tpu_custom_call" | custom-call | flops 4000000000 | bytes 1024 | tf_op jit(solution)/shard_map/narrow_dpool/pallas_call | solution.py:139
  45.0 0.7 all-to-all-done
  45.8 5.1 %all-to-all-start.1 = ((bf16[32,64,128]{2,1,0:T(8,128)(2,1)}), bf16[32,64,128]{2,1,0:T(8,128)(2,1)}, u32[]{:S(2)}, u32[]{:S(2)}) async-start(bf16[32,64,128]{2,1,0:T(8,128)(2,1)} %narrow_dpool.1), calls=%async_computation.1 | async-start | bytes 1048576 | tf_op jit(solution)/shard_map/all_to_all | solution.py:428
  50.9 5.2 %wide_sum.1.refs_3_.wide_ref = f32[512,256]{1,0:T(8,128)} custom-call(s32[3,64,4096]{2,1,0:T(8,128)} %count_hits.1.hits_ref, bf16[4096,128]{1,0:T(8,128)(2,1)S(1)} %bitcast.7, bf16[256,128]{1,0:T(8,128)(2,1)S(1)} %bitcast.9), custom_call_target="tpu_custom_call" | custom-call | flops 10000000 | bytes 1024 | tf_op jit(solution)/shard_map/wide_sum/pallas_call | solution.py:297
  56.1 1.0 %copy-done.1 = f32[512,256]{1,0:T(8,128)S(1)} copy-done((f32[512,256]{1,0:T(8,128)S(1)}, f32[512,256]{1,0:T(8,128)}, u32[]{:S(2)}) %copy-start.1) | copy-done | bytes 524312
  57.3 1.5 %collective-permute-start.12 = (bf16[1,256,128]{2,1,0:T(8,128)(2,1)S(1)}, bf16[1,256,128]{2,1,0:T(8,128)(2,1)S(1)}, u32[]{:S(2)}, u32[]{:S(2)}) collective-permute-start(bf16[1,256,128]{2,1,0:T(8,128)(2,1)S(1)} %get-tuple-element.41), channel_id=1, source_target_pairs={{0,1},{1,0},{2,3},{3,2},{4,5},{5,4},{6,7},{7,6},{8,9},{9,8},{10,11... | collective-permute-start | bytes 196616 | tf_op jit(solution)/shard_map/ppermute | solution.py:387
  58.7 2.1 %collective-permute-start.13 = (bf16[1,256,128]{2,1,0:T(8,128)(2,1)S(1)}, bf16[1,256,128]{2,1,0:T(8,128)(2,1)S(1)}, u32[]{:S(2)}, u32[]{:S(2)}) collective-permute-start(bf16[1,256,128]{2,1,0:T(8,128)(2,1)S(1)} %get-tuple-element.42), channel_id=1, source_target_pairs={{0,2},{1,3},{2,0},{3,1},{4,6},{5,7},{6,4},{7,5},{8,10},{9,11},{10,... | collective-permute-start | bytes 196616 | tf_op jit(solution)/shard_map/ppermute | solution.py:387
  60.9 7.7 %all-to-all-done.1.d_ref = bf16[32,64,128]{2,1,0:T(8,128)(2,1)} async-done(((bf16[32,64,128]{2,1,0:T(8,128)(2,1)}), bf16[32,64,128]{2,1,0:T(8,128)(2,1)}, u32[]{:S(2)}, u32[]{:S(2)}) %all-to-all-start.1) | async-done | bytes 524320 | tf_op jit(solution)/shard_map/all_to_all | solution.py:428
  68.6 5.4 %narrow_sum.1 = f32[512,256]{1,0:T(8,128)} custom-call(s32[3,64,4096]{2,1,0:T(8,128)} %count_hits.1.hits_ref, bf16[32,64,128]{2,1,0:T(8,128)(2,1)} %all-to-all-done.1.d_ref, f32[512,256]{1,0:T(8,128)} %wide_sum.1.refs_3_.wide_ref), custom_call_target="tpu_custom_call", output_to_operand_aliasing={{}: (2, {})} | custom-call | flops 10000000 | bytes 1024 | tf_op jit(solution)/shard_map/narrow_sum/pallas_call | solution.py:341
  74.0 0.7 add_multiply_fusion
  (36 shorter events, 2.0 us)
Async XLA Ops:
  1.4 10.8 %collective-permute-start = (bf16[1,64,128]{2,1,0:T(8,128)(2,1)S(1)}, bf16[1,64,128]{2,1,0:T(8,128)(2,1)S(1)}, u32[]{:S(2)}, u32[]{:S(2)}) collective-permute-start(bf16[1,64,128]{2,1,0:T(8,128)(2,1)S(1)} %slice.3), channel_id=1, source_target_pairs={{0,1},{1,0},{2,3},{3,2},{4,5},{5,4},{6,7},{7,6},{8,9},{9,8},{10,11... | collective-permute-start | bytes 49160 | tf_op jit(solution)/shard_map/ppermute | solution.py:387
  3.5 8.7 %collective-permute-start.1 = (bf16[1,64,128]{2,1,0:T(8,128)(2,1)S(1)}, bf16[1,64,128]{2,1,0:T(8,128)(2,1)S(1)}, u32[]{:S(2)}, u32[]{:S(2)}) collective-permute-start(bf16[1,64,128]{2,1,0:T(8,128)(2,1)S(1)} %slice.3), channel_id=1, source_target_pairs={{0,2},{1,3},{2,0},{3,1},{4,6},{5,7},{6,4},{7,5},{8,10},{9,11},{10,... | collective-permute-start | bytes 49160 | tf_op jit(solution)/shard_map/ppermute | solution.py:387
  5.8 6.4 %collective-permute-start.2 = (bf16[1,64,128]{2,1,0:T(8,128)(2,1)S(1)}, bf16[1,64,128]{2,1,0:T(8,128)(2,1)S(1)}, u32[]{:S(2)}, u32[]{:S(2)}) collective-permute-start(bf16[1,64,128]{2,1,0:T(8,128)(2,1)S(1)} %slice.3), channel_id=1, source_target_pairs={{0,3},{1,2},{2,1},{3,0},{4,7},{5,6},{6,5},{7,4},{8,11},{9,10},{10,... | collective-permute-start | bytes 49160 | tf_op jit(solution)/shard_map/ppermute | solution.py:387
  12.2 7.2 %copy-start = (bf16[32,128,128]{2,1,0:T(8,128)(2,1)S(1)}, bf16[32,128,128]{2,1,0:T(8,128)(2,1)}, u32[]{:S(2)}) copy-start(bf16[32,128,128]{2,1,0:T(8,128)(2,1)} %get-tuple-element.29.refs_2_) | copy-start | bytes 3145732
  12.2 33.5 %all-to-all-start = ((bf16[32,128,128]{2,1,0:T(8,128)(2,1)}), bf16[32,128,128]{2,1,0:T(8,128)(2,1)S(1)}, u32[]{:S(2)}, u32[]{:S(2)}) async-start(bf16[32,128,128]{2,1,0:T(8,128)(2,1)} %get-tuple-element.29.refs_2_), calls=%async_computation | async-start | bytes 2097152 | tf_op jit(solution)/shard_map/all_to_all | solution.py:415
  22.7 8.8 %collective-permute-start.10 = (bf16[4,64,128]{2,1,0:T(8,128)(2,1)S(1)}, bf16[4,64,128]{2,1,0:T(8,128)(2,1)S(1)}, u32[]{:S(2)}, u32[]{:S(2)}) collective-permute-start(bf16[4,64,128]{2,1,0:T(8,128)(2,1)S(1)} %pad_maximum_fusion.1), channel_id=1, source_target_pairs={{0,24},{4,28},{8,16},{12,20},{16,8},{20,12},{24,0},{28,4},{1,25},{... | collective-permute-start | bytes 196616 | tf_op jit(solution)/shard_map/ppermute | solution.py:387
  25.1 7.1 %collective-permute-start.8 = (bf16[4,64,128]{2,1,0:T(8,128)(2,1)S(1)}, bf16[4,64,128]{2,1,0:T(8,128)(2,1)S(1)}, u32[]{:S(2)}, u32[]{:S(2)}) collective-permute-start(bf16[4,64,128]{2,1,0:T(8,128)(2,1)S(1)} %pad_maximum_fusion.1), channel_id=1, source_target_pairs={{0,8},{4,12},{8,0},{12,4},{16,24},{20,28},{24,16},{28,20},{1,9},{5... | collective-permute-start | bytes 196616 | tf_op jit(solution)/shard_map/ppermute | solution.py:387
  25.4 8.4 %collective-permute-start.9 = (bf16[4,64,128]{2,1,0:T(8,128)(2,1)S(1)}, bf16[4,64,128]{2,1,0:T(8,128)(2,1)S(1)}, u32[]{:S(2)}, u32[]{:S(2)}) collective-permute-start(bf16[4,64,128]{2,1,0:T(8,128)(2,1)S(1)} %pad_maximum_fusion.1), channel_id=1, source_target_pairs={{0,16},{4,20},{8,24},{12,28},{16,0},{20,4},{24,8},{28,12},{1,17},{... | collective-permute-start | bytes 196616 | tf_op jit(solution)/shard_map/ppermute | solution.py:387
  25.5 10.0 %collective-permute-start.3 = (f32[8,256,128]{2,1,0:T(8,128)}, f32[8,256,128]{2,1,0:T(8,128)}, u32[]{:S(2)}, u32[]{:S(2)}) collective-permute-start(f32[8,256,128]{2,1,0:T(8,128)} %get-tuple-element.38.refs_0_), channel_id=1, source_target_pairs={{0,4},{4,0},{8,12},{12,8},{16,20},{20,16},{24,28},{28,24},{1,5},{5... | collective-permute-start | bytes 3145736 | tf_op jit(solution)/shard_map/ppermute | solution.py:387
  26.6 9.0 %collective-permute-start.4 = (f32[8,256,128]{2,1,0:T(8,128)S(1)}, f32[8,256,128]{2,1,0:T(8,128)}, u32[]{:S(2)}, u32[]{:S(2)}) collective-permute-start(f32[8,256,128]{2,1,0:T(8,128)S(1)} %get-tuple-element.31), channel_id=1, source_target_pairs={{0,4},{4,0},{8,12},{12,8},{16,20},{20,16},{24,28},{28,24},{1,5},{5... | collective-permute-start | bytes 3145736 | tf_op jit(solution)/shard_map/ppermute | solution.py:387
  33.8 1.6 %collective-permute-start.11 = (bf16[16,64,128]{2,1,0:T(8,128)(2,1)S(1)}, bf16[16,64,128]{2,1,0:T(8,128)(2,1)S(1)}, u32[]{:S(2)}, u32[]{:S(2)}) collective-permute-start(bf16[16,64,128]{2,1,0:T(8,128)(2,1)S(1)} %pad_maximum_fusion), channel_id=1, source_target_pairs={{0,4},{4,0},{8,12},{12,8},{16,20},{20,16},{24,28},{28,24},{1,5},{5... | collective-permute-start | bytes 786440 | tf_op jit(solution)/shard_map/ppermute | solution.py:387
  35.5 6.6 %copy-start.2 = (bf16[32,128,256]{2,1,0:T(8,128)(2,1)S(1)}, bf16[32,128,256]{2,1,0:T(8,128)(2,1)}, u32[]{:S(2)}) copy-start(bf16[32,128,256]{2,1,0:T(8,128)(2,1)} %get-tuple-element.27.refs_1_.g_ref) | copy-start | bytes 6291460
  39.4 16.7 %collective-permute-start.5 = (bf16[4,256,128]{2,1,0:T(8,128)(2,1)S(1)}, bf16[4,256,128]{2,1,0:T(8,128)(2,1)S(1)}, u32[]{:S(2)}, u32[]{:S(2)}) collective-permute-start(bf16[4,256,128]{2,1,0:T(8,128)(2,1)S(1)} %get-tuple-element.33), channel_id=1, source_target_pairs={{0,8},{4,12},{8,0},{12,4},{16,24},{20,28},{24,16},{28,20},{1,9},{5... | collective-permute-start | bytes 786440 | tf_op jit(solution)/shard_map/ppermute | solution.py:387
  39.6 16.5 %collective-permute-start.6 = (bf16[4,256,128]{2,1,0:T(8,128)(2,1)S(1)}, bf16[4,256,128]{2,1,0:T(8,128)(2,1)S(1)}, u32[]{:S(2)}, u32[]{:S(2)}) collective-permute-start(bf16[4,256,128]{2,1,0:T(8,128)(2,1)S(1)} %get-tuple-element.34), channel_id=1, source_target_pairs={{0,16},{4,20},{8,24},{12,28},{16,0},{20,4},{24,8},{28,12},{1,17},{... | collective-permute-start | bytes 786440 | tf_op jit(solution)/shard_map/ppermute | solution.py:387
  40.8 15.3 %collective-permute-start.7 = (bf16[4,256,128]{2,1,0:T(8,128)(2,1)S(1)}, bf16[4,256,128]{2,1,0:T(8,128)(2,1)S(1)}, u32[]{:S(2)}, u32[]{:S(2)}) collective-permute-start(bf16[4,256,128]{2,1,0:T(8,128)(2,1)S(1)} %get-tuple-element.35), channel_id=1, source_target_pairs={{0,24},{4,28},{8,16},{12,20},{16,8},{20,12},{24,0},{28,4},{1,25},{... | collective-permute-start | bytes 786440 | tf_op jit(solution)/shard_map/ppermute | solution.py:387
  42.1 8.8 %copy-start.3 = (bf16[1,256,128]{2,1,0:T(8,128)(2,1)S(1)}, bf16[1,256,128]{2,1,0:T(8,128)(2,1)}, u32[]{:S(2)}) copy-start(bf16[1,256,128]{2,1,0:T(8,128)(2,1)} %param.8) | copy-start | bytes 196612
  45.8 22.8 %all-to-all-start.1 = ((bf16[32,64,128]{2,1,0:T(8,128)(2,1)}), bf16[32,64,128]{2,1,0:T(8,128)(2,1)}, u32[]{:S(2)}, u32[]{:S(2)}) async-start(bf16[32,64,128]{2,1,0:T(8,128)(2,1)} %narrow_dpool.1), calls=%async_computation.1 | async-start | bytes 1048576 | tf_op jit(solution)/shard_map/all_to_all | solution.py:428
  56.1 1.0 %copy-start.1 = (f32[512,256]{1,0:T(8,128)S(1)}, f32[512,256]{1,0:T(8,128)}, u32[]{:S(2)}) copy-start(f32[512,256]{1,0:T(8,128)} %wide_sum.1.refs_3_.wide_ref) | copy-start | bytes 1572868
  57.3 16.7 %collective-permute-start.12 = (bf16[1,256,128]{2,1,0:T(8,128)(2,1)S(1)}, bf16[1,256,128]{2,1,0:T(8,128)(2,1)S(1)}, u32[]{:S(2)}, u32[]{:S(2)}) collective-permute-start(bf16[1,256,128]{2,1,0:T(8,128)(2,1)S(1)} %get-tuple-element.41), channel_id=1, source_target_pairs={{0,1},{1,0},{2,3},{3,2},{4,5},{5,4},{6,7},{7,6},{8,9},{9,8},{10,11... | collective-permute-start | bytes 196616 | tf_op jit(solution)/shard_map/ppermute | solution.py:387
  58.7 15.3 %collective-permute-start.13 = (bf16[1,256,128]{2,1,0:T(8,128)(2,1)S(1)}, bf16[1,256,128]{2,1,0:T(8,128)(2,1)S(1)}, u32[]{:S(2)}, u32[]{:S(2)}) collective-permute-start(bf16[1,256,128]{2,1,0:T(8,128)(2,1)S(1)} %get-tuple-element.42), channel_id=1, source_target_pairs={{0,2},{1,3},{2,0},{3,1},{4,6},{5,7},{6,4},{7,5},{8,10},{9,11},{10,... | collective-permute-start | bytes 196616 | tf_op jit(solution)/shard_map/ppermute | solution.py:387
  60.9 13.2 %collective-permute-start.14 = (bf16[1,256,128]{2,1,0:T(8,128)(2,1)S(1)}, bf16[1,256,128]{2,1,0:T(8,128)(2,1)S(1)}, u32[]{:S(2)}, u32[]{:S(2)}) collective-permute-start(bf16[1,256,128]{2,1,0:T(8,128)(2,1)S(1)} %get-tuple-element.43), channel_id=1, source_target_pairs={{0,3},{1,2},{2,1},{3,0},{4,7},{5,6},{6,5},{7,4},{8,11},{9,10},{10,... | collective-permute-start | bytes 196616 | tf_op jit(solution)/shard_map/ppermute | solution.py:387
